TPU v7x, 32 devices: a whole 2x2x4 slice. The times are simulated.
32 devices in a mesh: seq: 4 (over z), blk: 8 (over y, x, core).
Axes of the slice: x: 2, y: 2, z: 4, core: 2. Of those that a mesh axis runs over, the one named last changes fastest.
Arguments:
- train_acts: bfloat16 [4096, 4096], P(('seq', 'blk')), may hold values from -6 to 6
- train_grads: bfloat16 [4096, 14336], P(('seq', 'blk')), may hold values from -0.0234375 to 0.0234375
- block_table: int32 [8, 2], replicated, may hold values from 0 to 55, as said below
- seq_lengths: int32 [4], replicated, may hold values from 256 to 1024, as said below
- query_acts: bfloat16 [8, 256, 256], P('blk', 'seq'), may hold values from -6 to 6
- query_grads: bfloat16 [8, 256, 256], P('blk', 'seq'), may hold values from -6 to 6
- basis_acts: bfloat16 [8, 256, 256], P('blk', 'seq'), may hold values from -0.375 to 0.375
- basis_grads: bfloat16 [8, 256, 256], P('blk', 'seq'), may hold values from -0.375 to 0.375
- eigenvalues: float32 [8, 256, 256], P('blk', 'seq'), may hold values from 0.05 to 5
Outputs:
- scores: float32 [8, 4096], P(None, ('seq', 'blk'))
Inputs may be any that keep to these rules, and one draw needn't show every extreme that they name: `block_table`: column 0 of a row is an output-gradient block below 56, column 1 an activation block below 16; the last gradient block is named by some row. `seq_lengths`: some sequence has all 1024 tokens and some other one a quarter of them.
All inputs are finite; a program needn't handle non-finite values.
Results may differ from a plain program's by a relative error of at most 0.02.
Values may be sent and summed in bfloat16 or wider, within the bound.
No kernel may reach another device: no remote copies, remote signals or barrier semaphores. Data moves between devices by JAX's collectives and lax.ppermute only.
A program may use at most 64 MiB of HBM per device.

v0:
```python
import math

import jax
import jax.numpy as jnp
from jax import lax
from jax.sharding import PartitionSpec as P

BLOCK = 256
SEQ_LEN = 1024
QUERIES = 8
QTOK = 32


DAMPING = 0.1


def score_rows(rot_acts, rot_grads, right_mat):
    total_rows = rot_acts.shape[0]
    block_rows = math.gcd(total_rows, 512)

    def block_scores(pieces):
        act_piece, grad_piece = pieces
        mixed = jnp.dot(act_piece, right_mat, preferred_element_type=jnp.float32).reshape(
            -1, QUERIES, BLOCK
        )
        return jnp.sum(mixed * grad_piece.astype(jnp.float32)[:, None, :], axis=2)

    blocks = lax.map(
        block_scores,
        (rot_acts.reshape(-1, block_rows, BLOCK), rot_grads.reshape(-1, block_rows, BLOCK)),
    )
    return blocks.reshape(total_rows, QUERIES)


def on_device(
    train_acts,
    train_grads,
    block_table,
    seq_lengths,
    query_acts,
    query_grads,
    basis_acts,
    basis_grads,
    eigenvalues,
):
    gathered = (
        lax.all_gather(basis_acts, "seq", axis=1, tiled=True),
        lax.all_gather(basis_grads, "seq", axis=1, tiled=True),
        lax.all_gather(query_acts, "seq", axis=1, tiled=True),
        lax.all_gather(query_grads, "seq", axis=1, tiled=True),
    )
    eigen_full = lax.all_gather(eigenvalues, "seq", axis=1, tiled=True)
    basis_act = gathered[0][0]
    basis_grad = gathered[1][0]
    qrot_acts = jnp.dot(gathered[2][0], basis_act, preferred_element_type=jnp.float32).astype(
        jnp.bfloat16
    )
    qrot_grads = jnp.dot(gathered[3][0], basis_grad, preferred_element_type=jnp.float32).astype(
        jnp.bfloat16
    )
    qrot_acts = qrot_acts.reshape(QUERIES, QTOK, BLOCK)
    qrot_grads = qrot_grads.reshape(QUERIES, QTOK, BLOCK)
    outer = jnp.einsum("qsi,qsj->jqi", qrot_grads, qrot_acts, preferred_element_type=jnp.float32)
    divisor = eigen_full[0].T[:, None, :] + DAMPING
    right_mat = (outer / QTOK / divisor).astype(jnp.bfloat16).reshape(BLOCK, QUERIES * BLOCK)
    tok_dev = train_acts.shape[0]
    act_blocks = train_acts.reshape(tok_dev, -1, BLOCK)
    grad_blocks = train_grads.reshape(tok_dev, -1, BLOCK)
    act_sel = jnp.take(act_blocks, block_table[:, 1], axis=1)
    grad_sel = jnp.take(grad_blocks, block_table[:, 0], axis=1)
    slices = jnp.concatenate([act_sel, grad_sel], axis=2)
    received = lax.all_to_all(slices, "blk", split_axis=1, concat_axis=1, tiled=True)
    joined = received.reshape(-1, 2 * BLOCK)
    rot_acts = jnp.dot(joined[:, :BLOCK], basis_act, preferred_element_type=jnp.float32).astype(
        jnp.bfloat16
    )
    rot_grads = jnp.dot(joined[:, BLOCK:], basis_grad, preferred_element_type=jnp.float32).astype(
        jnp.bfloat16
    )
    owner_terms = score_rows(rot_acts, rot_grads, right_mat).reshape(
        received.shape[0], received.shape[1], QUERIES
    )
    own_scores = lax.psum_scatter(
        owner_terms.astype(jnp.bfloat16), "blk", scatter_dimension=1, tiled=True
    ).astype(jnp.float32)[:, 0, :]
    base_index = (lax.axis_index("seq") * lax.axis_size("blk") + lax.axis_index("blk")) * tok_dev
    position = base_index + jnp.arange(tok_dev, dtype=jnp.int32)
    valid = position % SEQ_LEN < seq_lengths[position // SEQ_LEN]
    return jnp.where(valid[None, :], own_scores.T, jnp.zeros((), jnp.float32))


def solution(mesh):
    in_specs = (
        P(("seq", "blk"), None),
        P(("seq", "blk"), None),
        P(),
        P(),
        P("blk", "seq", None),
        P("blk", "seq", None),
        P("blk", "seq", None),
        P("blk", "seq", None),
        P("blk", "seq", None),
    )
    out_specs = P(None, ("seq", "blk"))
    return jax.shard_map(
        on_device, mesh=mesh, in_specs=in_specs, out_specs=out_specs, check_vma=False
    )
```

profile of v0, /device:TPU:0, one launch (start us, length us, event | category | flops | bytes accessed | tf_op | source)
XLA Modules:
  0.0 125.4 jit_solution(10920298083064954452)
XLA Ops:
  0.0 0.8 fusion.15
  0.8 0.8 and_bitcast_fusion.1
  1.5 6.0 %copy.22 = bf16[128,14336]{0,1:T(8,128)(2,1)} copy(bf16[128,14336]{1,0:T(8,128)(2,1)} %param.12) | data formatting | bytes 7340032 | tf_op args[1]
  7.6 0.0 copy-start
  7.6 6.0 %copy.23 = bf16[128,56,256]{2,0,1:T(8,128)(2,1)} copy(bf16[128,56,256]{0,2,1:T(8,128)(2,1)} %bitcast.85) | data formatting | bytes 7340032 | tf_op jit(solution)/shard_map/reshape | solution.py:68
  13.6 0.0 copy-done
  13.6 0.7 copy.20
  14.2 0.5 copy.21
  14.8 2.6 %gather_fusion.1 = bf16[8,128,256]{2,1,0:T(8,128)(2,1)S(1)} fusion(bf16[128,56,256]{2,0,1:T(8,128)(2,1)} %copy.23, s32[1024]{0:T(1024)S(1)} %get-tuple-element.71), kind=kCustom, calls=%fused_computation.1 | custom fusion | bytes 1048608 | tf_op jit(solution)/shard_map/jit(_take)/gather | solution.py:70
  17.4 0.1 select_bitcast_fusion
  17.5 0.6 gather_fusion
  18.1 0.1 select_bitcast_fusion.1
  18.2 0.0 copy-start.2
  18.3 0.0 copy-start.3
  18.3 0.0 copy-start.4
  18.3 0.0 copy-start.1
  18.3 0.0 copy-start.6
  18.3 1.1 pad_maximum_fusion
  19.4 0.0 copy-start.5
  19.4 0.0 copy-start.7
  19.4 5.3 %all-to-all-start = ((bf16[128,8,512]{2,0,1:T(8,128)(2,1)}), bf16[128,8,512]{2,0,1:T(8,128)(2,1)S(1)}, u32[]{:S(2)}, u32[]{:S(2)}) async-start(bf16[128,8,512]{2,0,1:T(8,128)(2,1)} %pad_maximum_fusion), calls=%async_computation | async-start | bytes 2097152 | tf_op jit(solution)/shard_map/all_to_all | solution.py:72
  24.7 0.0 copy-done.2
  24.7 13.6 %all_gather.15 = bf16[1,256,256]{2,1,0:T(8,128)(2,1)S(1)} all-gather(bf16[1,64,256]{2,1,0:T(8,128)(2,1)S(1)} %copy-done.2), channel_id=1, replica_groups=mesh['seq'=4,'blk'=8] {'seq'}, dimensions={1}, use_global_device_ids=true | all-gather | bytes 163840 | tf_op jit(solution)/shard_map/all_gather | solution.py:47
  38.3 0.0 copy-done.3
  38.3 13.6 %all_gather.18 = bf16[1,256,256]{2,1,0:T(8,128)(2,1)S(1)} all-gather(bf16[1,64,256]{2,1,0:T(8,128)(2,1)S(1)} %copy-done.3), channel_id=1, replica_groups=mesh['seq'=4,'blk'=8] {'seq'}, dimensions={1}, use_global_device_ids=true | all-gather | bytes 163840 | tf_op jit(solution)/shard_map/all_gather | solution.py:48
  51.9 0.0 copy-done.4
  51.9 13.4 %all_gather.16 = bf16[1,256,256]{2,1,0:T(8,128)(2,1)S(1)} all-gather(bf16[1,64,256]{2,1,0:T(8,128)(2,1)S(1)} %copy-done.4), channel_id=1, replica_groups=mesh['seq'=4,'blk'=8] {'seq'}, dimensions={1}, use_global_device_ids=true | all-gather | bytes 163840 | tf_op jit(solution)/shard_map/all_gather | solution.py:49
  65.4 0.0 copy-done.1
  65.4 14.1 %all_gather.19 = f32[1,256,256]{2,1,0:T(8,128)S(1)} all-gather(f32[1,64,256]{2,1,0:T(8,128)S(1)} %copy-done.1), channel_id=1, replica_groups=mesh['seq'=4,'blk'=8] {'seq'}, dimensions={1}, use_global_device_ids=true | all-gather | bytes 327680 | tf_op jit(solution)/shard_map/all_gather | solution.py:52
  79.5 0.0 copy-done.6
  79.5 0.7 fusion.17
  80.2 0.2 convolution_convert_fusion.3
  80.4 0.0 copy-done.5
  80.4 13.4 %all_gather.17 = bf16[1,256,256]{2,1,0:T(8,128)(2,1)S(1)} all-gather(bf16[1,64,256]{2,1,0:T(8,128)(2,1)S(1)} %copy-done.5), channel_id=1, replica_groups=mesh['seq'=4,'blk'=8] {'seq'}, dimensions={1}, use_global_device_ids=true | all-gather | bytes 163840 | tf_op jit(solution)/shard_map/all_gather | solution.py:50
  93.7 0.0 copy-done.7
  93.7 0.6 dynamic-slice
  94.4 2.5 %fusion.12 = pred[128]{0:T(512)(128)(4,1)S(1)} fusion(s32[]{:T(128)} %bitcast.6, s32[]{:T(128)} %bitcast.7, s32[]{:T(128)} %bitcast.9, s32[]{:T(128)} %bitcast.8, s32[]{:T(128)S(6)} %mul.15), kind=kLoop, calls=%fused_computation.46 | loop fusion | flops 4864 | bytes 148 | tf_op jit(solution)/shard_map/lt | solution.py:88
  96.8 0.2 convolution_convert_fusion.2
  97.1 0.5 divide_convert_fusion
  97.5 0.0 all-to-all-done
  97.6 0.6 copy.30
  98.1 0.3 convolution_convert_fusion.1
  98.4 0.3 convolution_convert_fusion
  98.7 2.2 %while.10 = (s32[]{:T(128)}, bf16[2,512,8]{1,2,0:T(8,128)(2,1)S(1)}, bf16[2,512,256]{2,1,0:T(8,128)(2,1)S(1)}, bf16[256,2048]{0,1:T(8,128)(2,1)S(1)}, bf16[2,512,256]{2,1,0:T(8,128)(2,1)S(1)}, /*index=5*/s32[]{:T(128)}) while((s32[]{:T(128)}, bf16[2,512,8]{1,2,0:T(8,128)(2,1)S(1)}, bf16[2,512,256]{2,1,0:T(8,128)(2,1)S(1)}, ...), condition=%wide.region_2.3_spmd, body=%wide.region_0.0_spmd.sunk | while | flops 539095040 | bytes 3694673 | solution.py:28
  98.8 0.1 copy.32
  98.9 0.1 bitcast_convert_fusion.2
  99.0 0.8 multiply_reduce_fusion.2
  99.9 0.1 copy.32
  100.0 0.1 bitcast_convert_fusion.2
  100.1 0.8 multiply_reduce_fusion.2
  100.9 0.3 convert_element_type.42
  101.3 0.1 copy.27
  101.4 22.8 %all-reduce = bf16[128,8,8]{0,2,1:T(8,128)(2,1)S(1)} all-reduce(bf16[128,8,8]{0,2,1:T(8,128)(2,1)S(1)} %copy.27), channel_id=2, replica_groups=mesh['seq'=4,'blk'=8] {'blk'}, use_global_device_ids=true, to_apply=%region_3.4.clone | all-reduce | flops 8192 | bytes 32768
  124.2 1.2 fusion.11
  (8 shorter events, 0.1 us)
Async XLA Ops:
  7.6 6.0 %copy-start = (bf16[128,4096]{1,0:T(8,128)(2,1)S(1)}, bf16[128,4096]{1,0:T(8,128)(2,1)}, u32[]{:S(2)}) copy-start(bf16[128,4096]{1,0:T(8,128)(2,1)} %param.11) | copy-start | bytes 3145732
  18.2 6.4 %copy-start.2 = (bf16[1,64,256]{2,1,0:T(8,128)(2,1)S(1)}, bf16[1,64,256]{2,1,0:T(8,128)(2,1)}, u32[]{:S(2)}) copy-start(bf16[1,64,256]{2,1,0:T(8,128)(2,1)} %param.17) | copy-start | bytes 98308
  18.3 20.0 %copy-start.3 = (bf16[1,64,256]{2,1,0:T(8,128)(2,1)S(1)}, bf16[1,64,256]{2,1,0:T(8,128)(2,1)}, u32[]{:S(2)}) copy-start(bf16[1,64,256]{2,1,0:T(8,128)(2,1)} %param.18) | copy-start | bytes 98308
  18.3 33.6 %copy-start.4 = (bf16[1,64,256]{2,1,0:T(8,128)(2,1)S(1)}, bf16[1,64,256]{2,1,0:T(8,128)(2,1)}, u32[]{:S(2)}) copy-start(bf16[1,64,256]{2,1,0:T(8,128)(2,1)} %param.15) | copy-start | bytes 98308
  18.3 47.1 %copy-start.1 = (f32[1,64,256]{2,1,0:T(8,128)S(1)}, f32[1,64,256]{2,1,0:T(8,128)}, u32[]{:S(2)}) copy-start(f32[1,64,256]{2,1,0:T(8,128)} %param.19) | copy-start | bytes 196612
  18.3 61.2 %copy-start.6 = (s32[4]{0:T(128)S(1)}, s32[4]{0:T(128)}, u32[]{:S(2)}) copy-start(s32[4]{0:T(128)} %param.14) | copy-start | bytes 52
  19.4 61.0 %copy-start.5 = (bf16[1,64,256]{2,1,0:T(8,128)(2,1)S(1)}, bf16[1,64,256]{2,1,0:T(8,128)(2,1)}, u32[]{:S(2)}) copy-start(bf16[1,64,256]{2,1,0:T(8,128)(2,1)} %param.16) | copy-start | bytes 98308
  19.4 74.4 %copy-start.7 = (u32[32]{0:T(128)S(1)}, u32[32]{0:T(128)}, u32[]{:S(2)}) copy-start(u32[32]{0:T(128)} %constant.104) | copy-start | bytes 388
  19.4 78.2 %all-to-all-start = ((bf16[128,8,512]{2,0,1:T(8,128)(2,1)}), bf16[128,8,512]{2,0,1:T(8,128)(2,1)S(1)}, u32[]{:S(2)}, u32[]{:S(2)}) async-start(bf16[128,8,512]{2,0,1:T(8,128)(2,1)} %pad_maximum_fusion), calls=%async_computation | async-start | bytes 2097152 | tf_op jit(solution)/shard_map/all_to_all | solution.py:72
where the time goes:
time: 126 us; the launch traced here: 125 us
  blocking collectives  91 us (72%)
  local copies, waits for them, and re-layouts  19.1 us (15%)
  other arithmetic  6.6 us (5%)
  starting transfers between devices  5.3 us (4%)
  matrix products  3.06 us (2%)
    unnamed x1, blocking collectives  22.8 us
    all_gather x1, blocking collectives, on_device(): eigen_full = lax.all_gather(eigenvalues, 'seq', axis=1, tiled=True)  14.1 us
    all_gather x1, blocking collectives, on_device(): lax.all_gather(basis_grads, 'seq', axis=1, tiled=True)  13.6 us
    all_gather x1, blocking collectives, on_device(): lax.all_gather(basis_acts, 'seq', axis=1, tiled=True)  13.6 us
    all_gather x1, blocking collectives, on_device(): lax.all_gather(query_acts, 'seq', axis=1, tiled=True)  13.4 us
    all_gather x1, blocking collectives, on_device(): lax.all_gather(query_grads, 'seq', axis=1, tiled=True)  13.4 us
    unnamed x19, local copies, waits for them, and re-layouts  7.35 us
    reshape x1, local copies, waits for them, and re-layouts, on_device(): grad_blocks = train_grads.reshape(tok_dev, -1, BLOCK)  6 us
  transfers between devices with their start and end apart: 1, of which 0 were waited for; matrix products, arithmetic and copies ran while one was open for 4% of the time, Pallas kernels for 0%

commit v1 on v0

v1 whole, which is shorter than its diff:
```python
import functools

import jax
import jax.numpy as jnp
from jax import lax
from jax.experimental import pallas as pl
from jax.experimental.pallas import tpu as pltpu
from jax.sharding import PartitionSpec as P

BLOCK = 256
SEQ_LEN = 1024
QUERIES = 8
QTOK = 32
DAMPING = 0.1
VMEM_BYTES = 24 * 1024 * 1024

VMEM = pl.BlockSpec(memory_space=pltpu.VMEM)
SMEM = pl.BlockSpec(memory_space=pltpu.SMEM)
ANY = pl.BlockSpec(memory_space=pl.ANY)
NT = (((1,), (1,)), ((), ()))
TN = (((0,), (0,)), ((), ()))


def select_kernel(table_ref, acts_ref, grads_ref, out_ref, sem):
    pairs = out_ref.shape[0]
    copies = []
    for k in range(pairs):
        for half, (src, column) in enumerate(((acts_ref, 1), (grads_ref, 0))):
            start = pl.multiple_of(table_ref[k, column] * BLOCK, BLOCK)
            copy = pltpu.make_async_copy(
                src.at[:, pl.ds(start, BLOCK)],
                out_ref.at[k, :, pl.ds(half * BLOCK, BLOCK)],
                sem.at[2 * k + half],
            )
            copy.start()
            copies.append(copy)
    for copy in copies:
        copy.wait()


def select_blocks(table, acts, grads):
    pairs, tokens = table.shape[0], acts.shape[0]
    return pl.pallas_call(
        select_kernel,
        out_shape=jax.ShapeDtypeStruct((pairs, tokens, 2 * BLOCK), jnp.bfloat16),
        in_specs=[SMEM, ANY, ANY],
        out_specs=ANY,
        scratch_shapes=[pltpu.SemaphoreType.DMA((2 * pairs,))],
        compiler_params=pltpu.CompilerParams(vmem_limit_bytes=VMEM_BYTES),
        cost_estimate=pl.CostEstimate(
            flops=0, bytes_accessed=pairs * tokens * BLOCK * 8, transcendentals=0
        ),
        name="select_blocks",
    )(table, acts, grads)


def precond_kernel(shifts, rows, *refs):
    pieces = refs[:shifts]
    basis_act_ref, basis_grad_t_ref, precond_ref, full = refs[shifts:]
    me = lax.axis_index("seq")
    for m, piece in enumerate(pieces):
        owner = lax.rem(me - m + shifts, shifts)
        place = pl.ds(pl.multiple_of(owner * rows, rows), rows)
        for part in range(5):
            full[part, place, :] = piece[part * rows : (part + 1) * rows, :]
    basis_act, basis_grad = full[0], full[1]
    basis_act_ref[...] = basis_act
    basis_grad_t_ref[...] = basis_grad.astype(jnp.float32).T.astype(jnp.bfloat16)
    qrot_acts = jnp.dot(full[2], basis_act, preferred_element_type=jnp.float32).astype(jnp.bfloat16)
    qrot_grads = jnp.dot(full[3], basis_grad, preferred_element_type=jnp.float32).astype(jnp.bfloat16)
    scale = 1.0 / (QTOK * (full[4].astype(jnp.float32) + DAMPING))
    for q in range(QUERIES):
        tokens = slice(q * QTOK, (q + 1) * QTOK)
        outer = lax.dot_general(
            qrot_grads[tokens], qrot_acts[tokens], TN, preferred_element_type=jnp.float32
        )
        precond_ref[q] = (outer * scale).astype(jnp.bfloat16)


def make_precond(pieces):
    shifts, rows = len(pieces), pieces[0].shape[0] // 5
    square = jax.ShapeDtypeStruct((BLOCK, BLOCK), jnp.bfloat16)
    return pl.pallas_call(
        functools.partial(precond_kernel, shifts, rows),
        out_shape=(square, square, jax.ShapeDtypeStruct((QUERIES, BLOCK, BLOCK), jnp.bfloat16)),
        in_specs=[VMEM] * shifts,
        out_specs=(VMEM, VMEM, VMEM),
        scratch_shapes=[pltpu.VMEM((5, BLOCK, BLOCK), jnp.bfloat16)],
        compiler_params=pltpu.CompilerParams(vmem_limit_bytes=VMEM_BYTES),
        cost_estimate=pl.CostEstimate(
            flops=2 * BLOCK**3 * 3, bytes_accessed=2 * BLOCK * BLOCK * 15, transcendentals=0
        ),
        name="make_precond",
    )(*pieces)


def score_kernel(lengths_ref, slices_ref, basis_act_ref, basis_grad_t_ref, precond_ref, out_ref):
    sources, tokens = slices_ref.shape[0], slices_ref.shape[1]
    first = lax.axis_index("seq") * sources * tokens
    step = 2 if sources % 2 == 0 else 1

    def chunk(c, carry):
        acts = slices_ref[pl.ds(c * step, step), :, :BLOCK].reshape(step * tokens, BLOCK)
        grads = slices_ref[pl.ds(c * step, step), :, BLOCK:].reshape(step * tokens, BLOCK)
        rot_acts = jnp.dot(acts, basis_act_ref[...], preferred_element_type=jnp.float32).astype(
            jnp.bfloat16
        )
        rot_grads = lax.dot_general(
            basis_grad_t_ref[...], grads, NT, preferred_element_type=jnp.float32
        )
        rows = []
        for q in range(QUERIES):
            mixed = lax.dot_general(
                precond_ref[q], rot_acts, NT, preferred_element_type=jnp.float32
            )
            rows.append(jnp.sum(mixed * rot_grads, axis=0, keepdims=True))
        scores = jnp.concatenate(rows, axis=0)
        start = first + c * step * tokens
        position = start + lax.broadcasted_iota(jnp.int32, scores.shape, 1)
        low = start // SEQ_LEN
        valid = jnp.zeros(scores.shape, jnp.bool_)
        for s in range((step * tokens + SEQ_LEN - 2) // SEQ_LEN + 1):
            sequence = jnp.minimum(low + s, lengths_ref.shape[0] - 1)
            offset = position - sequence * SEQ_LEN
            valid |= (offset >= 0) & (offset < lengths_ref[sequence])
        scores = jnp.where(valid, scores, 0.0)
        for s in range(step):
            out_ref[c * step + s] = scores[:, s * tokens : (s + 1) * tokens]
        return carry

    lax.fori_loop(0, sources // step, chunk, 0, unroll=True if sources <= 8 else 1)


def partial_scores(lengths, slices, basis_act, basis_grad_t, precond):
    sources, tokens, _ = slices.shape
    return pl.pallas_call(
        score_kernel,
        out_shape=jax.ShapeDtypeStruct((sources, QUERIES, tokens), jnp.float32),
        in_specs=[SMEM, VMEM, VMEM, VMEM, VMEM],
        out_specs=VMEM,
        compiler_params=pltpu.CompilerParams(vmem_limit_bytes=VMEM_BYTES),
        cost_estimate=pl.CostEstimate(
            flops=2 * sources * tokens * BLOCK * BLOCK * (QUERIES + 2),
            bytes_accessed=slices.size * 2 + precond.size * 2,
            transcendentals=0,
        ),
        name="partial_scores",
    )(lengths, slices, basis_act, basis_grad_t, precond)


def on_device(
    train_acts,
    train_grads,
    block_table,
    seq_lengths,
    query_acts,
    query_grads,
    basis_acts,
    basis_grads,
    eigenvalues,
):
    groups = lax.axis_size("seq")
    packed = jnp.concatenate(
        [
            basis_acts[0],
            basis_grads[0],
            query_acts[0],
            query_grads[0],
            eigenvalues[0].astype(jnp.bfloat16),
        ],
        axis=0,
    )
    pieces = [packed]
    for m in range(1, groups):
        pieces.append(lax.ppermute(packed, "seq", [(i, (i + m) % groups) for i in range(groups)]))
    slices = select_blocks(block_table, train_acts, train_grads)
    received = lax.all_to_all(slices, "blk", split_axis=0, concat_axis=0, tiled=True)
    basis_act, basis_grad_t, precond = make_precond(pieces)
    partial = partial_scores(seq_lengths, received, basis_act, basis_grad_t, precond)
    spread = lax.all_to_all(partial, "blk", split_axis=0, concat_axis=0, tiled=True)
    return jnp.sum(spread, axis=0)


def solution(mesh):
    in_specs = (
        P(("seq", "blk"), None),
        P(("seq", "blk"), None),
        P(),
        P(),
        P("blk", "seq", None),
        P("blk", "seq", None),
        P("blk", "seq", None),
        P("blk", "seq", None),
        P("blk", "seq", None),
    )
    out_specs = P(None, ("seq", "blk"))
    return jax.shard_map(
        on_device, mesh=mesh, in_specs=in_specs, out_specs=out_specs, check_vma=False
    )
```

time: 126 us -> 40.4 us (0.32)
  the two profiles are of different devices: /device:TPU:0 before, /device:TPU:8 now
where the time goes in v1:
time: 40.4 us; the launch traced here: 40.1 us
  waiting for transfers between devices  13.4 us (33%)
  blocking collectives  8.48 us (21%)
  starting transfers between devices  8.4 us (21%)
  Pallas kernels  5.08 us (13%)
  local copies, waits for them, and re-layouts  4.06 us (10%)
  other arithmetic  0.61 us (2%)
    ppermute x3, waiting for transfers between devices, on_device(): lax.ppermute(packed, 'seq', [(i, (i + m) % groups) for i in range(groups)])  13.4 us
    all_to_all x1, blocking collectives, on_device(): lax.all_to_all(partial, 'blk', split_axis=0, concat_axis=0, tiled=True)  8.48 us
    ppermute x3, starting transfers between devices, on_device(): lax.ppermute(packed, 'seq', [(i, (i + m) % groups) for i in range(groups)])  4.67 us
    unnamed x21, local copies, waits for them, and re-layouts  4.06 us
    all_to_all x1, starting transfers between devices, on_device(): lax.all_to_all(slices, 'blk', split_axis=0, concat_axis=0, tiled=True)  3.74 us
    pallas_call x1, Pallas kernels, partial_scores(): pl.pallas_call(score_kernel, out_shape=jax.ShapeDtypeStruct((sources, QUE...  2.66 us
    pallas_call x1, Pallas kernels, select_blocks(): pl.pallas_call(select_kernel, out_shape=jax.ShapeDtypeStruct((pairs, toke...  1.72 us
  transfers between devices with their start and end apart: 4, of which 3 were waited for; matrix products, arithmetic and copies ran while one was open for 0% of the time, Pallas kernels for 2%

profile of v1, /device:TPU:8, one launch (start us, length us, event | category | flops | bytes accessed | tf_op | source)
XLA Modules:
  0.0 40.1 jit_solution(6534664234445415276)
XLA Ops:
  0.0 0.8 %copy.10.table_ref = s32[8,2]{1,0:T(8,128)S(1)} copy(s32[8,2]{0,1:T(2,128)} %param.11) | data formatting | bytes 128 | tf_op args[2]
  0.8 0.0 copy-start
  0.8 2.0 %copy-done = bf16[128,14336]{1,0:T(8,128)(2,1)S(1)} copy-done((bf16[128,14336]{1,0:T(8,128)(2,1)S(1)}, bf16[128,14336]{1,0:T(8,128)(2,1)}, u32[]{:S(2)}) %copy-start) | copy-done | bytes 3670040
  2.8 0.0 copy-start.1
  2.8 1.2 %copy-done.1 = bf16[128,4096]{1,0:T(8,128)(2,1)S(1)} copy-done((bf16[128,4096]{1,0:T(8,128)(2,1)S(1)}, bf16[128,4096]{1,0:T(8,128)(2,1)}, u32[]{:S(2)}) %copy-start.1) | copy-done | bytes 1048600
  4.0 0.0 copy-start.4
  4.0 0.0 copy-start.5
  4.0 0.0 copy-start.6
  4.0 0.0 copy-start.7
  4.0 0.0 copy-start.3
  4.0 0.0 copy-start.2
  4.1 1.7 %select_blocks.1 = bf16[8,128,512]{2,1,0:T(8,128)(2,1)} custom-call(s32[8,2]{1,0:T(8,128)S(1)} %copy.10.table_ref, bf16[128,4096]{1,0:T(8,128)(2,1)S(1)} %copy-done.1, bf16[128,14336]{1,0:T(8,128)(2,1)S(1)} %copy-done), custom_call_target="tpu_custom_call" | custom-call | bytes 2097152 | tf_op jit(solution)/shard_map/select_blocks/pallas_call | solution.py:43
  5.8 3.7 %all-to-all-start = ((bf16[8,128,512]{2,1,0:T(8,128)(2,1)}), bf16[8,128,512]{2,1,0:T(8,128)(2,1)S(1)}, u32[]{:S(2)}, u32[]{:S(2)}) async-start(bf16[8,128,512]{2,1,0:T(8,128)(2,1)} %select_blocks.1), calls=%async_computation | async-start | bytes 2097152 | tf_op jit(solution)/shard_map/all_to_all | solution.py:177
  9.5 0.0 copy-done.4
  9.5 0.0 copy-done.5
  9.6 0.0 copy-done.6
  9.6 0.0 copy-done.7
  9.6 0.0 copy-done.3
  9.6 1.6 %collective-permute-start = (bf16[320,256]{1,0:T(8,128)(2,1)S(1)}, bf16[320,256]{1,0:T(8,128)(2,1)S(1)}, u32[]{:S(2)}, u32[]{:S(2)}) collective-permute-start(bf16[320,256]{1,0:T(8,128)(2,1)S(1)} %bitcast_dynamic-update-slice_fusion.refs_0_), channel_id=1, source_target_pairs={{0,8},{8,16},{16,24},{24,0},{1,9},{9,17},{17,25},{25,1},{2,10},{10... | collective-permute-start | bytes 491528 | tf_op jit(solution)/shard_map/ppermute | solution.py:175
  11.3 1.2 %collective-permute-start.1 = (bf16[320,256]{1,0:T(8,128)(2,1)S(1)}, bf16[320,256]{1,0:T(8,128)(2,1)S(1)}, u32[]{:S(2)}, u32[]{:S(2)}) collective-permute-start(bf16[320,256]{1,0:T(8,128)(2,1)S(1)} %bitcast_dynamic-update-slice_fusion.refs_0_), channel_id=1, source_target_pairs={{0,16},{8,24},{16,0},{24,8},{1,17},{9,25},{17,1},{25,9},{2,18},{10... | collective-permute-start | bytes 491528 | tf_op jit(solution)/shard_map/ppermute | solution.py:175
  12.5 1.8 %collective-permute-start.2 = (bf16[320,256]{1,0:T(8,128)(2,1)S(1)}, bf16[320,256]{1,0:T(8,128)(2,1)S(1)}, u32[]{:S(2)}, u32[]{:S(2)}) collective-permute-start(bf16[320,256]{1,0:T(8,128)(2,1)S(1)} %bitcast_dynamic-update-slice_fusion.refs_0_), channel_id=1, source_target_pairs={{0,24},{8,0},{16,8},{24,16},{1,25},{9,1},{17,9},{25,17},{2,26},{10... | collective-permute-start | bytes 491528 | tf_op jit(solution)/shard_map/ppermute | solution.py:175
  14.3 8.4 %collective-permute-done.refs_1_ = bf16[320,256]{1,0:T(8,128)(2,1)S(1)} collective-permute-done((bf16[320,256]{1,0:T(8,128)(2,1)S(1)}, bf16[320,256]{1,0:T(8,128)(2,1)S(1)}, u32[]{:S(2)}, u32[]{:S(2)}) %collective-permute-start) | collective-permute-done | bytes 163872 | tf_op jit(solution)/shard_map/ppermute | solution.py:175
  22.6 3.3 %collective-permute-done.1.refs_2_ = bf16[320,256]{1,0:T(8,128)(2,1)S(1)} collective-permute-done((bf16[320,256]{1,0:T(8,128)(2,1)S(1)}, bf16[320,256]{1,0:T(8,128)(2,1)S(1)}, u32[]{:S(2)}, u32[]{:S(2)}) %collective-permute-start.1) | collective-permute-done | bytes 163872 | tf_op jit(solution)/shard_map/ppermute | solution.py:175
  25.9 1.8 %collective-permute-done.2.refs_3_ = bf16[320,256]{1,0:T(8,128)(2,1)S(1)} collective-permute-done((bf16[320,256]{1,0:T(8,128)(2,1)S(1)}, bf16[320,256]{1,0:T(8,128)(2,1)S(1)}, u32[]{:S(2)}, u32[]{:S(2)}) %collective-permute-start.2) | collective-permute-done | bytes 163872 | tf_op jit(solution)/shard_map/ppermute | solution.py:175
  27.7 0.7 %make_precond.1 = (bf16[256,256]{1,0:T(8,128)(2,1)S(1)}, bf16[256,256]{1,0:T(8,128)(2,1)S(1)}, bf16[8,256,256]{2,1,0:T(8,128)(2,1)S(1)}) custom-call(bf16[320,256]{1,0:T(8,128)(2,1)S(1)} %bitcast_dynamic-update-slice_fusion.refs_0_, bf16[320,256]{1,0:T(8,128)(2,1)S(1)} %collective-permute-done.refs_1_, bf16[320,256]{1,0:T(8,128)(2,1)S(1)} %collective-permute-done.1.refs_2_, ...), custom_call_target="tpu_custom_call" | custom-call | flops 100663296 | bytes 1966080 | tf_op jit(solution)/shard_map/make_precond/pallas_call | solution.py:83
  28.4 0.0 all-to-all-done.slices_ref
  28.4 0.0 copy-done.2
  28.4 2.7 %partial_scores.1 = f32[8,8,128]{2,1,0:T(8,128)S(1)} custom-call(s32[4]{0:T(128)S(1)} %copy-done.2, bf16[8,128,512]{2,1,0:T(8,128)(2,1)S(1)} %all-to-all-done.slices_ref, bf16[256,256]{1,0:T(8,128)(2,1)S(1)} %get-tuple-element.8.basis_act_ref, bf16[256,256]{1,0:T(8,128)(2,1)S(1)} %get-tuple-element.9.basis_grad_t_ref, ...), custom_call_target="tpu_custom_call" | custom-call | flops 1342177280 | bytes 2097152 | tf_op jit(solution)/shard_map/partial_scores/pallas_call | solution.py:136
  31.1 8.5 %all_to_all.10 = f32[8,8,128]{2,1,0:T(8,128)S(1)} all-to-all(f32[8,8,128]{2,1,0:T(8,128)S(1)} %partial_scores.1), channel_id=1, replica_groups=mesh['seq'=4,'blk'=8] {'blk'}, dimensions={0} | all-to-all | bytes 65536 | tf_op jit(solution)/shard_map/all_to_all | solution.py:180
  39.5 0.6 %reduce_sum.9 = f32[8,128]{1,0:T(8,128)} reduce(f32[8,8,128]{2,1,0:T(8,128)S(1)} %all_to_all.10, f32[]{:T(128)} %constant.0.clone.1), dimensions={0}, to_apply=%region_0.0 | reduce | flops 7168 | bytes 36868 | tf_op jit(solution)/shard_map/reduce_sum | solution.py:181
  (5 shorter events, 0.0 us)
Async XLA Ops:
  0.8 2.0 %copy-start = (bf16[128,14336]{1,0:T(8,128)(2,1)S(1)}, bf16[128,14336]{1,0:T(8,128)(2,1)}, u32[]{:S(2)}) copy-start(bf16[128,14336]{1,0:T(8,128)(2,1)} %grads_ref.1) | copy-start | bytes 11010052
  2.8 1.2 %copy-start.1 = (bf16[128,4096]{1,0:T(8,128)(2,1)S(1)}, bf16[128,4096]{1,0:T(8,128)(2,1)}, u32[]{:S(2)}) copy-start(bf16[128,4096]{1,0:T(8,128)(2,1)} %acts_ref.1) | copy-start | bytes 3145732
  4.0 5.5 %copy-start.4 = (bf16[1,64,256]{2,1,0:T(8,128)(2,1)S(1)}, bf16[1,64,256]{2,1,0:T(8,128)(2,1)}, u32[]{:S(2)}) copy-start(bf16[1,64,256]{2,1,0:T(8,128)(2,1)} %param.15) | copy-start | bytes 98308
  4.0 5.5 %copy-start.5 = (bf16[1,64,256]{2,1,0:T(8,128)(2,1)S(1)}, bf16[1,64,256]{2,1,0:T(8,128)(2,1)}, u32[]{:S(2)}) copy-start(bf16[1,64,256]{2,1,0:T(8,128)(2,1)} %param.16) | copy-start | bytes 98308
  4.0 5.5 %copy-start.6 = (bf16[1,64,256]{2,1,0:T(8,128)(2,1)S(1)}, bf16[1,64,256]{2,1,0:T(8,128)(2,1)}, u32[]{:S(2)}) copy-start(bf16[1,64,256]{2,1,0:T(8,128)(2,1)} %param.13) | copy-start | bytes 98308
  4.0 5.6 %copy-start.7 = (bf16[1,64,256]{2,1,0:T(8,128)(2,1)S(1)}, bf16[1,64,256]{2,1,0:T(8,128)(2,1)}, u32[]{:S(2)}) copy-start(bf16[1,64,256]{2,1,0:T(8,128)(2,1)} %param.14) | copy-start | bytes 98308
  4.0 5.6 %copy-start.3 = (f32[1,64,256]{2,1,0:T(8,128)S(1)}, f32[1,64,256]{2,1,0:T(8,128)}, u32[]{:S(2)}) copy-start(f32[1,64,256]{2,1,0:T(8,128)} %param.17) | copy-start | bytes 196612
  4.0 24.3 %copy-start.2 = (s32[4]{0:T(128)S(1)}, s32[4]{0:T(128)}, u32[]{:S(2)}) copy-start(s32[4]{0:T(128)} %lengths_ref.1) | copy-start | bytes 52
  5.8 22.6 %all-to-all-start = ((bf16[8,128,512]{2,1,0:T(8,128)(2,1)}), bf16[8,128,512]{2,1,0:T(8,128)(2,1)S(1)}, u32[]{:S(2)}, u32[]{:S(2)}) async-start(bf16[8,128,512]{2,1,0:T(8,128)(2,1)} %select_blocks.1), calls=%async_computation | async-start | bytes 2097152 | tf_op jit(solution)/shard_map/all_to_all | solution.py:177
  9.6 13.0 %collective-permute-start = (bf16[320,256]{1,0:T(8,128)(2,1)S(1)}, bf16[320,256]{1,0:T(8,128)(2,1)S(1)}, u32[]{:S(2)}, u32[]{:S(2)}) collective-permute-start(bf16[320,256]{1,0:T(8,128)(2,1)S(1)} %bitcast_dynamic-update-slice_fusion.refs_0_), channel_id=1, source_target_pairs={{0,8},{8,16},{16,24},{24,0},{1,9},{9,17},{17,25},{25,1},{2,10},{10... | collective-permute-start | bytes 491528 | tf_op jit(solution)/shard_map/ppermute | solution.py:175
  11.3 14.7 %collective-permute-start.1 = (bf16[320,256]{1,0:T(8,128)(2,1)S(1)}, bf16[320,256]{1,0:T(8,128)(2,1)S(1)}, u32[]{:S(2)}, u32[]{:S(2)}) collective-permute-start(bf16[320,256]{1,0:T(8,128)(2,1)S(1)} %bitcast_dynamic-update-slice_fusion.refs_0_), channel_id=1, source_target_pairs={{0,16},{8,24},{16,0},{24,8},{1,17},{9,25},{17,1},{25,9},{2,18},{10... | collective-permute-start | bytes 491528 | tf_op jit(solution)/shard_map/ppermute | solution.py:175
  12.5 15.2 %collective-permute-start.2 = (bf16[320,256]{1,0:T(8,128)(2,1)S(1)}, bf16[320,256]{1,0:T(8,128)(2,1)S(1)}, u32[]{:S(2)}, u32[]{:S(2)}) collective-permute-start(bf16[320,256]{1,0:T(8,128)(2,1)S(1)} %bitcast_dynamic-update-slice_fusion.refs_0_), channel_id=1, source_target_pairs={{0,24},{8,0},{16,8},{24,16},{1,25},{9,1},{17,9},{25,17},{2,26},{10... | collective-permute-start | bytes 491528 | tf_op jit(solution)/shard_map/ppermute | solution.py:175

commit v2 on v1

v2 whole, which is shorter than its diff:
```python
import functools

import jax
import jax.numpy as jnp
from jax import lax
from jax.experimental import pallas as pl
from jax.experimental.pallas import tpu as pltpu
from jax.sharding import PartitionSpec as P

BLOCK = 256
SEQ_LEN = 1024
QUERIES = 8
QTOK = 32
DAMPING = 0.1
CORES = 2
PACK_VMEM = 16 * 1024 * 1024
VMEM_BYTES = 24 * 1024 * 1024

VMEM = pl.BlockSpec(memory_space=pltpu.VMEM)
SMEM = pl.BlockSpec(memory_space=pltpu.SMEM)
HBM = pl.BlockSpec(memory_space=pltpu.HBM)
NT = (((1,), (1,)), ((), ()))
TN = (((0,), (0,)), ((), ()))


def swap(array, axis, bits):
    return lax.ppermute(array, axis, [(i, i ^ bits) for i in range(lax.axis_size(axis))])


def pack_kernel(table_ref, acts_ref, grads_ref, *refs):
    shards, packed_ref = refs[:5], refs[5]
    chunks, raw_eigen, sem = refs[6:-2], refs[-2], refs[-1]
    me = lax.axis_index("blk")
    rows = raw_eigen.shape[0]
    copies = []
    for part, shard in enumerate(shards):
        target = raw_eigen if part == 4 else packed_ref.at[pl.ds(part * rows, rows), :]
        copies.append(pltpu.make_async_copy(shard.at[0], target, sem.at[part]))
    for m, chunk in enumerate(chunks):
        for core in range(CORES):
            owner = me ^ (CORES * m + core)
            for half, (source, row) in enumerate(((acts_ref, 1), (grads_ref, 0))):
                start = pl.multiple_of(table_ref[row, owner] * BLOCK, BLOCK)
                copies.append(
                    pltpu.make_async_copy(
                        source.at[:, pl.ds(start, BLOCK)],
                        chunk.at[core, :, pl.ds(half * BLOCK, BLOCK)],
                        sem.at[len(copies)],
                    )
                )
    for copy in copies:
        copy.start()
    for copy in copies[:5]:
        copy.wait()
    packed_ref[4 * rows :, :] = raw_eigen[...].astype(jnp.bfloat16)
    for copy in copies[5:]:
        copy.wait()


def pack(table, acts, grads, *shards):
    pairs, tokens, rows = table.shape[1], acts.shape[0], shards[0].shape[1]
    chunk = pltpu.VMEM((CORES, tokens, 2 * BLOCK), jnp.bfloat16)
    packed = pltpu.VMEM((5 * rows, BLOCK), jnp.bfloat16)
    large = [pltpu.with_memory_space_constraint(a, pltpu.HBM) for a in (acts, grads, *shards)]
    chips = pairs // CORES
    return pl.pallas_call(
        pack_kernel,
        out_shape=(packed,) + (chunk,) * chips,
        in_specs=[SMEM] + [HBM] * 7,
        out_specs=(VMEM,) * (1 + chips),
        scratch_shapes=[
            pltpu.VMEM((rows, BLOCK), jnp.float32),
            pltpu.SemaphoreType.DMA((5 + 2 * pairs,)),
        ],
        compiler_params=pltpu.CompilerParams(vmem_limit_bytes=PACK_VMEM),
        cost_estimate=pl.CostEstimate(
            flops=0, bytes_accessed=pairs * tokens * BLOCK * 8, transcendentals=0
        ),
        name="pack",
    )(table, *large)


def precond_kernel(rows, *refs):
    pieces = refs[:-4]
    basis_act_ref, basis_grad_t_ref, precond_ref, full = refs[-4:]
    me = lax.axis_index("seq")
    for m, piece in enumerate(pieces):
        place = pl.ds(pl.multiple_of((me ^ m) * rows, rows), rows)
        for part in range(5):
            full[part, place, :] = piece[part * rows : (part + 1) * rows, :]
    basis_act, basis_grad = full[0], full[1]
    basis_act_ref[...] = basis_act
    basis_grad_t_ref[...] = basis_grad.astype(jnp.float32).T.astype(jnp.bfloat16)
    qrot_acts = jnp.dot(full[2], basis_act, preferred_element_type=jnp.float32).astype(jnp.bfloat16)
    qrot_grads = jnp.dot(full[3], basis_grad, preferred_element_type=jnp.float32).astype(jnp.bfloat16)
    scale = 1.0 / (QTOK * (full[4].astype(jnp.float32) + DAMPING))
    for q in range(QUERIES):
        tokens = slice(q * QTOK, (q + 1) * QTOK)
        outer = lax.dot_general(
            qrot_grads[tokens], qrot_acts[tokens], TN, preferred_element_type=jnp.float32
        )
        precond_ref[q] = (outer * scale).astype(jnp.bfloat16)


def make_precond(pieces):
    rows = pieces[0].shape[0] // 5
    square = jax.ShapeDtypeStruct((BLOCK, BLOCK), jnp.bfloat16)
    return pl.pallas_call(
        functools.partial(precond_kernel, rows),
        out_shape=(square, square, jax.ShapeDtypeStruct((QUERIES, BLOCK, BLOCK), jnp.bfloat16)),
        in_specs=[VMEM] * len(pieces),
        out_specs=(VMEM, VMEM, VMEM),
        scratch_shapes=[pltpu.VMEM((5, BLOCK, BLOCK), jnp.bfloat16)],
        compiler_params=pltpu.CompilerParams(vmem_limit_bytes=VMEM_BYTES),
        cost_estimate=pl.CostEstimate(
            flops=2 * BLOCK**3 * 3, bytes_accessed=2 * BLOCK * BLOCK * 15, transcendentals=0
        ),
        name="make_precond",
    )(*pieces)


def valid_mask(lengths_ref, start, shape):
    position = start + lax.broadcasted_iota(jnp.int32, shape, 1)
    low = start // SEQ_LEN
    valid = jnp.zeros(shape, jnp.bool_)
    for s in range((shape[1] + SEQ_LEN - 2) // SEQ_LEN + 1):
        sequence = jnp.minimum(low + s, lengths_ref.shape[0] - 1)
        offset = position - sequence * SEQ_LEN
        valid |= (offset >= 0) & (offset < lengths_ref[sequence])
    return valid


def score_kernel(core, chips, lengths_ref, basis_act_ref, basis_grad_t_ref, precond_ref, *refs):
    chunks, before, outs = refs[:chips], refs[chips : -chips], refs[-chips:]
    tokens = chunks[0].shape[1]
    me = lax.axis_index("blk")
    group = lax.axis_index("seq") * lax.axis_size("blk")
    for m in range(0, chips, 2):
        both = chunks[m : m + 2]
        acts = jnp.concatenate([c[core, :, :BLOCK] for c in both], axis=0)
        grads = jnp.concatenate([c[core, :, BLOCK:] for c in both], axis=0)
        rot_acts = jnp.dot(acts, basis_act_ref[...], preferred_element_type=jnp.float32).astype(
            jnp.bfloat16
        )
        rot_grads = lax.dot_general(
            basis_grad_t_ref[...], grads, NT, preferred_element_type=jnp.float32
        )
        rows = []
        for q in range(QUERIES):
            mixed = lax.dot_general(
                precond_ref[q], rot_acts, NT, preferred_element_type=jnp.float32
            )
            rows.append(jnp.sum(mixed * rot_grads, axis=0, keepdims=True))
        scores = jnp.concatenate(rows, axis=0)
        for s in range(len(both)):
            part = scores[:, s * tokens : (s + 1) * tokens]
            if core:
                start = (group + (me ^ (CORES * (m + s)))) * tokens
                valid = valid_mask(lengths_ref, start, part.shape)
                part = jnp.where(valid, part + before[m + s][...], 0.0)
            outs[m + s][...] = part


def partial_scores(core, lengths, weights, chunks, before):
    chips, tokens = len(chunks), chunks[0].shape[1]
    return pl.pallas_call(
        functools.partial(score_kernel, core, chips),
        out_shape=(jax.ShapeDtypeStruct((QUERIES, tokens), jnp.float32),) * chips,
        in_specs=[SMEM] + [VMEM] * (3 + chips + len(before)),
        out_specs=(VMEM,) * chips,
        compiler_params=pltpu.CompilerParams(vmem_limit_bytes=VMEM_BYTES),
        cost_estimate=pl.CostEstimate(
            flops=2 * chips * tokens * BLOCK * BLOCK * (QUERIES + 2),
            bytes_accessed=2 * BLOCK * (chips * tokens * 2 + BLOCK * (QUERIES + 2)),
            transcendentals=0,
        ),
        name="partial_scores",
    )(lengths, *weights, *chunks, *before)


def on_device(
    train_acts,
    train_grads,
    block_table,
    seq_lengths,
    query_acts,
    query_grads,
    basis_acts,
    basis_grads,
    eigenvalues,
):
    groups, chips = lax.axis_size("seq"), lax.axis_size("blk") // CORES
    packed, *chunks = pack(
        block_table.T,
        train_acts,
        train_grads,
        basis_acts,
        basis_grads,
        query_acts,
        query_grads,
        eigenvalues,
    )
    own = [packed] + [swap(packed, "seq", m) for m in range(1, groups)]
    chunks = chunks[:1] + [swap(chunks[m], "blk", CORES * m) for m in range(1, chips)]
    other = [swap(piece, "blk", 1) for piece in own]
    scores = partial_scores(0, seq_lengths, make_precond(own), chunks, ())
    scores = partial_scores(1, seq_lengths, make_precond(other), chunks, scores)
    total = scores[0]
    for m in range(1, chips):
        total = total + swap(scores[m], "blk", CORES * m)
    return total


def solution(mesh):
    in_specs = (
        P(("seq", "blk"), None),
        P(("seq", "blk"), None),
        P(),
        P(),
        P("blk", "seq", None),
        P("blk", "seq", None),
        P("blk", "seq", None),
        P("blk", "seq", None),
        P("blk", "seq", None),
    )
    out_specs = P(None, ("seq", "blk"))
    return jax.shard_map(
        on_device, mesh=mesh, in_specs=in_specs, out_specs=out_specs, check_vma=False
    )
```

time: 40.4 us -> 36.1 us (0.89)
  the two profiles are of different devices: /device:TPU:8 before, /device:TPU:0 now
where the time goes in v2:
time: 36.1 us; the launch traced here: 35.9 us
  starting transfers between devices  16.4 us (45%)
  waiting for transfers between devices  11.3 us (31%)
  Pallas kernels  6.85 us (19%)
  local copies, waits for them, and re-layouts  0.7 us (2%)
  other arithmetic  0.6 us (2%)
    ppermute x13, starting transfers between devices, swap(): lax.ppermute(array, axis, [(i, i ^ bits) for i in range(lax.axis_size(axi...  16.4 us
    ppermute x13, waiting for transfers between devices, swap(): lax.ppermute(array, axis, [(i, i ^ bits) for i in range(lax.axis_size(axi...  11.3 us
    pallas_call x2, Pallas kernels, partial_scores(): pl.pallas_call(functools.partial(score_kernel, core, chips), out_shape=(j...  3.42 us
    pallas_call x1, Pallas kernels, pack(): pl.pallas_call(pack_kernel, out_shape=(packed,) + (chunk,) * chips, in_sp...  2.05 us
    pallas_call x2, Pallas kernels, make_precond(): pl.pallas_call(functools.partial(precond_kernel, rows), out_shape=(square...  1.38 us
  transfers between devices with their start and end apart: 13, of which 4 were waited for; matrix products, arithmetic and copies ran while one was open for 0% of the time, Pallas kernels for 7%

profile of v2, /device:TPU:0, one launch (start us, length us, event | category | flops | bytes accessed | tf_op | source)
XLA Modules:
  0.0 35.9 jit_solution(16841384831269934536)
XLA Ops:
  0.0 0.0 copy-start.1
  0.0 0.0 copy-start
  0.0 0.7 %copy-done = s32[8,2]{0,1:T(2,128)S(1)} copy-done((s32[8,2]{0,1:T(2,128)S(1)}, s32[8,2]{0,1:T(2,128)}, u32[]{:S(2)}) %copy-start) | copy-done | bytes 88
  0.7 2.0 %pack.1 = (bf16[320,256]{1,0:T(8,128)(2,1)S(1)}, bf16[2,128,512]{2,1,0:T(8,128)(2,1)S(1)}, bf16[2,128,512]{2,1,0:T(8,128)(2,1)S(1)}, bf16[2,128,512]{2,1,0:T(8,128)(2,1)S(1)}, bf16[2,128,512]{2,1,0:T(8,128)(2,1)S(1)}) custom-call(s32[2,8]{1,0:T(2,128)S(1)} %bitcast.1, bf16[128,4096]{1,0:T(8,128)(2,1)} %acts_ref.1, bf16[128,14336]{1,0:T(8,128)(2,1)} %grads_ref.1, ...), custom_call_target="tpu_custom_call" | custom-call | bytes 2097152 | tf_op jit(solution)/shard_map/pack/pallas_call | solution.py:66
  2.8 3.1 %collective-permute-start.1 = (bf16[320,256]{1,0:T(8,128)(2,1)S(1)}, bf16[320,256]{1,0:T(8,128)(2,1)S(1)}, u32[]{:S(2)}, u32[]{:S(2)}) collective-permute-start(bf16[320,256]{1,0:T(8,128)(2,1)S(1)} %get-tuple-element.24.refs_0_), channel_id=1, source_target_pairs={{0,8},{8,0},{16,24},{24,16},{1,9},{9,1},{17,25},{25,17},{2,10},{10... | collective-permute-start | bytes 491528 | tf_op jit(solution)/shard_map/ppermute | solution.py:27
  5.8 1.5 %collective-permute-start.7 = (bf16[2,128,512]{2,1,0:T(8,128)(2,1)S(1)}, bf16[2,128,512]{2,1,0:T(8,128)(2,1)S(1)}, u32[]{:S(2)}, u32[]{:S(2)}) collective-permute-start(bf16[2,128,512]{2,1,0:T(8,128)(2,1)S(1)} %get-tuple-element.29), channel_id=1, source_target_pairs={{0,2},{1,3},{2,0},{3,1},{4,6},{5,7},{6,4},{7,5},{8,10},{9,11},{10,... | collective-permute-start | bytes 786440 | tf_op jit(solution)/shard_map/ppermute | solution.py:27
  7.3 1.5 %collective-permute-start.8 = (bf16[2,128,512]{2,1,0:T(8,128)(2,1)S(1)}, bf16[2,128,512]{2,1,0:T(8,128)(2,1)S(1)}, u32[]{:S(2)}, u32[]{:S(2)}) collective-permute-start(bf16[2,128,512]{2,1,0:T(8,128)(2,1)S(1)} %get-tuple-element.30), channel_id=1, source_target_pairs={{0,4},{1,5},{2,6},{3,7},{4,0},{5,1},{6,2},{7,3},{8,12},{9,13},{10,... | collective-permute-start | bytes 786440 | tf_op jit(solution)/shard_map/ppermute | solution.py:27
  8.9 2.6 %collective-permute-start.3 = (bf16[320,256]{1,0:T(8,128)(2,1)S(1)}, bf16[320,256]{1,0:T(8,128)(2,1)S(1)}, u32[]{:S(2)}, u32[]{:S(2)}) collective-permute-start(bf16[320,256]{1,0:T(8,128)(2,1)S(1)} %get-tuple-element.24.refs_0_), channel_id=1, source_target_pairs={{0,16},{8,24},{16,0},{24,8},{1,17},{9,25},{17,1},{25,9},{2,18},{10... | collective-permute-start | bytes 491528 | tf_op jit(solution)/shard_map/ppermute | solution.py:27
  11.4 0.2 collective-permute-start.5
  11.7 0.0 collective-permute-done.1.refs_1_
  11.7 2.9 %collective-permute-start.9 = (bf16[2,128,512]{2,1,0:T(8,128)(2,1)S(1)}, bf16[2,128,512]{2,1,0:T(8,128)(2,1)S(1)}, u32[]{:S(2)}, u32[]{:S(2)}) collective-permute-start(bf16[2,128,512]{2,1,0:T(8,128)(2,1)S(1)} %get-tuple-element.31), channel_id=1, source_target_pairs={{0,6},{1,7},{2,4},{3,5},{4,2},{5,3},{6,0},{7,1},{8,14},{9,15},{10,... | collective-permute-start | bytes 786440 | tf_op jit(solution)/shard_map/ppermute | solution.py:27
  14.6 8.4 %collective-permute-done.3.refs_2_ = bf16[320,256]{1,0:T(8,128)(2,1)S(1)} collective-permute-done((bf16[320,256]{1,0:T(8,128)(2,1)S(1)}, bf16[320,256]{1,0:T(8,128)(2,1)S(1)}, u32[]{:S(2)}, u32[]{:S(2)}) %collective-permute-start.3) | collective-permute-done | bytes 163872 | tf_op jit(solution)/shard_map/ppermute | solution.py:27
  22.9 0.0 collective-permute-start
  22.9 0.0 collective-permute-done.5.refs_3_
  22.9 0.5 %collective-permute-start.2 = (bf16[320,256]{1,0:T(8,128)(2,1)S(1)}, bf16[320,256]{1,0:T(8,128)(2,1)S(1)}, u32[]{:S(2)}, u32[]{:S(2)}) collective-permute-start(bf16[320,256]{1,0:T(8,128)(2,1)S(1)} %collective-permute-done.1.refs_1_), channel_id=1, source_target_pairs={{0,1},{1,0},{2,3},{3,2},{4,5},{5,4},{6,7},{7,6},{8,9},{9,8},{10,11... | collective-permute-start | bytes 491528 | tf_op jit(solution)/shard_map/ppermute | solution.py:27
  23.4 0.0 collective-permute-done.7.refs_1_
  23.4 0.1 collective-permute-start.4
  23.5 0.0 collective-permute-done.8.refs_2_
  23.5 0.4 %collective-permute-start.6 = (bf16[320,256]{1,0:T(8,128)(2,1)S(1)}, bf16[320,256]{1,0:T(8,128)(2,1)S(1)}, u32[]{:S(2)}, u32[]{:S(2)}) collective-permute-start(bf16[320,256]{1,0:T(8,128)(2,1)S(1)} %collective-permute-done.5.refs_3_), channel_id=1, source_target_pairs={{0,1},{1,0},{2,3},{3,2},{4,5},{5,4},{6,7},{7,6},{8,9},{9,8},{10,11... | collective-permute-start | bytes 491528 | tf_op jit(solution)/shard_map/ppermute | solution.py:27
  24.0 0.7 %make_precond.3 = (bf16[256,256]{1,0:T(8,128)(2,1)S(1)}, bf16[256,256]{1,0:T(8,128)(2,1)S(1)}, bf16[8,256,256]{2,1,0:T(8,128)(2,1)S(1)}) custom-call(bf16[320,256]{1,0:T(8,128)(2,1)S(1)} %get-tuple-element.24.refs_0_, bf16[320,256]{1,0:T(8,128)(2,1)S(1)} %collective-permute-done.1.refs_1_, bf16[320,256]{1,0:T(8,128)(2,1)S(1)} %collective-permute-done.3.refs_2_, ...), custom_call_target="tpu_custom_call" | custom-call | flops 100663296 | bytes 1966080 | tf_op jit(solution)/shard_map/make_precond/pallas_call | solution.py:108
  24.7 0.0 collective-permute-done.9.refs_3_
  24.7 0.0 copy-done.1
  24.7 1.7 %partial_scores.2 = (f32[8,128]{1,0:T(8,128)S(1)}, f32[8,128]{1,0:T(8,128)S(1)}, f32[8,128]{1,0:T(8,128)S(1)}, f32[8,128]{1,0:T(8,128)S(1)}) custom-call(s32[4]{0:T(128)S(1)} %copy-done.1, bf16[256,256]{1,0:T(8,128)(2,1)S(1)} %get-tuple-element.32.basis_act_ref, bf16[256,256]{1,0:T(8,128)(2,1)S(1)} %get-tuple-element.33.basis_grad_t_ref, ...), custom_call_target="tpu_custom_call" | custom-call | flops 671088640 | bytes 1835008 | tf_op jit(solution)/shard_map/partial_scores/pallas_call | solution.py:166
  26.4 0.0 collective-permute-done.refs_0_
  26.4 0.0 collective-permute-done.2.refs_1_
  26.4 0.0 collective-permute-done.4.refs_2_
  26.4 0.0 collective-permute-done.6.refs_3_
  26.4 0.7 %make_precond.2 = (bf16[256,256]{1,0:T(8,128)(2,1)S(1)}, bf16[256,256]{1,0:T(8,128)(2,1)S(1)}, bf16[8,256,256]{2,1,0:T(8,128)(2,1)S(1)}) custom-call(bf16[320,256]{1,0:T(8,128)(2,1)S(1)} %collective-permute-done.refs_0_, bf16[320,256]{1,0:T(8,128)(2,1)S(1)} %collective-permute-done.2.refs_1_, bf16[320,256]{1,0:T(8,128)(2,1)S(1)} %collective-permute-done.4.refs_2_, ...), custom_call_target="tpu_custom_call" | custom-call | flops 100663296 | bytes 1966080 | tf_op jit(solution)/shard_map/make_precond/pallas_call | solution.py:108
  27.1 1.7 %partial_scores.3 = (f32[8,128]{1,0:T(8,128)S(1)}, f32[8,128]{1,0:T(8,128)S(1)}, f32[8,128]{1,0:T(8,128)S(1)}, f32[8,128]{1,0:T(8,128)S(1)}) custom-call(s32[4]{0:T(128)S(1)} %copy-done.1, bf16[256,256]{1,0:T(8,128)(2,1)S(1)} %get-tuple-element.25.basis_act_ref, bf16[256,256]{1,0:T(8,128)(2,1)S(1)} %get-tuple-element.26.basis_grad_t_ref, ...), custom_call_target="tpu_custom_call" | custom-call | flops 671088640 | bytes 1835008 | tf_op jit(solution)/shard_map/partial_scores/pallas_call | solution.py:166
  28.8 1.1 %collective-permute-start.10 = (f32[8,128]{1,0:T(8,128)S(1)}, f32[8,128]{1,0:T(8,128)S(1)}, u32[]{:S(2)}, u32[]{:S(2)}) collective-permute-start(f32[8,128]{1,0:T(8,128)S(1)} %get-tuple-element.40), channel_id=1, source_target_pairs={{0,2},{1,3},{2,0},{3,1},{4,6},{5,7},{6,4},{7,5},{8,10},{9,11},{10,... | collective-permute-start | bytes 12296 | tf_op jit(solution)/shard_map/ppermute | solution.py:27
  29.9 0.9 %collective-permute-start.11 = (f32[8,128]{1,0:T(8,128)S(1)}, f32[8,128]{1,0:T(8,128)S(1)}, u32[]{:S(2)}, u32[]{:S(2)}) collective-permute-start(f32[8,128]{1,0:T(8,128)S(1)} %get-tuple-element.41), channel_id=1, source_target_pairs={{0,4},{1,5},{2,6},{3,7},{4,0},{5,1},{6,2},{7,3},{8,12},{9,13},{10,... | collective-permute-start | bytes 12296 | tf_op jit(solution)/shard_map/ppermute | solution.py:27
  30.8 1.6 %collective-permute-start.12 = (f32[8,128]{1,0:T(8,128)S(1)}, f32[8,128]{1,0:T(8,128)S(1)}, u32[]{:S(2)}, u32[]{:S(2)}) collective-permute-start(f32[8,128]{1,0:T(8,128)S(1)} %get-tuple-element.42), channel_id=1, source_target_pairs={{0,6},{1,7},{2,4},{3,5},{4,2},{5,3},{6,0},{7,1},{8,14},{9,15},{10,... | collective-permute-start | bytes 12296 | tf_op jit(solution)/shard_map/ppermute | solution.py:27
  32.4 0.1 collective-permute-done.10
  32.5 1.0 %collective-permute-done.11 = f32[8,128]{1,0:T(8,128)S(1)} collective-permute-done((f32[8,128]{1,0:T(8,128)S(1)}, f32[8,128]{1,0:T(8,128)S(1)}, u32[]{:S(2)}, u32[]{:S(2)}) %collective-permute-start.11) | collective-permute-done | bytes 4128 | tf_op jit(solution)/shard_map/ppermute | solution.py:27
  33.5 1.8 %collective-permute-done.12 = f32[8,128]{1,0:T(8,128)S(1)} collective-permute-done((f32[8,128]{1,0:T(8,128)S(1)}, f32[8,128]{1,0:T(8,128)S(1)}, u32[]{:S(2)}, u32[]{:S(2)}) %collective-permute-start.12) | collective-permute-done | bytes 4128 | tf_op jit(solution)/shard_map/ppermute | solution.py:27
  35.3 0.6 %add_add_fusion = f32[8,128]{1,0:T(8,128)} fusion(f32[8,128]{1,0:T(8,128)S(1)} %collective-permute-done.12, f32[8,128]{1,0:T(8,128)S(1)} %collective-permute-done.11, f32[8,128]{1,0:T(8,128)S(1)} %get-tuple-element.39, f32[8,128]{1,0:T(8,128)S(1)} %collective-permute-done.10), kind=kLoop, calls=%fused_computation | loop fusion | flops 3072 | bytes 20480 | tf_op jit(solution)/shard_map/add | solution.py:210
Async XLA Ops:
  0.0 24.7 %copy-start.1 = (s32[4]{0:T(128)S(1)}, s32[4]{0:T(128)}, u32[]{:S(2)}) copy-start(s32[4]{0:T(128)} %lengths_ref.3) | copy-start | bytes 52
  0.0 0.7 %copy-start = (s32[8,2]{0,1:T(2,128)S(1)}, s32[8,2]{0,1:T(2,128)}, u32[]{:S(2)}) copy-start(s32[8,2]{0,1:T(2,128)} %param.11) | copy-start | bytes 196
  2.8 8.9 %collective-permute-start.1 = (bf16[320,256]{1,0:T(8,128)(2,1)S(1)}, bf16[320,256]{1,0:T(8,128)(2,1)S(1)}, u32[]{:S(2)}, u32[]{:S(2)}) collective-permute-start(bf16[320,256]{1,0:T(8,128)(2,1)S(1)} %get-tuple-element.24.refs_0_), channel_id=1, source_target_pairs={{0,8},{8,0},{16,24},{24,16},{1,9},{9,1},{17,25},{25,17},{2,10},{10... | collective-permute-start | bytes 491528 | tf_op jit(solution)/shard_map/ppermute | solution.py:27
  5.8 17.6 %collective-permute-start.7 = (bf16[2,128,512]{2,1,0:T(8,128)(2,1)S(1)}, bf16[2,128,512]{2,1,0:T(8,128)(2,1)S(1)}, u32[]{:S(2)}, u32[]{:S(2)}) collective-permute-start(bf16[2,128,512]{2,1,0:T(8,128)(2,1)S(1)} %get-tuple-element.29), channel_id=1, source_target_pairs={{0,2},{1,3},{2,0},{3,1},{4,6},{5,7},{6,4},{7,5},{8,10},{9,11},{10,... | collective-permute-start | bytes 786440 | tf_op jit(solution)/shard_map/ppermute | solution.py:27
  7.3 16.2 %collective-permute-start.8 = (bf16[2,128,512]{2,1,0:T(8,128)(2,1)S(1)}, bf16[2,128,512]{2,1,0:T(8,128)(2,1)S(1)}, u32[]{:S(2)}, u32[]{:S(2)}) collective-permute-start(bf16[2,128,512]{2,1,0:T(8,128)(2,1)S(1)} %get-tuple-element.30), channel_id=1, source_target_pairs={{0,4},{1,5},{2,6},{3,7},{4,0},{5,1},{6,2},{7,3},{8,12},{9,13},{10,... | collective-permute-start | bytes 786440 | tf_op jit(solution)/shard_map/ppermute | solution.py:27
  8.9 14.1 %collective-permute-start.3 = (bf16[320,256]{1,0:T(8,128)(2,1)S(1)}, bf16[320,256]{1,0:T(8,128)(2,1)S(1)}, u32[]{:S(2)}, u32[]{:S(2)}) collective-permute-start(bf16[320,256]{1,0:T(8,128)(2,1)S(1)} %get-tuple-element.24.refs_0_), channel_id=1, source_target_pairs={{0,16},{8,24},{16,0},{24,8},{1,17},{9,25},{17,1},{25,9},{2,18},{10... | collective-permute-start | bytes 491528 | tf_op jit(solution)/shard_map/ppermute | solution.py:27
  11.4 11.5 %collective-permute-start.5 = (bf16[320,256]{1,0:T(8,128)(2,1)S(1)}, bf16[320,256]{1,0:T(8,128)(2,1)S(1)}, u32[]{:S(2)}, u32[]{:S(2)}) collective-permute-start(bf16[320,256]{1,0:T(8,128)(2,1)S(1)} %get-tuple-element.24.refs_0_), channel_id=1, source_target_pairs={{0,24},{8,16},{16,8},{24,0},{1,25},{9,17},{17,9},{25,1},{2,26},{10... | collective-permute-start | bytes 491528 | tf_op jit(solution)/shard_map/ppermute | solution.py:27
  11.7 13.0 %collective-permute-start.9 = (bf16[2,128,512]{2,1,0:T(8,128)(2,1)S(1)}, bf16[2,128,512]{2,1,0:T(8,128)(2,1)S(1)}, u32[]{:S(2)}, u32[]{:S(2)}) collective-permute-start(bf16[2,128,512]{2,1,0:T(8,128)(2,1)S(1)} %get-tuple-element.31), channel_id=1, source_target_pairs={{0,6},{1,7},{2,4},{3,5},{4,2},{5,3},{6,0},{7,1},{8,14},{9,15},{10,... | collective-permute-start | bytes 786440 | tf_op jit(solution)/shard_map/ppermute | solution.py:27
  22.9 3.5 %collective-permute-start = (bf16[320,256]{1,0:T(8,128)(2,1)S(1)}, bf16[320,256]{1,0:T(8,128)(2,1)S(1)}, u32[]{:S(2)}, u32[]{:S(2)}) collective-permute-start(bf16[320,256]{1,0:T(8,128)(2,1)S(1)} %get-tuple-element.24.refs_0_), channel_id=1, source_target_pairs={{0,1},{1,0},{2,3},{3,2},{4,5},{5,4},{6,7},{7,6},{8,9},{9,8},{10,11... | collective-permute-start | bytes 491528 | tf_op jit(solution)/shard_map/ppermute | solution.py:27
  22.9 3.5 %collective-permute-start.2 = (bf16[320,256]{1,0:T(8,128)(2,1)S(1)}, bf16[320,256]{1,0:T(8,128)(2,1)S(1)}, u32[]{:S(2)}, u32[]{:S(2)}) collective-permute-start(bf16[320,256]{1,0:T(8,128)(2,1)S(1)} %collective-permute-done.1.refs_1_), channel_id=1, source_target_pairs={{0,1},{1,0},{2,3},{3,2},{4,5},{5,4},{6,7},{7,6},{8,9},{9,8},{10,11... | collective-permute-start | bytes 491528 | tf_op jit(solution)/shard_map/ppermute | solution.py:27
  23.4 3.0 %collective-permute-start.4 = (bf16[320,256]{1,0:T(8,128)(2,1)S(1)}, bf16[320,256]{1,0:T(8,128)(2,1)S(1)}, u32[]{:S(2)}, u32[]{:S(2)}) collective-permute-start(bf16[320,256]{1,0:T(8,128)(2,1)S(1)} %collective-permute-done.3.refs_2_), channel_id=1, source_target_pairs={{0,1},{1,0},{2,3},{3,2},{4,5},{5,4},{6,7},{7,6},{8,9},{9,8},{10,11... | collective-permute-start | bytes 491528 | tf_op jit(solution)/shard_map/ppermute | solution.py:27
  23.5 2.9 %collective-permute-start.6 = (bf16[320,256]{1,0:T(8,128)(2,1)S(1)}, bf16[320,256]{1,0:T(8,128)(2,1)S(1)}, u32[]{:S(2)}, u32[]{:S(2)}) collective-permute-start(bf16[320,256]{1,0:T(8,128)(2,1)S(1)} %collective-permute-done.5.refs_3_), channel_id=1, source_target_pairs={{0,1},{1,0},{2,3},{3,2},{4,5},{5,4},{6,7},{7,6},{8,9},{9,8},{10,11... | collective-permute-start | bytes 491528 | tf_op jit(solution)/shard_map/ppermute | solution.py:27
  28.8 3.7 %collective-permute-start.10 = (f32[8,128]{1,0:T(8,128)S(1)}, f32[8,128]{1,0:T(8,128)S(1)}, u32[]{:S(2)}, u32[]{:S(2)}) collective-permute-start(f32[8,128]{1,0:T(8,128)S(1)} %get-tuple-element.40), channel_id=1, source_target_pairs={{0,2},{1,3},{2,0},{3,1},{4,6},{5,7},{6,4},{7,5},{8,10},{9,11},{10,... | collective-permute-start | bytes 12296 | tf_op jit(solution)/shard_map/ppermute | solution.py:27
  29.9 3.6 %collective-permute-start.11 = (f32[8,128]{1,0:T(8,128)S(1)}, f32[8,128]{1,0:T(8,128)S(1)}, u32[]{:S(2)}, u32[]{:S(2)}) collective-permute-start(f32[8,128]{1,0:T(8,128)S(1)} %get-tuple-element.41), channel_id=1, source_target_pairs={{0,4},{1,5},{2,6},{3,7},{4,0},{5,1},{6,2},{7,3},{8,12},{9,13},{10,... | collective-permute-start | bytes 12296 | tf_op jit(solution)/shard_map/ppermute | solution.py:27
  30.8 4.5 %collective-permute-start.12 = (f32[8,128]{1,0:T(8,128)S(1)}, f32[8,128]{1,0:T(8,128)S(1)}, u32[]{:S(2)}, u32[]{:S(2)}) collective-permute-start(f32[8,128]{1,0:T(8,128)S(1)} %get-tuple-element.42), channel_id=1, source_target_pairs={{0,6},{1,7},{2,4},{3,5},{4,2},{5,3},{6,0},{7,1},{8,14},{9,15},{10,... | collective-permute-start | bytes 12296 | tf_op jit(solution)/shard_map/ppermute | solution.py:27

commit v3 on v2

--- a/solution.py
+++ b/solution.py
@@ -61,7 +61,7 @@
     pairs, tokens, rows = table.shape[1], acts.shape[0], shards[0].shape[1]
     chunk = pltpu.VMEM((CORES, tokens, 2 * BLOCK), jnp.bfloat16)
     packed = pltpu.VMEM((5 * rows, BLOCK), jnp.bfloat16)
-    large = [pltpu.with_memory_space_constraint(a, pltpu.HBM) for a in (acts, grads, *shards)]
+    table, *large = [pltpu.with_memory_space_constraint(a, pltpu.HBM) for a in (table, acts, grads, *shards)]
     chips = pairs // CORES
     return pl.pallas_call(
         pack_kernel,
@@ -80,14 +80,7 @@
     )(table, *large)
 
 
-def precond_kernel(rows, *refs):
-    pieces = refs[:-4]
-    basis_act_ref, basis_grad_t_ref, precond_ref, full = refs[-4:]
-    me = lax.axis_index("seq")
-    for m, piece in enumerate(pieces):
-        place = pl.ds(pl.multiple_of((me ^ m) * rows, rows), rows)
-        for part in range(5):
-            full[part, place, :] = piece[part * rows : (part + 1) * rows, :]
+def precond(full, basis_act_ref, basis_grad_t_ref, precond_ref):
     basis_act, basis_grad = full[0], full[1]
     basis_act_ref[...] = basis_act
     basis_grad_t_ref[...] = basis_grad.astype(jnp.float32).T.astype(jnp.bfloat16)
@@ -102,21 +95,40 @@
         precond_ref[q] = (outer * scale).astype(jnp.bfloat16)
 
 
-def make_precond(pieces):
-    rows = pieces[0].shape[0] // 5
+def own_kernel(rows, *refs):
+    pieces, full, weights = refs[:-4], refs[-4], refs[-3:]
+    me = lax.axis_index("seq")
+    for m, piece in enumerate(pieces):
+        place = pl.ds(pl.multiple_of((me ^ m) * rows, rows), rows)
+        for part in range(5):
+            full[part, place, :] = piece[part * rows : (part + 1) * rows, :]
+    precond(full, *weights)
+
+
+def make_precond(kernel, name, operands, more):
     square = jax.ShapeDtypeStruct((BLOCK, BLOCK), jnp.bfloat16)
+    outs = more + (square, square, jax.ShapeDtypeStruct((QUERIES, BLOCK, BLOCK), jnp.bfloat16))
     return pl.pallas_call(
-        functools.partial(precond_kernel, rows),
-        out_shape=(square, square, jax.ShapeDtypeStruct((QUERIES, BLOCK, BLOCK), jnp.bfloat16)),
-        in_specs=[VMEM] * len(pieces),
-        out_specs=(VMEM, VMEM, VMEM),
-        scratch_shapes=[pltpu.VMEM((5, BLOCK, BLOCK), jnp.bfloat16)],
+        kernel,
+        out_shape=outs,
+        in_specs=[VMEM] * len(operands),
+        out_specs=(VMEM,) * len(outs),
         compiler_params=pltpu.CompilerParams(vmem_limit_bytes=VMEM_BYTES),
         cost_estimate=pl.CostEstimate(
             flops=2 * BLOCK**3 * 3, bytes_accessed=2 * BLOCK * BLOCK * 15, transcendentals=0
         ),
-        name="make_precond",
-    )(*pieces)
+        name=name,
+    )(*operands)
+
+
+def own_precond(pieces):
+    rows = pieces[0].shape[0] // 5
+    full = jax.ShapeDtypeStruct((5, BLOCK, BLOCK), jnp.bfloat16)
+    return make_precond(functools.partial(own_kernel, rows), "own_precond", pieces, (full,))
+
+
+def other_precond(full):
+    return make_precond(precond, "other_precond", (full,), ())
 
 
 def valid_mask(lengths_ref, start, shape):
@@ -200,11 +212,15 @@
         query_grads,
         eigenvalues,
     )
-    own = [packed] + [swap(packed, "seq", m) for m in range(1, groups)]
+    own = [packed]
+    for m in range(1, groups):
+        own.append(swap(own[m & (m - 1)], "seq", m & -m))
     chunks = chunks[:1] + [swap(chunks[m], "blk", CORES * m) for m in range(1, chips)]
-    other = [swap(piece, "blk", 1) for piece in own]
-    scores = partial_scores(0, seq_lengths, make_precond(own), chunks, ())
-    scores = partial_scores(1, seq_lengths, make_precond(other), chunks, scores)
+    own, chunks = lax.optimization_barrier((own, chunks))
+    full, *weights = own_precond(own)
+    other = other_precond(swap(full, "blk", 1))
+    scores = partial_scores(0, seq_lengths, weights, chunks, ())
+    scores = partial_scores(1, seq_lengths, other, chunks, scores)
     total = scores[0]
     for m in range(1, chips):
         total = total + swap(scores[m], "blk", CORES * m)

time: 36.1 us -> 34.3 us (0.950)
  starting transfers between devices: 16.4 us -> 13.5 us
  waiting for transfers between devices: 11.3 us -> 12.8 us
  local copies, waits for them, and re-layouts: 0.7 us -> 0.01 us
    ppermute x13 -> x10, starting transfers between devices: 16.4 us -> 13.5 us  [swap(): lax.ppermute(array, axis, [(i, i ^ bits) for i in range(lax.axis_size(axi...]
    ppermute x13 -> x10, waiting for transfers between devices: 11.3 us -> 12.8 us  [swap(): lax.ppermute(array, axis, [(i, i ^ bits) for i in range(lax.axis_size(axi...]
    unnamed x4 -> x2, local copies, waits for them, and re-layouts: 0.7 us -> 0.01 us
  transfers between devices with their start and end apart: 13 -> 10, of which waited for: 4 -> 7; matrix products, arithmetic and copies ran while one was open for 0% -> 0% of each run, Pallas kernels for 7% -> 5%
where the time goes in v3:
time: 34.3 us; the launch traced here: 34.1 us
  starting transfers between devices  13.5 us (39%)
  waiting for transfers between devices  12.8 us (37%)
  Pallas kernels  7.15 us (21%)
  other arithmetic  0.6 us (2%)
    ppermute x10, starting transfers between devices, swap(): lax.ppermute(array, axis, [(i, i ^ bits) for i in range(lax.axis_size(axi...  13.5 us
    ppermute x10, waiting for transfers between devices, swap(): lax.ppermute(array, axis, [(i, i ^ bits) for i in range(lax.axis_size(axi...  12.8 us
    pallas_call x2, Pallas kernels, partial_scores(): pl.pallas_call(functools.partial(score_kernel, core, chips), out_shape=(j...  3.47 us
    pallas_call x1, Pallas kernels, pack(): pl.pallas_call(pack_kernel, out_shape=(packed,) + (chunk,) * chips, in_sp...  2.32 us
    pallas_call x2, Pallas kernels, make_precond(): pl.pallas_call(kernel, out_shape=outs, in_specs=[VMEM] * len(operands), o...  1.36 us
  transfers between devices with their start and end apart: 10, of which 7 were waited for; matrix products, arithmetic and copies ran while one was open for 0% of the time, Pallas kernels for 5%

profile of v3, /device:TPU:0, one launch (start us, length us, event | category | flops | bytes accessed | tf_op | source)
XLA Modules:
  0.0 34.1 jit_solution(14520176320330497486)
XLA Ops:
  0.0 0.0 copy-start
  0.0 2.3 %pack.1 = (bf16[320,256]{1,0:T(8,128)(2,1)S(1)}, bf16[2,128,512]{2,1,0:T(8,128)(2,1)S(1)}, bf16[2,128,512]{2,1,0:T(8,128)(2,1)S(1)}, bf16[2,128,512]{2,1,0:T(8,128)(2,1)S(1)}, bf16[2,128,512]{2,1,0:T(8,128)(2,1)S(1)}) custom-call(s32[2,8]{1,0:T(2,128)} %bitcast.1, bf16[128,4096]{1,0:T(8,128)(2,1)} %acts_ref.1, bf16[128,14336]{1,0:T(8,128)(2,1)} %grads_ref.1, ...), custom_call_target="tpu_custom_call" | custom-call | bytes 2097152 | tf_op jit(solution)/shard_map/pack/pallas_call | solution.py:66
  2.3 4.1 %collective-permute-start.1 = (bf16[320,256]{1,0:T(8,128)(2,1)S(1)}, bf16[320,256]{1,0:T(8,128)(2,1)S(1)}, u32[]{:S(2)}, u32[]{:S(2)}) collective-permute-start(bf16[320,256]{1,0:T(8,128)(2,1)S(1)} %get-tuple-element.38.refs_0_), channel_id=1, source_target_pairs={{0,16},{8,24},{16,0},{24,8},{1,17},{9,25},{17,1},{25,9},{2,18},{10... | collective-permute-start | bytes 491528 | tf_op jit(solution)/shard_map/ppermute | solution.py:27
  6.4 1.5 %collective-permute-start.3 = (bf16[2,128,512]{2,1,0:T(8,128)(2,1)S(1)}, bf16[2,128,512]{2,1,0:T(8,128)(2,1)S(1)}, u32[]{:S(2)}, u32[]{:S(2)}) collective-permute-start(bf16[2,128,512]{2,1,0:T(8,128)(2,1)S(1)} %get-tuple-element.35), channel_id=1, source_target_pairs={{0,2},{1,3},{2,0},{3,1},{4,6},{5,7},{6,4},{7,5},{8,10},{9,11},{10,... | collective-permute-start | bytes 786440 | tf_op jit(solution)/shard_map/ppermute | solution.py:27
  7.9 1.5 %collective-permute-start.4 = (bf16[2,128,512]{2,1,0:T(8,128)(2,1)S(1)}, bf16[2,128,512]{2,1,0:T(8,128)(2,1)S(1)}, u32[]{:S(2)}, u32[]{:S(2)}) collective-permute-start(bf16[2,128,512]{2,1,0:T(8,128)(2,1)S(1)} %get-tuple-element.36), channel_id=1, source_target_pairs={{0,4},{1,5},{2,6},{3,7},{4,0},{5,1},{6,2},{7,3},{8,12},{9,13},{10,... | collective-permute-start | bytes 786440 | tf_op jit(solution)/shard_map/ppermute | solution.py:27
  9.4 0.5 %collective-permute-start.5 = (bf16[2,128,512]{2,1,0:T(8,128)(2,1)S(1)}, bf16[2,128,512]{2,1,0:T(8,128)(2,1)S(1)}, u32[]{:S(2)}, u32[]{:S(2)}) collective-permute-start(bf16[2,128,512]{2,1,0:T(8,128)(2,1)S(1)} %get-tuple-element.37), channel_id=1, source_target_pairs={{0,6},{1,7},{2,4},{3,5},{4,2},{5,3},{6,0},{7,1},{8,14},{9,15},{10,... | collective-permute-start | bytes 786440 | tf_op jit(solution)/shard_map/ppermute | solution.py:27
  9.9 1.6 %collective-permute-start = (bf16[320,256]{1,0:T(8,128)(2,1)S(1)}, bf16[320,256]{1,0:T(8,128)(2,1)S(1)}, u32[]{:S(2)}, u32[]{:S(2)}) collective-permute-start(bf16[320,256]{1,0:T(8,128)(2,1)S(1)} %get-tuple-element.38.refs_0_), channel_id=1, source_target_pairs={{0,8},{8,0},{16,24},{24,16},{1,9},{9,1},{17,25},{25,17},{2,10},{10... | collective-permute-start | bytes 491528 | tf_op jit(solution)/shard_map/ppermute | solution.py:27
  11.5 2.7 %collective-permute-done.1.refs_2_ = bf16[320,256]{1,0:T(8,128)(2,1)S(1)} collective-permute-done((bf16[320,256]{1,0:T(8,128)(2,1)S(1)}, bf16[320,256]{1,0:T(8,128)(2,1)S(1)}, u32[]{:S(2)}, u32[]{:S(2)}) %collective-permute-start.1) | collective-permute-done | bytes 163872 | tf_op jit(solution)/shard_map/ppermute | solution.py:27
  14.2 0.7 %collective-permute-start.2 = (bf16[320,256]{1,0:T(8,128)(2,1)S(1)}, bf16[320,256]{1,0:T(8,128)(2,1)S(1)}, u32[]{:S(2)}, u32[]{:S(2)}) collective-permute-start(bf16[320,256]{1,0:T(8,128)(2,1)S(1)} %collective-permute-done.1.refs_2_), channel_id=1, source_target_pairs={{0,8},{8,0},{16,24},{24,16},{1,9},{9,1},{17,25},{25,17},{2,10},{10... | collective-permute-start | bytes 491528 | tf_op jit(solution)/shard_map/ppermute | solution.py:27
  14.9 2.9 %collective-permute-done.refs_1_ = bf16[320,256]{1,0:T(8,128)(2,1)S(1)} collective-permute-done((bf16[320,256]{1,0:T(8,128)(2,1)S(1)}, bf16[320,256]{1,0:T(8,128)(2,1)S(1)}, u32[]{:S(2)}, u32[]{:S(2)}) %collective-permute-start) | collective-permute-done | bytes 163872 | tf_op jit(solution)/shard_map/ppermute | solution.py:27
  17.8 0.0 collective-permute-done.3.refs_1_
  17.8 3.2 %collective-permute-done.4.refs_2_ = bf16[2,128,512]{2,1,0:T(8,128)(2,1)S(1)} collective-permute-done((bf16[2,128,512]{2,1,0:T(8,128)(2,1)S(1)}, bf16[2,128,512]{2,1,0:T(8,128)(2,1)S(1)}, u32[]{:S(2)}, u32[]{:S(2)}) %collective-permute-start.4) | collective-permute-done | bytes 262176 | tf_op jit(solution)/shard_map/ppermute | solution.py:27
  21.0 0.0 collective-permute-done.5.refs_3_
  21.0 0.0 collective-permute-done.2.refs_3_
  21.0 0.7 %own_precond.1 = (bf16[5,256,256]{2,1,0:T(8,128)(2,1)S(1)}, bf16[256,256]{1,0:T(8,128)(2,1)S(1)}, bf16[256,256]{1,0:T(8,128)(2,1)S(1)}, bf16[8,256,256]{2,1,0:T(8,128)(2,1)S(1)}) custom-call(bf16[320,256]{1,0:T(8,128)(2,1)S(1)} %get-tuple-element.38.refs_0_, bf16[320,256]{1,0:T(8,128)(2,1)S(1)} %collective-permute-done.refs_1_, ...), custom_call_target="tpu_custom_call" | custom-call | flops 100663296 | bytes 1966080 | tf_op jit(solution)/shard_map/own_precond/pallas_call | solution.py:111
  21.8 0.1 collective-permute-start.6
  21.8 0.0 copy-done
  21.8 1.7 %partial_scores.2 = (f32[8,128]{1,0:T(8,128)S(1)}, f32[8,128]{1,0:T(8,128)S(1)}, f32[8,128]{1,0:T(8,128)S(1)}, f32[8,128]{1,0:T(8,128)S(1)}) custom-call(s32[4]{0:T(128)S(1)} %copy-done, bf16[256,256]{1,0:T(8,128)(2,1)S(1)} %get-tuple-element.50.basis_act_ref, bf16[256,256]{1,0:T(8,128)(2,1)S(1)} %get-tuple-element.51.basis_grad_t_ref, ...), custom_call_target="tpu_custom_call" | custom-call | flops 671088640 | bytes 1835008 | tf_op jit(solution)/shard_map/partial_scores/pallas_call | solution.py:178
  23.6 0.3 %collective-permute-done.6.full = bf16[5,256,256]{2,1,0:T(8,128)(2,1)S(1)} collective-permute-done((bf16[5,256,256]{2,1,0:T(8,128)(2,1)S(1)}, bf16[5,256,256]{2,1,0:T(8,128)(2,1)S(1)}, u32[]{:S(2)}, u32[]{:S(2)}) %collective-permute-start.6) | collective-permute-done | bytes 655392 | tf_op jit(solution)/shard_map/ppermute | solution.py:27
  23.9 0.6 %other_precond.1 = (bf16[256,256]{1,0:T(8,128)(2,1)S(1)}, bf16[256,256]{1,0:T(8,128)(2,1)S(1)}, bf16[8,256,256]{2,1,0:T(8,128)(2,1)S(1)}) custom-call(bf16[5,256,256]{2,1,0:T(8,128)(2,1)S(1)} %collective-permute-done.6.full), custom_call_target="tpu_custom_call" | custom-call | flops 100663296 | bytes 1966080 | tf_op jit(solution)/shard_map/other_precond/pallas_call | solution.py:111
  24.6 1.7 %partial_scores.3 = (f32[8,128]{1,0:T(8,128)S(1)}, f32[8,128]{1,0:T(8,128)S(1)}, f32[8,128]{1,0:T(8,128)S(1)}, f32[8,128]{1,0:T(8,128)S(1)}) custom-call(s32[4]{0:T(128)S(1)} %copy-done, bf16[256,256]{1,0:T(8,128)(2,1)S(1)} %get-tuple-element.43.basis_act_ref, bf16[256,256]{1,0:T(8,128)(2,1)S(1)} %get-tuple-element.44.basis_grad_t_ref, ...), custom_call_target="tpu_custom_call" | custom-call | flops 671088640 | bytes 1835008 | tf_op jit(solution)/shard_map/partial_scores/pallas_call | solution.py:178
  26.3 1.3 %collective-permute-start.7 = (f32[8,128]{1,0:T(8,128)S(1)}, f32[8,128]{1,0:T(8,128)S(1)}, u32[]{:S(2)}, u32[]{:S(2)}) collective-permute-start(f32[8,128]{1,0:T(8,128)S(1)} %get-tuple-element.58), channel_id=1, source_target_pairs={{0,2},{1,3},{2,0},{3,1},{4,6},{5,7},{6,4},{7,5},{8,10},{9,11},{10,... | collective-permute-start | bytes 12296 | tf_op jit(solution)/shard_map/ppermute | solution.py:27
  27.6 1.4 %collective-permute-start.8 = (f32[8,128]{1,0:T(8,128)S(1)}, f32[8,128]{1,0:T(8,128)S(1)}, u32[]{:S(2)}, u32[]{:S(2)}) collective-permute-start(f32[8,128]{1,0:T(8,128)S(1)} %get-tuple-element.59), channel_id=1, source_target_pairs={{0,4},{1,5},{2,6},{3,7},{4,0},{5,1},{6,2},{7,3},{8,12},{9,13},{10,... | collective-permute-start | bytes 12296 | tf_op jit(solution)/shard_map/ppermute | solution.py:27
  29.0 0.9 %collective-permute-start.9 = (f32[8,128]{1,0:T(8,128)S(1)}, f32[8,128]{1,0:T(8,128)S(1)}, u32[]{:S(2)}, u32[]{:S(2)}) collective-permute-start(f32[8,128]{1,0:T(8,128)S(1)} %get-tuple-element.60), channel_id=1, source_target_pairs={{0,6},{1,7},{2,4},{3,5},{4,2},{5,3},{6,0},{7,1},{8,14},{9,15},{10,... | collective-permute-start | bytes 12296 | tf_op jit(solution)/shard_map/ppermute | solution.py:27
  29.9 0.1 collective-permute-done.7
  30.0 1.2 %collective-permute-done.8 = f32[8,128]{1,0:T(8,128)S(1)} collective-permute-done((f32[8,128]{1,0:T(8,128)S(1)}, f32[8,128]{1,0:T(8,128)S(1)}, u32[]{:S(2)}, u32[]{:S(2)}) %collective-permute-start.8) | collective-permute-done | bytes 4128 | tf_op jit(solution)/shard_map/ppermute | solution.py:27
  31.2 2.3 %collective-permute-done.9 = f32[8,128]{1,0:T(8,128)S(1)} collective-permute-done((f32[8,128]{1,0:T(8,128)S(1)}, f32[8,128]{1,0:T(8,128)S(1)}, u32[]{:S(2)}, u32[]{:S(2)}) %collective-permute-start.9) | collective-permute-done | bytes 4128 | tf_op jit(solution)/shard_map/ppermute | solution.py:27
  33.5 0.6 %add_add_fusion = f32[8,128]{1,0:T(8,128)} fusion(f32[8,128]{1,0:T(8,128)S(1)} %collective-permute-done.9, f32[8,128]{1,0:T(8,128)S(1)} %collective-permute-done.8, f32[8,128]{1,0:T(8,128)S(1)} %get-tuple-element.57, f32[8,128]{1,0:T(8,128)S(1)} %collective-permute-done.7), kind=kLoop, calls=%fused_computation | loop fusion | flops 3072 | bytes 20480 | tf_op jit(solution)/shard_map/add | solution.py:226
Async XLA Ops:
  0.0 21.8 %copy-start = (s32[4]{0:T(128)S(1)}, s32[4]{0:T(128)}, u32[]{:S(2)}) copy-start(s32[4]{0:T(128)} %lengths_ref.3) | copy-start | bytes 52
  2.3 11.9 %collective-permute-start.1 = (bf16[320,256]{1,0:T(8,128)(2,1)S(1)}, bf16[320,256]{1,0:T(8,128)(2,1)S(1)}, u32[]{:S(2)}, u32[]{:S(2)}) collective-permute-start(bf16[320,256]{1,0:T(8,128)(2,1)S(1)} %get-tuple-element.38.refs_0_), channel_id=1, source_target_pairs={{0,16},{8,24},{16,0},{24,8},{1,17},{9,25},{17,1},{25,9},{2,18},{10... | collective-permute-start | bytes 491528 | tf_op jit(solution)/shard_map/ppermute | solution.py:27
  6.4 11.4 %collective-permute-start.3 = (bf16[2,128,512]{2,1,0:T(8,128)(2,1)S(1)}, bf16[2,128,512]{2,1,0:T(8,128)(2,1)S(1)}, u32[]{:S(2)}, u32[]{:S(2)}) collective-permute-start(bf16[2,128,512]{2,1,0:T(8,128)(2,1)S(1)} %get-tuple-element.35), channel_id=1, source_target_pairs={{0,2},{1,3},{2,0},{3,1},{4,6},{5,7},{6,4},{7,5},{8,10},{9,11},{10,... | collective-permute-start | bytes 786440 | tf_op jit(solution)/shard_map/ppermute | solution.py:27
  7.9 13.1 %collective-permute-start.4 = (bf16[2,128,512]{2,1,0:T(8,128)(2,1)S(1)}, bf16[2,128,512]{2,1,0:T(8,128)(2,1)S(1)}, u32[]{:S(2)}, u32[]{:S(2)}) collective-permute-start(bf16[2,128,512]{2,1,0:T(8,128)(2,1)S(1)} %get-tuple-element.36), channel_id=1, source_target_pairs={{0,4},{1,5},{2,6},{3,7},{4,0},{5,1},{6,2},{7,3},{8,12},{9,13},{10,... | collective-permute-start | bytes 786440 | tf_op jit(solution)/shard_map/ppermute | solution.py:27
  9.4 11.6 %collective-permute-start.5 = (bf16[2,128,512]{2,1,0:T(8,128)(2,1)S(1)}, bf16[2,128,512]{2,1,0:T(8,128)(2,1)S(1)}, u32[]{:S(2)}, u32[]{:S(2)}) collective-permute-start(bf16[2,128,512]{2,1,0:T(8,128)(2,1)S(1)} %get-tuple-element.37), channel_id=1, source_target_pairs={{0,6},{1,7},{2,4},{3,5},{4,2},{5,3},{6,0},{7,1},{8,14},{9,15},{10,... | collective-permute-start | bytes 786440 | tf_op jit(solution)/shard_map/ppermute | solution.py:27
  9.9 7.9 %collective-permute-start = (bf16[320,256]{1,0:T(8,128)(2,1)S(1)}, bf16[320,256]{1,0:T(8,128)(2,1)S(1)}, u32[]{:S(2)}, u32[]{:S(2)}) collective-permute-start(bf16[320,256]{1,0:T(8,128)(2,1)S(1)} %get-tuple-element.38.refs_0_), channel_id=1, source_target_pairs={{0,8},{8,0},{16,24},{24,16},{1,9},{9,1},{17,25},{25,17},{2,10},{10... | collective-permute-start | bytes 491528 | tf_op jit(solution)/shard_map/ppermute | solution.py:27
  14.2 6.8 %collective-permute-start.2 = (bf16[320,256]{1,0:T(8,128)(2,1)S(1)}, bf16[320,256]{1,0:T(8,128)(2,1)S(1)}, u32[]{:S(2)}, u32[]{:S(2)}) collective-permute-start(bf16[320,256]{1,0:T(8,128)(2,1)S(1)} %collective-permute-done.1.refs_2_), channel_id=1, source_target_pairs={{0,8},{8,0},{16,24},{24,16},{1,9},{9,1},{17,25},{25,17},{2,10},{10... | collective-permute-start | bytes 491528 | tf_op jit(solution)/shard_map/ppermute | solution.py:27
  21.8 2.2 %collective-permute-start.6 = (bf16[5,256,256]{2,1,0:T(8,128)(2,1)S(1)}, bf16[5,256,256]{2,1,0:T(8,128)(2,1)S(1)}, u32[]{:S(2)}, u32[]{:S(2)}) collective-permute-start(bf16[5,256,256]{2,1,0:T(8,128)(2,1)S(1)} %get-tuple-element.42), channel_id=1, source_target_pairs={{0,1},{1,0},{2,3},{3,2},{4,5},{5,4},{6,7},{7,6},{8,9},{9,8},{10,11... | collective-permute-start | bytes 1966088 | tf_op jit(solution)/shard_map/ppermute | solution.py:27
  26.3 3.7 %collective-permute-start.7 = (f32[8,128]{1,0:T(8,128)S(1)}, f32[8,128]{1,0:T(8,128)S(1)}, u32[]{:S(2)}, u32[]{:S(2)}) collective-permute-start(f32[8,128]{1,0:T(8,128)S(1)} %get-tuple-element.58), channel_id=1, source_target_pairs={{0,2},{1,3},{2,0},{3,1},{4,6},{5,7},{6,4},{7,5},{8,10},{9,11},{10,... | collective-permute-start | bytes 12296 | tf_op jit(solution)/shard_map/ppermute | solution.py:27
  27.6 3.6 %collective-permute-start.8 = (f32[8,128]{1,0:T(8,128)S(1)}, f32[8,128]{1,0:T(8,128)S(1)}, u32[]{:S(2)}, u32[]{:S(2)}) collective-permute-start(f32[8,128]{1,0:T(8,128)S(1)} %get-tuple-element.59), channel_id=1, source_target_pairs={{0,4},{1,5},{2,6},{3,7},{4,0},{5,1},{6,2},{7,3},{8,12},{9,13},{10,... | collective-permute-start | bytes 12296 | tf_op jit(solution)/shard_map/ppermute | solution.py:27
  29.0 4.5 %collective-permute-start.9 = (f32[8,128]{1,0:T(8,128)S(1)}, f32[8,128]{1,0:T(8,128)S(1)}, u32[]{:S(2)}, u32[]{:S(2)}) collective-permute-start(f32[8,128]{1,0:T(8,128)S(1)} %get-tuple-element.60), channel_id=1, source_target_pairs={{0,6},{1,7},{2,4},{3,5},{4,2},{5,3},{6,0},{7,1},{8,14},{9,15},{10,... | collective-permute-start | bytes 12296 | tf_op jit(solution)/shard_map/ppermute | solution.py:27

commit v4 on v2

v4 whole, which is shorter than its diff:
```python
import functools

import jax
import jax.numpy as jnp
from jax import lax
from jax.experimental import pallas as pl
from jax.experimental.pallas import tpu as pltpu
from jax.sharding import PartitionSpec as P

BLOCK = 256
SEQ_LEN = 1024
QUERIES = 8
QTOK = 32
DAMPING = 0.1
CORES = 2
WIDTH = 4
PACK_VMEM = 16 * 1024 * 1024
VMEM_BYTES = 24 * 1024 * 1024

VMEM = pl.BlockSpec(memory_space=pltpu.VMEM)
HBM = pl.BlockSpec(memory_space=pltpu.HBM)
TT = (((0,), (1,)), ((), ()))
TN = (((0,), (0,)), ((), ()))


def swap(array, axis, bits):
    return lax.ppermute(array, axis, [(i, i ^ bits) for i in range(lax.axis_size(axis))])


def valid_mask(lengths, sequences, start, shape):
    position = start + lax.broadcasted_iota(jnp.int32, shape, 1)
    low = start // SEQ_LEN
    valid = jnp.zeros(shape, jnp.float32)
    for s in range((shape[1] + SEQ_LEN - 2) // SEQ_LEN + 1):
        sequence = jnp.minimum(low + s, sequences - 1)
        offset = position - sequence * SEQ_LEN
        valid = jnp.where((offset >= 0) & (offset < lengths[sequence]), 1.0, valid)
    return valid


def pack_kernel(table_ref, lengths_ref, acts_ref, grads_ref, *refs):
    shards, packed_ref, mask_ref = refs[:5], refs[5], refs[6]
    chunks, (raw_eigen, table, lengths, sem) = refs[7:-4], refs[-4:]
    me = lax.axis_index("blk")
    rows, tokens = raw_eigen.shape[0], acts_ref.shape[0]
    scalars = [
        pltpu.make_async_copy(table_ref, table, sem.at[0]),
        pltpu.make_async_copy(lengths_ref, lengths, sem.at[1]),
    ]
    weights = []
    for part, shard in enumerate(shards):
        target = raw_eigen if part == 4 else packed_ref.at[pl.ds(part * rows, rows), :]
        weights.append(pltpu.make_async_copy(shard.at[0], target, sem.at[2 + part]))
    for copy in scalars + weights:
        copy.start()
    scalars[0].wait()
    copies = []
    for m, chunk in enumerate(chunks):
        for core in range(CORES):
            owner = me ^ (CORES * m + core)
            for half, (source, row) in enumerate(((acts_ref, 1), (grads_ref, 0))):
                start = pl.multiple_of(table[row, owner] * BLOCK, BLOCK)
                copy = pltpu.make_async_copy(
                    source.at[:, pl.ds(start, BLOCK)],
                    chunk.at[core, :, pl.ds(half * BLOCK, BLOCK)],
                    sem.at[7 + len(copies)],
                )
                copy.start()
                copies.append(copy)
    scalars[1].wait()
    group = lax.axis_index("seq") * lax.axis_size("blk")
    for m in range(len(chunks)):
        start = (group + (me ^ (CORES * m))) * tokens
        mask_ref[m] = valid_mask(lengths, lengths_ref.shape[0], start, mask_ref.shape[1:])
    for copy in weights:
        copy.wait()
    packed_ref[4 * rows :, :] = raw_eigen[...].astype(jnp.bfloat16)
    for copy in copies:
        copy.wait()


def pack(table, lengths, acts, grads, *shards):
    pairs, tokens, rows = table.shape[1], acts.shape[0], shards[0].shape[1]
    chips = pairs // CORES
    chunk = pltpu.VMEM((CORES, tokens, 2 * BLOCK), jnp.bfloat16)
    packed = pltpu.VMEM((5 * rows, BLOCK), jnp.bfloat16)
    mask = pltpu.VMEM((chips, QUERIES, tokens), jnp.float32)
    operands = [
        pltpu.with_memory_space_constraint(a, pltpu.HBM) for a in (table, lengths, acts, grads, *shards)
    ]
    return pl.pallas_call(
        pack_kernel,
        out_shape=(packed, mask) + (chunk,) * chips,
        in_specs=[HBM] * len(operands),
        out_specs=(VMEM,) * (2 + chips),
        scratch_shapes=[
            pltpu.VMEM((rows, BLOCK), jnp.float32),
            pltpu.SMEM(table.shape, jnp.int32),
            pltpu.SMEM(lengths.shape, jnp.int32),
            pltpu.SemaphoreType.DMA((7 + 2 * pairs,)),
        ],
        compiler_params=pltpu.CompilerParams(vmem_limit_bytes=PACK_VMEM),
        cost_estimate=pl.CostEstimate(
            flops=0, bytes_accessed=pairs * tokens * BLOCK * 8, transcendentals=0
        ),
        name="pack",
    )(*operands)


def join_kernel(*refs):
    pieces, out = refs[:-1], refs[-1]
    rows = pieces[0].shape[0]
    for m, piece in enumerate(pieces):
        out[m * rows : (m + 1) * rows, :] = piece[...]


def join(pieces):
    rows = pieces[0].shape[0]
    return pl.pallas_call(
        join_kernel,
        out_shape=jax.ShapeDtypeStruct((len(pieces) * rows, BLOCK), jnp.bfloat16),
        in_specs=[VMEM] * len(pieces),
        out_specs=VMEM,
        compiler_params=pltpu.CompilerParams(vmem_limit_bytes=VMEM_BYTES),
        name="join",
    )(*pieces)


def pair_kernel(core, rows, chips, first_ref, last_ref, *refs):
    chunks, before = refs[:chips], refs[chips : -chips - 2]
    outs, full, precond = refs[-chips - 2 : -2], refs[-2], refs[-1]
    me = lax.axis_index("seq")
    if core:
        first_ref = first_ref.at[1 - lax.rem(lax.axis_index("blk"), CORES)]
    for odd, pieces in enumerate((first_ref, last_ref)):
        for i in range(pieces.shape[0] // (5 * rows)):
            place = pl.ds(pl.multiple_of((me ^ (2 * i + odd)) * rows, rows), rows)
            for part in range(5):
                start = (5 * i + part) * rows
                full[part, place, :] = pieces[start : start + rows, :]
    basis_act, basis_grad = full[0], full[1]
    qrot_acts = jnp.dot(full[2], basis_act, preferred_element_type=jnp.float32).astype(jnp.bfloat16)
    qrot_grads = jnp.dot(full[3], basis_grad, preferred_element_type=jnp.float32).astype(jnp.bfloat16)
    scale = 1.0 / (QTOK * (full[4].astype(jnp.float32) + DAMPING))
    for q in range(QUERIES):
        tokens = slice(q * QTOK, (q + 1) * QTOK)
        outer = lax.dot_general(
            qrot_grads[tokens], qrot_acts[tokens], TN, preferred_element_type=jnp.float32
        )
        precond[q] = (outer * scale).astype(jnp.bfloat16)
    tokens = chunks[0].shape[1]
    for m in range(0, chips, WIDTH):
        some = chunks[m : m + WIDTH]
        acts = jnp.concatenate([c[core, :, :BLOCK] for c in some], axis=0)
        grads = jnp.concatenate([c[core, :, BLOCK:] for c in some], axis=0)
        rot_acts = lax.dot_general(
            basis_act, acts, TT, preferred_element_type=jnp.float32
        ).astype(jnp.bfloat16)
        rot_grads = lax.dot_general(basis_grad, grads, TT, preferred_element_type=jnp.float32)
        sums = []
        for q in range(QUERIES):
            mixed = jnp.dot(precond[q], rot_acts, preferred_element_type=jnp.float32)
            sums.append(jnp.sum(mixed * rot_grads, axis=0, keepdims=True))
        scores = jnp.concatenate(sums, axis=0)
        for s in range(len(some)):
            part = scores[:, s * tokens : (s + 1) * tokens]
            if core:
                part = jnp.where(before[0][m + s] > 0, part + before[1 + m + s][...], 0.0)
            outs[m + s][...] = part


def pair_scores(core, first, last, chunks, before):
    chips, tokens = len(chunks), chunks[0].shape[1]
    rows = BLOCK // lax.axis_size("seq")
    operands = (first, last, *chunks, *before)
    return pl.pallas_call(
        functools.partial(pair_kernel, core, rows, chips),
        out_shape=(jax.ShapeDtypeStruct((QUERIES, tokens), jnp.float32),) * chips,
        in_specs=[VMEM] * len(operands),
        out_specs=(VMEM,) * chips,
        scratch_shapes=[
            pltpu.VMEM((5, BLOCK, BLOCK), jnp.bfloat16),
            pltpu.VMEM((QUERIES, BLOCK, BLOCK), jnp.bfloat16),
        ],
        compiler_params=pltpu.CompilerParams(vmem_limit_bytes=VMEM_BYTES),
        cost_estimate=pl.CostEstimate(
            flops=2 * chips * tokens * BLOCK * BLOCK * (QUERIES + 2),
            bytes_accessed=2 * BLOCK * (chips * tokens * 2 + BLOCK * (QUERIES + 2)),
            transcendentals=0,
        ),
        name="pair_scores",
    )(*operands)


def on_device(
    train_acts,
    train_grads,
    block_table,
    seq_lengths,
    query_acts,
    query_grads,
    basis_acts,
    basis_grads,
    eigenvalues,
):
    groups, chips = lax.axis_size("seq"), lax.axis_size("blk") // CORES
    packed, mask, *chunks = pack(
        block_table.T,
        seq_lengths,
        train_acts,
        train_grads,
        basis_acts,
        basis_grads,
        query_acts,
        query_grads,
        eigenvalues,
    )
    own = [packed]
    for m in range(1, groups):
        own.append(swap(own[m & (m - 1)], "seq", m & -m))
    far = sorted(range(1, chips), key=lambda m: -m.bit_count())
    chunks = [chunks[0]] + [swap(chunks[m], "blk", CORES * m) for m in far]
    first = join(own[::2])
    pairs = [list(range(c, c + CORES)) for c in range(0, chips * CORES, CORES)]
    both = lax.all_gather(first, "blk", axis=0, axis_index_groups=pairs)
    first, last, both, chunks = lax.optimization_barrier((first, own[1::2], both, chunks))
    chunks = [chunks[0]] + [chunks[1 + far.index(m)] for m in range(1, chips)]
    last = join(last)
    there = swap(last, "blk", 1)
    scores = pair_scores(0, first, last, chunks, ())
    scores = pair_scores(1, both, there, chunks, (mask, *scores))
    total = scores[0]
    for m in [k ^ (k >> 1) for k in range(1, chips)]:
        total = total + swap(scores[m], "blk", CORES * m)
    return total


def solution(mesh):
    in_specs = (
        P(("seq", "blk"), None),
        P(("seq", "blk"), None),
        P(),
        P(),
        P("blk", "seq", None),
        P("blk", "seq", None),
        P("blk", "seq", None),
        P("blk", "seq", None),
        P("blk", "seq", None),
    )
    out_specs = P(None, ("seq", "blk"))
    return jax.shard_map(
        on_device, mesh=mesh, in_specs=in_specs, out_specs=out_specs, check_vma=False
    )
```

time: 36.1 us -> 31.2 us (0.86)
  starting transfers between devices: 16.4 us -> 13.5 us
  blocking collectives: 0 us -> 2.26 us
  waiting for transfers between devices: 11.3 us -> 9.46 us
  Pallas kernels: 6.85 us -> 5.08 us
  local copies, waits for them, and re-layouts: 0.7 us -> 0 us
    ppermute x13 -> x10, starting transfers between devices: 16.4 us -> 13.5 us  [swap(): lax.ppermute(array, axis, [(i, i ^ bits) for i in range(lax.axis_size(axi...]
    all_gather x0 -> x1, blocking collectives: none -> 2.26 us  [on_device(): both = lax.all_gather(first, 'blk', axis=0, axis_index_groups=pairs)]
    ppermute x13 -> x10, waiting for transfers between devices: 11.3 us -> 9.46 us  [swap(): lax.ppermute(array, axis, [(i, i ^ bits) for i in range(lax.axis_size(axi...]
    pallas_call x5, Pallas kernels: 6.85 us -> 5.08 us  [the longest x2 2.9 us: pair_scores(): pl.pallas_call(functools.partial(pair_kernel, core, rows, chips), out_sha...]
    unnamed x4 -> x0, local copies, waits for them, and re-layouts: 0.7 us -> none
  transfers between devices with their start and end apart: 13 -> 10, of which waited for: 4 -> 7; matrix products, arithmetic and copies ran while one was open for 0% -> 0% of each run, Pallas kernels for 7% -> 5%
where the time goes in v4:
time: 31.2 us; the launch traced here: 31 us
  starting transfers between devices  13.5 us (43%)
  waiting for transfers between devices  9.46 us (30%)
  Pallas kernels  5.08 us (16%)
  blocking collectives  2.26 us (7%)
  other arithmetic  0.6 us (2%)
    ppermute x10, starting transfers between devices, swap(): lax.ppermute(array, axis, [(i, i ^ bits) for i in range(lax.axis_size(axi...  13.5 us
    ppermute x10, waiting for transfers between devices, swap(): lax.ppermute(array, axis, [(i, i ^ bits) for i in range(lax.axis_size(axi...  9.46 us
    pallas_call x2, Pallas kernels, pair_scores(): pl.pallas_call(functools.partial(pair_kernel, core, rows, chips), out_sha...  2.9 us
    all_gather x1, blocking collectives, on_device(): both = lax.all_gather(first, 'blk', axis=0, axis_index_groups=pairs)  2.26 us
    pallas_call x1, Pallas kernels, pack(): pl.pallas_call(pack_kernel, out_shape=(packed, mask) + (chunk,) * chips,...  2.13 us
  transfers between devices with their start and end apart: 10, of which 7 were waited for; matrix products, arithmetic and copies ran while one was open for 0% of the time, Pallas kernels for 5%

profile of v4, /device:TPU:0, one launch (start us, length us, event | category | flops | bytes accessed | tf_op | source)
XLA Modules:
  0.0 31.0 jit_solution(14050520997710848982)
XLA Ops:
  0.0 2.1 %pack.1 = (bf16[320,256]{1,0:T(8,128)(2,1)S(1)}, f32[4,8,128]{2,1,0:T(8,128)S(1)}, bf16[2,128,512]{2,1,0:T(8,128)(2,1)S(1)}, bf16[2,128,512]{2,1,0:T(8,128)(2,1)...) custom-call(s32[2,8]{1,0:T(2,128)} %bitcast.3, s32[4]{0:T(128)} %lengths_ref.1, ...), custom_call_target="tpu_custom_call" | custom-call | bytes 2097152 | tf_op jit(solution)/shard_map/pack/pallas_call | solution.py:91
  2.1 4.1 %collective-permute-start = (bf16[320,256]{1,0:T(8,128)(2,1)S(1)}, bf16[320,256]{1,0:T(8,128)(2,1)S(1)}, u32[]{:S(2)}, u32[]{:S(2)}) collective-permute-start(bf16[320,256]{1,0:T(8,128)(2,1)S(1)} %get-tuple-element.27.refs_0_), channel_id=1, source_target_pairs={{0,16},{8,24},{16,0},{24,8},{1,17},{9,25},{17,1},{25,9},{2,18},{10... | collective-permute-start | bytes 491528 | tf_op jit(solution)/shard_map/ppermute | solution.py:27
  6.2 2.4 %collective-permute-start.3 = (bf16[2,128,512]{2,1,0:T(8,128)(2,1)S(1)}, bf16[2,128,512]{2,1,0:T(8,128)(2,1)S(1)}, u32[]{:S(2)}, u32[]{:S(2)}) collective-permute-start(bf16[2,128,512]{2,1,0:T(8,128)(2,1)S(1)} %get-tuple-element.29), channel_id=1, source_target_pairs={{0,6},{1,7},{2,4},{3,5},{4,2},{5,3},{6,0},{7,1},{8,14},{9,15},{10,... | collective-permute-start | bytes 786440 | tf_op jit(solution)/shard_map/ppermute | solution.py:27
  8.7 0.5 %collective-permute-start.4 = (bf16[2,128,512]{2,1,0:T(8,128)(2,1)S(1)}, bf16[2,128,512]{2,1,0:T(8,128)(2,1)S(1)}, u32[]{:S(2)}, u32[]{:S(2)}) collective-permute-start(bf16[2,128,512]{2,1,0:T(8,128)(2,1)S(1)} %get-tuple-element.30), channel_id=1, source_target_pairs={{0,2},{1,3},{2,0},{3,1},{4,6},{5,7},{6,4},{7,5},{8,10},{9,11},{10,... | collective-permute-start | bytes 786440 | tf_op jit(solution)/shard_map/ppermute | solution.py:27
  9.2 0.5 %collective-permute-start.5 = (bf16[2,128,512]{2,1,0:T(8,128)(2,1)S(1)}, bf16[2,128,512]{2,1,0:T(8,128)(2,1)S(1)}, u32[]{:S(2)}, u32[]{:S(2)}) collective-permute-start(bf16[2,128,512]{2,1,0:T(8,128)(2,1)S(1)} %get-tuple-element.31), channel_id=1, source_target_pairs={{0,4},{1,5},{2,6},{3,7},{4,0},{5,1},{6,2},{7,3},{8,12},{9,13},{10,... | collective-permute-start | bytes 786440 | tf_op jit(solution)/shard_map/ppermute | solution.py:27
  9.7 1.6 %collective-permute-start.1 = (bf16[320,256]{1,0:T(8,128)(2,1)S(1)}, bf16[320,256]{1,0:T(8,128)(2,1)S(1)}, u32[]{:S(2)}, u32[]{:S(2)}) collective-permute-start(bf16[320,256]{1,0:T(8,128)(2,1)S(1)} %get-tuple-element.27.refs_0_), channel_id=1, source_target_pairs={{0,8},{8,0},{16,24},{24,16},{1,9},{9,1},{17,25},{25,17},{2,10},{10... | collective-permute-start | bytes 491528 | tf_op jit(solution)/shard_map/ppermute | solution.py:27
  11.3 2.7 %collective-permute-done.refs_1_ = bf16[320,256]{1,0:T(8,128)(2,1)S(1)} collective-permute-done((bf16[320,256]{1,0:T(8,128)(2,1)S(1)}, bf16[320,256]{1,0:T(8,128)(2,1)S(1)}, u32[]{:S(2)}, u32[]{:S(2)}) %collective-permute-start) | collective-permute-done | bytes 163872 | tf_op jit(solution)/shard_map/ppermute | solution.py:27
  14.1 0.7 %collective-permute-start.2 = (bf16[320,256]{1,0:T(8,128)(2,1)S(1)}, bf16[320,256]{1,0:T(8,128)(2,1)S(1)}, u32[]{:S(2)}, u32[]{:S(2)}) collective-permute-start(bf16[320,256]{1,0:T(8,128)(2,1)S(1)} %collective-permute-done.refs_1_), channel_id=1, source_target_pairs={{0,8},{8,0},{16,24},{24,16},{1,9},{9,1},{17,25},{25,17},{2,10},{10... | collective-permute-start | bytes 491528 | tf_op jit(solution)/shard_map/ppermute | solution.py:27
  14.8 2.3 %all-gather = bf16[1280,256]{1,0:T(8,128)(2,1)S(1)} all-gather(bf16[640,256]{1,0:T(8,128)(2,1)S(1)} %join.2.first_ref), channel_id=2, replica_groups={{0,1},{2,3},{4,5},{6,7},{8,9},{10,11},{12,13},{14,15},{16,17},{18,19},{..., dimensions={0}, use_global_device_ids=true | all-gather | bytes 983040 | tf_op jit(solution)/shard_map/all_gather | solution.py:225
  17.1 0.6 %collective-permute-done.1.refs_0_ = bf16[320,256]{1,0:T(8,128)(2,1)S(1)} collective-permute-done((bf16[320,256]{1,0:T(8,128)(2,1)S(1)}, bf16[320,256]{1,0:T(8,128)(2,1)S(1)}, u32[]{:S(2)}, u32[]{:S(2)}) %collective-permute-start.1) | collective-permute-done | bytes 163872 | tf_op jit(solution)/shard_map/ppermute | solution.py:27
  17.6 0.0 collective-permute-done.3.refs_3_
  17.6 3.0 %collective-permute-done.4.refs_1_ = bf16[2,128,512]{2,1,0:T(8,128)(2,1)S(1)} collective-permute-done((bf16[2,128,512]{2,1,0:T(8,128)(2,1)S(1)}, bf16[2,128,512]{2,1,0:T(8,128)(2,1)S(1)}, u32[]{:S(2)}, u32[]{:S(2)}) %collective-permute-start.4) | collective-permute-done | bytes 262176 | tf_op jit(solution)/shard_map/ppermute | solution.py:27
  20.6 0.0 collective-permute-done.5.refs_2_
  20.6 0.0 collective-permute-done.2.refs_1_
  20.7 0.1 collective-permute-start.6
  20.7 1.4 %pair_scores.2 = (f32[8,128]{1,0:T(8,128)S(1)}, f32[8,128]{1,0:T(8,128)S(1)}, f32[8,128]{1,0:T(8,128)S(1)}, f32[8,128]{1,0:T(8,128)S(1)}) custom-call(bf16[640,256]{1,0:T(8,128)(2,1)S(1)} %join.2.first_ref, bf16[640,256]{1,0:T(8,128)(2,1)S(1)} %join.3.last_ref, bf16[2,128,512]{2,1,0:T(8,128)(2,1)S(1)} %get-tuple-element.35.refs_0_, ...), custom_call_target="tpu_custom_call" | custom-call | flops 671088640 | bytes 1835008 | tf_op jit(solution)/shard_map/pair_scores/pallas_call | solution.py:176
  22.2 0.2 collective-permute-done.6.last_ref
  22.4 1.5 %pair_scores.3 = (f32[8,128]{1,0:T(8,128)S(1)}, f32[8,128]{1,0:T(8,128)S(1)}, f32[8,128]{1,0:T(8,128)S(1)}, f32[8,128]{1,0:T(8,128)S(1)}) custom-call(bf16[2,640,256]{2,1,0:T(8,128)(2,1)S(1)} %bitcast.2, bf16[640,256]{1,0:T(8,128)(2,1)S(1)} %collective-permute-done.6.last_ref, bf16[2,128,512]{2,1,0:T(8,128)(2,1)S(1)} %get-tuple-element.35.refs_0_, ...), custom_call_target="tpu_custom_call" | custom-call | flops 671088640 | bytes 1835008 | tf_op jit(solution)/shard_map/pair_scores/pallas_call | solution.py:176
  23.8 1.6 %collective-permute-start.7 = (f32[8,128]{1,0:T(8,128)S(1)}, f32[8,128]{1,0:T(8,128)S(1)}, u32[]{:S(2)}, u32[]{:S(2)}) collective-permute-start(f32[8,128]{1,0:T(8,128)S(1)} %get-tuple-element.46), channel_id=1, source_target_pairs={{0,2},{1,3},{2,0},{3,1},{4,6},{5,7},{6,4},{7,5},{8,10},{9,11},{10,... | collective-permute-start | bytes 12296 | tf_op jit(solution)/shard_map/ppermute | solution.py:27
  25.4 1.4 %collective-permute-start.8 = (f32[8,128]{1,0:T(8,128)S(1)}, f32[8,128]{1,0:T(8,128)S(1)}, u32[]{:S(2)}, u32[]{:S(2)}) collective-permute-start(f32[8,128]{1,0:T(8,128)S(1)} %get-tuple-element.47), channel_id=1, source_target_pairs={{0,6},{1,7},{2,4},{3,5},{4,2},{5,3},{6,0},{7,1},{8,14},{9,15},{10,... | collective-permute-start | bytes 12296 | tf_op jit(solution)/shard_map/ppermute | solution.py:27
  26.8 0.6 %collective-permute-start.9 = (f32[8,128]{1,0:T(8,128)S(1)}, f32[8,128]{1,0:T(8,128)S(1)}, u32[]{:S(2)}, u32[]{:S(2)}) collective-permute-start(f32[8,128]{1,0:T(8,128)S(1)} %get-tuple-element.48), channel_id=1, source_target_pairs={{0,4},{1,5},{2,6},{3,7},{4,0},{5,1},{6,2},{7,3},{8,12},{9,13},{10,... | collective-permute-start | bytes 12296 | tf_op jit(solution)/shard_map/ppermute | solution.py:27
  27.4 0.1 collective-permute-done.7
  27.5 2.4 %collective-permute-done.8 = f32[8,128]{1,0:T(8,128)S(1)} collective-permute-done((f32[8,128]{1,0:T(8,128)S(1)}, f32[8,128]{1,0:T(8,128)S(1)}, u32[]{:S(2)}, u32[]{:S(2)}) %collective-permute-start.8) | collective-permute-done | bytes 4128 | tf_op jit(solution)/shard_map/ppermute | solution.py:27
  29.9 0.5 %collective-permute-done.9 = f32[8,128]{1,0:T(8,128)S(1)} collective-permute-done((f32[8,128]{1,0:T(8,128)S(1)}, f32[8,128]{1,0:T(8,128)S(1)}, u32[]{:S(2)}, u32[]{:S(2)}) %collective-permute-start.9) | collective-permute-done | bytes 4128 | tf_op jit(solution)/shard_map/ppermute | solution.py:27
  30.4 0.6 %add_add_fusion = f32[8,128]{1,0:T(8,128)} fusion(f32[8,128]{1,0:T(8,128)S(1)} %collective-permute-done.9, f32[8,128]{1,0:T(8,128)S(1)} %collective-permute-done.8, f32[8,128]{1,0:T(8,128)S(1)} %get-tuple-element.45, f32[8,128]{1,0:T(8,128)S(1)} %collective-permute-done.7), kind=kLoop, calls=%fused_computation | loop fusion | flops 3072 | bytes 20480 | tf_op jit(solution)/shard_map/add | solution.py:234
  (2 shorter events, 0.0 us)
Async XLA Ops:
  2.1 11.9 %collective-permute-start = (bf16[320,256]{1,0:T(8,128)(2,1)S(1)}, bf16[320,256]{1,0:T(8,128)(2,1)S(1)}, u32[]{:S(2)}, u32[]{:S(2)}) collective-permute-start(bf16[320,256]{1,0:T(8,128)(2,1)S(1)} %get-tuple-element.27.refs_0_), channel_id=1, source_target_pairs={{0,16},{8,24},{16,0},{24,8},{1,17},{9,25},{17,1},{25,9},{2,18},{10... | collective-permute-start | bytes 491528 | tf_op jit(solution)/shard_map/ppermute | solution.py:27
  6.2 11.4 %collective-permute-start.3 = (bf16[2,128,512]{2,1,0:T(8,128)(2,1)S(1)}, bf16[2,128,512]{2,1,0:T(8,128)(2,1)S(1)}, u32[]{:S(2)}, u32[]{:S(2)}) collective-permute-start(bf16[2,128,512]{2,1,0:T(8,128)(2,1)S(1)} %get-tuple-element.29), channel_id=1, source_target_pairs={{0,6},{1,7},{2,4},{3,5},{4,2},{5,3},{6,0},{7,1},{8,14},{9,15},{10,... | collective-permute-start | bytes 786440 | tf_op jit(solution)/shard_map/ppermute | solution.py:27
  8.7 11.9 %collective-permute-start.4 = (bf16[2,128,512]{2,1,0:T(8,128)(2,1)S(1)}, bf16[2,128,512]{2,1,0:T(8,128)(2,1)S(1)}, u32[]{:S(2)}, u32[]{:S(2)}) collective-permute-start(bf16[2,128,512]{2,1,0:T(8,128)(2,1)S(1)} %get-tuple-element.30), channel_id=1, source_target_pairs={{0,2},{1,3},{2,0},{3,1},{4,6},{5,7},{6,4},{7,5},{8,10},{9,11},{10,... | collective-permute-start | bytes 786440 | tf_op jit(solution)/shard_map/ppermute | solution.py:27
  9.2 11.4 %collective-permute-start.5 = (bf16[2,128,512]{2,1,0:T(8,128)(2,1)S(1)}, bf16[2,128,512]{2,1,0:T(8,128)(2,1)S(1)}, u32[]{:S(2)}, u32[]{:S(2)}) collective-permute-start(bf16[2,128,512]{2,1,0:T(8,128)(2,1)S(1)} %get-tuple-element.31), channel_id=1, source_target_pairs={{0,4},{1,5},{2,6},{3,7},{4,0},{5,1},{6,2},{7,3},{8,12},{9,13},{10,... | collective-permute-start | bytes 786440 | tf_op jit(solution)/shard_map/ppermute | solution.py:27
  9.7 7.9 %collective-permute-start.1 = (bf16[320,256]{1,0:T(8,128)(2,1)S(1)}, bf16[320,256]{1,0:T(8,128)(2,1)S(1)}, u32[]{:S(2)}, u32[]{:S(2)}) collective-permute-start(bf16[320,256]{1,0:T(8,128)(2,1)S(1)} %get-tuple-element.27.refs_0_), channel_id=1, source_target_pairs={{0,8},{8,0},{16,24},{24,16},{1,9},{9,1},{17,25},{25,17},{2,10},{10... | collective-permute-start | bytes 491528 | tf_op jit(solution)/shard_map/ppermute | solution.py:27
  14.1 6.5 %collective-permute-start.2 = (bf16[320,256]{1,0:T(8,128)(2,1)S(1)}, bf16[320,256]{1,0:T(8,128)(2,1)S(1)}, u32[]{:S(2)}, u32[]{:S(2)}) collective-permute-start(bf16[320,256]{1,0:T(8,128)(2,1)S(1)} %collective-permute-done.refs_1_), channel_id=1, source_target_pairs={{0,8},{8,0},{16,24},{24,16},{1,9},{9,1},{17,25},{25,17},{2,10},{10... | collective-permute-start | bytes 491528 | tf_op jit(solution)/shard_map/ppermute | solution.py:27
  20.7 1.7 %collective-permute-start.6 = (bf16[640,256]{1,0:T(8,128)(2,1)S(1)}, bf16[640,256]{1,0:T(8,128)(2,1)S(1)}, u32[]{:S(2)}, u32[]{:S(2)}) collective-permute-start(bf16[640,256]{1,0:T(8,128)(2,1)S(1)} %join.3.last_ref), channel_id=1, source_target_pairs={{0,1},{1,0},{2,3},{3,2},{4,5},{5,4},{6,7},{7,6},{8,9},{9,8},{10,11... | collective-permute-start | bytes 983048 | tf_op jit(solution)/shard_map/ppermute | solution.py:27
  23.8 3.7 %collective-permute-start.7 = (f32[8,128]{1,0:T(8,128)S(1)}, f32[8,128]{1,0:T(8,128)S(1)}, u32[]{:S(2)}, u32[]{:S(2)}) collective-permute-start(f32[8,128]{1,0:T(8,128)S(1)} %get-tuple-element.46), channel_id=1, source_target_pairs={{0,2},{1,3},{2,0},{3,1},{4,6},{5,7},{6,4},{7,5},{8,10},{9,11},{10,... | collective-permute-start | bytes 12296 | tf_op jit(solution)/shard_map/ppermute | solution.py:27
  25.4 4.5 %collective-permute-start.8 = (f32[8,128]{1,0:T(8,128)S(1)}, f32[8,128]{1,0:T(8,128)S(1)}, u32[]{:S(2)}, u32[]{:S(2)}) collective-permute-start(f32[8,128]{1,0:T(8,128)S(1)} %get-tuple-element.47), channel_id=1, source_target_pairs={{0,6},{1,7},{2,4},{3,5},{4,2},{5,3},{6,0},{7,1},{8,14},{9,15},{10,... | collective-permute-start | bytes 12296 | tf_op jit(solution)/shard_map/ppermute | solution.py:27
  26.8 3.6 %collective-permute-start.9 = (f32[8,128]{1,0:T(8,128)S(1)}, f32[8,128]{1,0:T(8,128)S(1)}, u32[]{:S(2)}, u32[]{:S(2)}) collective-permute-start(f32[8,128]{1,0:T(8,128)S(1)} %get-tuple-element.48), channel_id=1, source_target_pairs={{0,4},{1,5},{2,6},{3,7},{4,0},{5,1},{6,2},{7,3},{8,12},{9,13},{10,... | collective-permute-start | bytes 12296 | tf_op jit(solution)/shard_map/ppermute | solution.py:27

commit v5 on v4

--- a/solution.py
+++ b/solution.py
@@ -38,7 +38,52 @@
     return valid
 
 
-def pack_kernel(table_ref, lengths_ref, acts_ref, grads_ref, *refs):
+def copy_blocks(table, distances, acts_ref, grads_ref, chunks, sem):
+    me = lax.axis_index("blk")
+    copies = []
+    for m, chunk in zip(distances, chunks):
+        for core in range(CORES):
+            owner = me ^ (CORES * m + core)
+            for half, (source, row) in enumerate(((acts_ref, 1), (grads_ref, 0))):
+                start = pl.multiple_of(table[row, owner] * BLOCK, BLOCK)
+                copy = pltpu.make_async_copy(
+                    source.at[:, pl.ds(start, BLOCK)],
+                    chunk.at[core, :, pl.ds(half * BLOCK, BLOCK)],
+                    sem.at[len(copies)],
+                )
+                copy.start()
+                copies.append(copy)
+    return copies
+
+
+def blocks_kernel(distances, table_ref, acts_ref, grads_ref, *refs):
+    chunks, (table, sem, table_sem) = refs[:-3], refs[-3:]
+    copy = pltpu.make_async_copy(table_ref, table, table_sem)
+    copy.start()
+    copy.wait()
+    for copy in copy_blocks(table, distances, acts_ref, grads_ref, chunks, sem):
+        copy.wait()
+
+
+def take_blocks(distances, table, acts, grads):
+    tokens = acts.shape[0]
+    operands = [pltpu.with_memory_space_constraint(a, pltpu.HBM) for a in (table, acts, grads)]
+    return pl.pallas_call(
+        functools.partial(blocks_kernel, distances),
+        out_shape=(pltpu.VMEM((CORES, tokens, 2 * BLOCK), jnp.bfloat16),) * len(distances),
+        in_specs=[HBM] * 3,
+        out_specs=(VMEM,) * len(distances),
+        scratch_shapes=[
+            pltpu.SMEM(table.shape, jnp.int32),
+            pltpu.SemaphoreType.DMA((2 * CORES * len(distances),)),
+            pltpu.SemaphoreType.DMA,
+        ],
+        compiler_params=pltpu.CompilerParams(vmem_limit_bytes=VMEM_BYTES),
+        name="take_blocks",
+    )(*operands)
+
+
+def pack_kernel(distances, table_ref, lengths_ref, acts_ref, grads_ref, *refs):
     shards, packed_ref, mask_ref = refs[:5], refs[5], refs[6]
     chunks, (raw_eigen, table, lengths, sem) = refs[7:-4], refs[-4:]
     me = lax.axis_index("blk")
@@ -54,22 +99,10 @@
     for copy in scalars + weights:
         copy.start()
     scalars[0].wait()
-    copies = []
-    for m, chunk in enumerate(chunks):
-        for core in range(CORES):
-            owner = me ^ (CORES * m + core)
-            for half, (source, row) in enumerate(((acts_ref, 1), (grads_ref, 0))):
-                start = pl.multiple_of(table[row, owner] * BLOCK, BLOCK)
-                copy = pltpu.make_async_copy(
-                    source.at[:, pl.ds(start, BLOCK)],
-                    chunk.at[core, :, pl.ds(half * BLOCK, BLOCK)],
-                    sem.at[7 + len(copies)],
-                )
-                copy.start()
-                copies.append(copy)
+    copies = copy_blocks(table, distances, acts_ref, grads_ref, chunks, sem.at[pl.ds(7, 2 * CORES)])
     scalars[1].wait()
     group = lax.axis_index("seq") * lax.axis_size("blk")
-    for m in range(len(chunks)):
+    for m in range(mask_ref.shape[0]):
         start = (group + (me ^ (CORES * m))) * tokens
         mask_ref[m] = valid_mask(lengths, lengths_ref.shape[0], start, mask_ref.shape[1:])
     for copy in weights:
@@ -79,7 +112,7 @@
         copy.wait()
 
 
-def pack(table, lengths, acts, grads, *shards):
+def pack(distances, table, lengths, acts, grads, *shards):
     pairs, tokens, rows = table.shape[1], acts.shape[0], shards[0].shape[1]
     chips = pairs // CORES
     chunk = pltpu.VMEM((CORES, tokens, 2 * BLOCK), jnp.bfloat16)
@@ -89,10 +122,10 @@
         pltpu.with_memory_space_constraint(a, pltpu.HBM) for a in (table, lengths, acts, grads, *shards)
     ]
     return pl.pallas_call(
-        pack_kernel,
-        out_shape=(packed, mask) + (chunk,) * chips,
+        functools.partial(pack_kernel, distances),
+        out_shape=(packed, mask) + (chunk,) * len(distances),
         in_specs=[HBM] * len(operands),
-        out_specs=(VMEM,) * (2 + chips),
+        out_specs=(VMEM,) * (2 + len(distances)),
         scratch_shapes=[
             pltpu.VMEM((rows, BLOCK), jnp.float32),
             pltpu.SMEM(table.shape, jnp.int32),
@@ -132,22 +165,18 @@
     me = lax.axis_index("seq")
     if core:
         first_ref = first_ref.at[1 - lax.rem(lax.axis_index("blk"), CORES)]
-    for odd, pieces in enumerate((first_ref, last_ref)):
-        for i in range(pieces.shape[0] // (5 * rows)):
-            place = pl.ds(pl.multiple_of((me ^ (2 * i + odd)) * rows, rows), rows)
+    m = 0
+    for pieces in (first_ref, last_ref):
+        for first in range(0, pieces.shape[0], 5 * rows):
+            place = pl.ds(pl.multiple_of((me ^ m) * rows, rows), rows)
             for part in range(5):
-                start = (5 * i + part) * rows
+                start = first + part * rows
                 full[part, place, :] = pieces[start : start + rows, :]
+            m += 1
     basis_act, basis_grad = full[0], full[1]
     qrot_acts = jnp.dot(full[2], basis_act, preferred_element_type=jnp.float32).astype(jnp.bfloat16)
     qrot_grads = jnp.dot(full[3], basis_grad, preferred_element_type=jnp.float32).astype(jnp.bfloat16)
     scale = 1.0 / (QTOK * (full[4].astype(jnp.float32) + DAMPING))
-    for q in range(QUERIES):
-        tokens = slice(q * QTOK, (q + 1) * QTOK)
-        outer = lax.dot_general(
-            qrot_grads[tokens], qrot_acts[tokens], TN, preferred_element_type=jnp.float32
-        )
-        precond[q] = (outer * scale).astype(jnp.bfloat16)
     tokens = chunks[0].shape[1]
     for m in range(0, chips, WIDTH):
         some = chunks[m : m + WIDTH]
@@ -157,6 +186,13 @@
             basis_act, acts, TT, preferred_element_type=jnp.float32
         ).astype(jnp.bfloat16)
         rot_grads = lax.dot_general(basis_grad, grads, TT, preferred_element_type=jnp.float32)
+        if m == 0:
+            for q in range(QUERIES):
+                rows_q = slice(q * QTOK, (q + 1) * QTOK)
+                outer = lax.dot_general(
+                    qrot_grads[rows_q], qrot_acts[rows_q], TN, preferred_element_type=jnp.float32
+                )
+                precond[q] = (outer * scale).astype(jnp.bfloat16)
         sums = []
         for q in range(QUERIES):
             mixed = jnp.dot(precond[q], rot_acts, preferred_element_type=jnp.float32)
@@ -204,7 +240,9 @@
     eigenvalues,
 ):
     groups, chips = lax.axis_size("seq"), lax.axis_size("blk") // CORES
-    packed, mask, *chunks = pack(
+    far = sorted(range(1, chips), key=lambda m: -m.bit_count())
+    packed, mask, *ahead = pack(
+        far[:1],
         block_table.T,
         seq_lengths,
         train_acts,
@@ -218,14 +256,17 @@
     own = [packed]
     for m in range(1, groups):
         own.append(swap(own[m & (m - 1)], "seq", m & -m))
-    far = sorted(range(1, chips), key=lambda m: -m.bit_count())
+    others = far[1:] + [0]
+    chunks = dict(zip(far[:1], ahead)) | dict(
+        zip(others, take_blocks(others, block_table.T, train_acts, train_grads))
+    )
     chunks = [chunks[0]] + [swap(chunks[m], "blk", CORES * m) for m in far]
-    first = join(own[::2])
+    early, chunks[1] = lax.optimization_barrier((own[:-1], chunks[1]))
+    first = join(early)
     pairs = [list(range(c, c + CORES)) for c in range(0, chips * CORES, CORES)]
     both = lax.all_gather(first, "blk", axis=0, axis_index_groups=pairs)
-    first, last, both, chunks = lax.optimization_barrier((first, own[1::2], both, chunks))
+    first, last, both, chunks = lax.optimization_barrier((first, own[-1], both, chunks))
     chunks = [chunks[0]] + [chunks[1 + far.index(m)] for m in range(1, chips)]
-    last = join(last)
     there = swap(last, "blk", 1)
     scores = pair_scores(0, first, last, chunks, ())
     scores = pair_scores(1, both, there, chunks, (mask, *scores))

time: 31.2 us -> 30.5 us (0.978)
  waiting for transfers between devices: 9.46 us -> 7.32 us
  Pallas kernels: 5.08 us -> 6.53 us
    ppermute x10, waiting for transfers between devices: 9.46 us -> 7.32 us  [swap(): lax.ppermute(array, axis, [(i, i ^ bits) for i in range(lax.axis_size(axi...]
    pallas_call x1 -> x2, Pallas kernels: 2.13 us -> 3.96 us  [the longest x1 2.11 us: take_blocks(): pl.pallas_call(functools.partial(blocks_kernel, distances), out_shape=(pl...]
    pallas_call x2, Pallas kernels: 2.9 us -> 2.53 us  [pair_scores(): pl.pallas_call(functools.partial(pair_kernel, core, rows, chips), out_sha...]
  transfers between devices with their start and end apart: 10 -> 10, of which waited for: 7 -> 8; matrix products, arithmetic and copies ran while one was open for 0% -> 0% of each run, Pallas kernels for 5% -> 11%
where the time goes in v5:
time: 30.5 us; the launch traced here: 30.2 us
  starting transfers between devices  13.2 us (43%)
  waiting for transfers between devices  7.32 us (24%)
  Pallas kernels  6.53 us (21%)
  blocking collectives  2.51 us (8%)
  other arithmetic  0.6 us (2%)
    ppermute x10, starting transfers between devices, swap(): lax.ppermute(array, axis, [(i, i ^ bits) for i in range(lax.axis_size(axi...  13.2 us
    ppermute x10, waiting for transfers between devices, swap(): lax.ppermute(array, axis, [(i, i ^ bits) for i in range(lax.axis_size(axi...  7.32 us
    pallas_call x2, Pallas kernels, pair_scores(): pl.pallas_call(functools.partial(pair_kernel, core, rows, chips), out_sha...  2.53 us
    all_gather x1, blocking collectives, on_device(): both = lax.all_gather(first, 'blk', axis=0, axis_index_groups=pairs)  2.51 us
    pallas_call x1, Pallas kernels, take_blocks(): pl.pallas_call(functools.partial(blocks_kernel, distances), out_shape=(pl...  2.11 us
    pallas_call x1, Pallas kernels, pack(): pl.pallas_call(functools.partial(pack_kernel, distances), out_shape=(pack...  1.85 us
  transfers between devices with their start and end apart: 10, of which 8 were waited for; matrix products, arithmetic and copies ran while one was open for 0% of the time, Pallas kernels for 11%

profile of v5, /device:TPU:0, one launch (start us, length us, event | category | flops | bytes accessed | tf_op | source)
XLA Modules:
  0.0 30.2 jit_solution(17800565303155325217)
XLA Ops:
  0.0 1.9 %pack.1 = (bf16[320,256]{1,0:T(8,128)(2,1)S(1)}, f32[4,8,128]{2,1,0:T(8,128)S(1)}, bf16[2,128,512]{2,1,0:T(8,128)(2,1)S(1)}) custom-call(s32[2,8]{1,0:T(2,128)} %bitcast.3, s32[4]{0:T(128)} %lengths_ref.1, bf16[128,4096]{1,0:T(8,128)(2,1)} %acts_ref.3, bf16[128,14336]{1,0:T(8,128)(2,1)} %grads_ref.3, bf16[1,64,256]{2,1,0:T(8,128)(2,1)} %refs_0_.1, ...), custom_call_target="tpu_custom_call" | custom-call | bytes 2097152 | tf_op jit(solution)/shard_map/pack/pallas_call | solution.py:124
  1.9 4.0 %collective-permute-start.2 = (bf16[2,128,512]{2,1,0:T(8,128)(2,1)S(1)}, bf16[2,128,512]{2,1,0:T(8,128)(2,1)S(1)}, u32[]{:S(2)}, u32[]{:S(2)}) collective-permute-start(bf16[2,128,512]{2,1,0:T(8,128)(2,1)S(1)} %get-tuple-element.31), channel_id=1, source_target_pairs={{0,6},{1,7},{2,4},{3,5},{4,2},{5,3},{6,0},{7,1},{8,14},{9,15},{10,... | collective-permute-start | bytes 786440 | tf_op jit(solution)/shard_map/ppermute | solution.py:27
  5.8 2.6 %collective-permute-start.1 = (bf16[320,256]{1,0:T(8,128)(2,1)S(1)}, bf16[320,256]{1,0:T(8,128)(2,1)S(1)}, u32[]{:S(2)}, u32[]{:S(2)}) collective-permute-start(bf16[320,256]{1,0:T(8,128)(2,1)S(1)} %get-tuple-element.32.refs_0_), channel_id=1, source_target_pairs={{0,16},{8,24},{16,0},{24,8},{1,17},{9,25},{17,1},{25,9},{2,18},{10... | collective-permute-start | bytes 491528 | tf_op jit(solution)/shard_map/ppermute | solution.py:27
  8.4 1.6 %collective-permute-start = (bf16[320,256]{1,0:T(8,128)(2,1)S(1)}, bf16[320,256]{1,0:T(8,128)(2,1)S(1)}, u32[]{:S(2)}, u32[]{:S(2)}) collective-permute-start(bf16[320,256]{1,0:T(8,128)(2,1)S(1)} %get-tuple-element.32.refs_0_), channel_id=1, source_target_pairs={{0,8},{8,0},{16,24},{24,16},{1,9},{9,1},{17,25},{25,17},{2,10},{10... | collective-permute-start | bytes 491528 | tf_op jit(solution)/shard_map/ppermute | solution.py:27
  10.0 2.1 %take_blocks.1 = (bf16[2,128,512]{2,1,0:T(8,128)(2,1)S(1)}, bf16[2,128,512]{2,1,0:T(8,128)(2,1)S(1)}, bf16[2,128,512]{2,1,0:T(8,128)(2,1)S(1)}) custom-call(s32[2,8]{1,0:T(2,128)} %bitcast.4, bf16[128,4096]{1,0:T(8,128)(2,1)} %acts_ref.3, bf16[128,14336]{1,0:T(8,128)(2,1)} %grads_ref.3), custom_call_target="tpu_custom_call" | custom-call | tf_op jit(solution)/shard_map/take_blocks/pallas_call | solution.py:71
  12.1 0.5 %collective-permute-start.4 = (bf16[2,128,512]{2,1,0:T(8,128)(2,1)S(1)}, bf16[2,128,512]{2,1,0:T(8,128)(2,1)S(1)}, u32[]{:S(2)}, u32[]{:S(2)}) collective-permute-start(bf16[2,128,512]{2,1,0:T(8,128)(2,1)S(1)} %get-tuple-element.37), channel_id=1, source_target_pairs={{0,2},{1,3},{2,0},{3,1},{4,6},{5,7},{6,4},{7,5},{8,10},{9,11},{10,... | collective-permute-start | bytes 786440 | tf_op jit(solution)/shard_map/ppermute | solution.py:27
  12.6 0.5 %collective-permute-start.5 = (bf16[2,128,512]{2,1,0:T(8,128)(2,1)S(1)}, bf16[2,128,512]{2,1,0:T(8,128)(2,1)S(1)}, u32[]{:S(2)}, u32[]{:S(2)}) collective-permute-start(bf16[2,128,512]{2,1,0:T(8,128)(2,1)S(1)} %get-tuple-element.38), channel_id=1, source_target_pairs={{0,4},{1,5},{2,6},{3,7},{4,0},{5,1},{6,2},{7,3},{8,12},{9,13},{10,... | collective-permute-start | bytes 786440 | tf_op jit(solution)/shard_map/ppermute | solution.py:27
  13.1 2.9 %collective-permute-done.1.refs_2_ = bf16[320,256]{1,0:T(8,128)(2,1)S(1)} collective-permute-done((bf16[320,256]{1,0:T(8,128)(2,1)S(1)}, bf16[320,256]{1,0:T(8,128)(2,1)S(1)}, u32[]{:S(2)}, u32[]{:S(2)}) %collective-permute-start.1) | collective-permute-done | bytes 163872 | tf_op jit(solution)/shard_map/ppermute | solution.py:27
  16.0 0.6 %collective-permute-start.3 = (bf16[320,256]{1,0:T(8,128)(2,1)S(1)}, bf16[320,256]{1,0:T(8,128)(2,1)S(1)}, u32[]{:S(2)}, u32[]{:S(2)}) collective-permute-start(bf16[320,256]{1,0:T(8,128)(2,1)S(1)} %collective-permute-done.1.refs_2_), channel_id=1, source_target_pairs={{0,8},{8,0},{16,24},{24,16},{1,9},{9,1},{17,25},{25,17},{2,10},{10... | collective-permute-start | bytes 491528 | tf_op jit(solution)/shard_map/ppermute | solution.py:27
  16.6 0.0 collective-permute-done.refs_1_
  16.6 0.0 collective-permute-done.2.refs_3_
  16.6 2.5 %all-gather = bf16[1920,256]{1,0:T(8,128)(2,1)S(1)} all-gather(bf16[960,256]{1,0:T(8,128)(2,1)S(1)} %join.1.first_ref), channel_id=2, replica_groups={{0,1},{2,3},{4,5},{6,7},{8,9},{10,11},{12,13},{14,15},{16,17},{18,19},{..., dimensions={0}, use_global_device_ids=true | all-gather | bytes 1474560 | tf_op jit(solution)/shard_map/all_gather | solution.py:267
  19.1 0.2 collective-permute-done.4.refs_1_
  19.4 0.1 collective-permute-done.5.refs_2_
  19.5 1.8 %collective-permute-done.3.last_ref = bf16[320,256]{1,0:T(8,128)(2,1)S(1)} collective-permute-done((bf16[320,256]{1,0:T(8,128)(2,1)S(1)}, bf16[320,256]{1,0:T(8,128)(2,1)S(1)}, u32[]{:S(2)}, u32[]{:S(2)}) %collective-permute-start.3) | collective-permute-done | bytes 163872 | tf_op jit(solution)/shard_map/ppermute | solution.py:27
  21.3 0.0 collective-permute-start.6
  21.3 1.3 %pair_scores.2 = (f32[8,128]{1,0:T(8,128)S(1)}, f32[8,128]{1,0:T(8,128)S(1)}, f32[8,128]{1,0:T(8,128)S(1)}, f32[8,128]{1,0:T(8,128)S(1)}) custom-call(bf16[960,256]{1,0:T(8,128)(2,1)S(1)} %join.1.first_ref, bf16[320,256]{1,0:T(8,128)(2,1)S(1)} %collective-permute-done.3.last_ref, bf16[2,128,512]{2,1,0:T(8,128)(2,1)S(1)} %get-tuple-element.41.refs_0_, ...), custom_call_target="tpu_custom_call" | custom-call | flops 671088640 | bytes 1835008 | tf_op jit(solution)/shard_map/pair_scores/pallas_call | solution.py:212
  22.6 0.1 collective-permute-done.6.last_ref
  22.7 1.3 %pair_scores.3 = (f32[8,128]{1,0:T(8,128)S(1)}, f32[8,128]{1,0:T(8,128)S(1)}, f32[8,128]{1,0:T(8,128)S(1)}, f32[8,128]{1,0:T(8,128)S(1)}) custom-call(bf16[2,960,256]{2,1,0:T(8,128)(2,1)S(1)} %bitcast.2, bf16[320,256]{1,0:T(8,128)(2,1)S(1)} %collective-permute-done.6.last_ref, bf16[2,128,512]{2,1,0:T(8,128)(2,1)S(1)} %get-tuple-element.41.refs_0_, ...), custom_call_target="tpu_custom_call" | custom-call | flops 671088640 | bytes 1835008 | tf_op jit(solution)/shard_map/pair_scores/pallas_call | solution.py:212
  24.0 0.6 %collective-permute-start.7 = (f32[8,128]{1,0:T(8,128)S(1)}, f32[8,128]{1,0:T(8,128)S(1)}, u32[]{:S(2)}, u32[]{:S(2)}) collective-permute-start(f32[8,128]{1,0:T(8,128)S(1)} %get-tuple-element.52), channel_id=1, source_target_pairs={{0,2},{1,3},{2,0},{3,1},{4,6},{5,7},{6,4},{7,5},{8,10},{9,11},{10,... | collective-permute-start | bytes 12296 | tf_op jit(solution)/shard_map/ppermute | solution.py:27
  24.6 1.4 %collective-permute-start.8 = (f32[8,128]{1,0:T(8,128)S(1)}, f32[8,128]{1,0:T(8,128)S(1)}, u32[]{:S(2)}, u32[]{:S(2)}) collective-permute-start(f32[8,128]{1,0:T(8,128)S(1)} %get-tuple-element.53), channel_id=1, source_target_pairs={{0,6},{1,7},{2,4},{3,5},{4,2},{5,3},{6,0},{7,1},{8,14},{9,15},{10,... | collective-permute-start | bytes 12296 | tf_op jit(solution)/shard_map/ppermute | solution.py:27
  26.0 1.5 %collective-permute-start.9 = (f32[8,128]{1,0:T(8,128)S(1)}, f32[8,128]{1,0:T(8,128)S(1)}, u32[]{:S(2)}, u32[]{:S(2)}) collective-permute-start(f32[8,128]{1,0:T(8,128)S(1)} %get-tuple-element.54), channel_id=1, source_target_pairs={{0,4},{1,5},{2,6},{3,7},{4,0},{5,1},{6,2},{7,3},{8,12},{9,13},{10,... | collective-permute-start | bytes 12296 | tf_op jit(solution)/shard_map/ppermute | solution.py:27
  27.6 0.1 collective-permute-done.7
  27.7 1.4 %collective-permute-done.8 = f32[8,128]{1,0:T(8,128)S(1)} collective-permute-done((f32[8,128]{1,0:T(8,128)S(1)}, f32[8,128]{1,0:T(8,128)S(1)}, u32[]{:S(2)}, u32[]{:S(2)}) %collective-permute-start.8) | collective-permute-done | bytes 4128 | tf_op jit(solution)/shard_map/ppermute | solution.py:27
  29.1 0.5 %collective-permute-done.9 = f32[8,128]{1,0:T(8,128)S(1)} collective-permute-done((f32[8,128]{1,0:T(8,128)S(1)}, f32[8,128]{1,0:T(8,128)S(1)}, u32[]{:S(2)}, u32[]{:S(2)}) %collective-permute-start.9) | collective-permute-done | bytes 4128 | tf_op jit(solution)/shard_map/ppermute | solution.py:27
  29.6 0.6 %add_add_fusion = f32[8,128]{1,0:T(8,128)} fusion(f32[8,128]{1,0:T(8,128)S(1)} %collective-permute-done.9, f32[8,128]{1,0:T(8,128)S(1)} %collective-permute-done.8, f32[8,128]{1,0:T(8,128)S(1)} %get-tuple-element.51, f32[8,128]{1,0:T(8,128)S(1)} %collective-permute-done.7), kind=kLoop, calls=%fused_computation | loop fusion | flops 3072 | bytes 20480 | tf_op jit(solution)/shard_map/add | solution.py:275
  (1 shorter events, 0.0 us)
Async XLA Ops:
  1.9 14.7 %collective-permute-start.2 = (bf16[2,128,512]{2,1,0:T(8,128)(2,1)S(1)}, bf16[2,128,512]{2,1,0:T(8,128)(2,1)S(1)}, u32[]{:S(2)}, u32[]{:S(2)}) collective-permute-start(bf16[2,128,512]{2,1,0:T(8,128)(2,1)S(1)} %get-tuple-element.31), channel_id=1, source_target_pairs={{0,6},{1,7},{2,4},{3,5},{4,2},{5,3},{6,0},{7,1},{8,14},{9,15},{10,... | collective-permute-start | bytes 786440 | tf_op jit(solution)/shard_map/ppermute | solution.py:27
  5.8 10.2 %collective-permute-start.1 = (bf16[320,256]{1,0:T(8,128)(2,1)S(1)}, bf16[320,256]{1,0:T(8,128)(2,1)S(1)}, u32[]{:S(2)}, u32[]{:S(2)}) collective-permute-start(bf16[320,256]{1,0:T(8,128)(2,1)S(1)} %get-tuple-element.32.refs_0_), channel_id=1, source_target_pairs={{0,16},{8,24},{16,0},{24,8},{1,17},{9,25},{17,1},{25,9},{2,18},{10... | collective-permute-start | bytes 491528 | tf_op jit(solution)/shard_map/ppermute | solution.py:27
  8.4 8.2 %collective-permute-start = (bf16[320,256]{1,0:T(8,128)(2,1)S(1)}, bf16[320,256]{1,0:T(8,128)(2,1)S(1)}, u32[]{:S(2)}, u32[]{:S(2)}) collective-permute-start(bf16[320,256]{1,0:T(8,128)(2,1)S(1)} %get-tuple-element.32.refs_0_), channel_id=1, source_target_pairs={{0,8},{8,0},{16,24},{24,16},{1,9},{9,1},{17,25},{25,17},{2,10},{10... | collective-permute-start | bytes 491528 | tf_op jit(solution)/shard_map/ppermute | solution.py:27
  12.1 7.3 %collective-permute-start.4 = (bf16[2,128,512]{2,1,0:T(8,128)(2,1)S(1)}, bf16[2,128,512]{2,1,0:T(8,128)(2,1)S(1)}, u32[]{:S(2)}, u32[]{:S(2)}) collective-permute-start(bf16[2,128,512]{2,1,0:T(8,128)(2,1)S(1)} %get-tuple-element.37), channel_id=1, source_target_pairs={{0,2},{1,3},{2,0},{3,1},{4,6},{5,7},{6,4},{7,5},{8,10},{9,11},{10,... | collective-permute-start | bytes 786440 | tf_op jit(solution)/shard_map/ppermute | solution.py:27
  12.6 6.9 %collective-permute-start.5 = (bf16[2,128,512]{2,1,0:T(8,128)(2,1)S(1)}, bf16[2,128,512]{2,1,0:T(8,128)(2,1)S(1)}, u32[]{:S(2)}, u32[]{:S(2)}) collective-permute-start(bf16[2,128,512]{2,1,0:T(8,128)(2,1)S(1)} %get-tuple-element.38), channel_id=1, source_target_pairs={{0,4},{1,5},{2,6},{3,7},{4,0},{5,1},{6,2},{7,3},{8,12},{9,13},{10,... | collective-permute-start | bytes 786440 | tf_op jit(solution)/shard_map/ppermute | solution.py:27
  16.0 5.3 %collective-permute-start.3 = (bf16[320,256]{1,0:T(8,128)(2,1)S(1)}, bf16[320,256]{1,0:T(8,128)(2,1)S(1)}, u32[]{:S(2)}, u32[]{:S(2)}) collective-permute-start(bf16[320,256]{1,0:T(8,128)(2,1)S(1)} %collective-permute-done.1.refs_2_), channel_id=1, source_target_pairs={{0,8},{8,0},{16,24},{24,16},{1,9},{9,1},{17,25},{25,17},{2,10},{10... | collective-permute-start | bytes 491528 | tf_op jit(solution)/shard_map/ppermute | solution.py:27
  21.3 1.4 %collective-permute-start.6 = (bf16[320,256]{1,0:T(8,128)(2,1)S(1)}, bf16[320,256]{1,0:T(8,128)(2,1)S(1)}, u32[]{:S(2)}, u32[]{:S(2)}) collective-permute-start(bf16[320,256]{1,0:T(8,128)(2,1)S(1)} %collective-permute-done.3.last_ref), channel_id=1, source_target_pairs={{0,1},{1,0},{2,3},{3,2},{4,5},{5,4},{6,7},{7,6},{8,9},{9,8},{10,11... | collective-permute-start | bytes 491528 | tf_op jit(solution)/shard_map/ppermute | solution.py:27
  24.0 3.7 %collective-permute-start.7 = (f32[8,128]{1,0:T(8,128)S(1)}, f32[8,128]{1,0:T(8,128)S(1)}, u32[]{:S(2)}, u32[]{:S(2)}) collective-permute-start(f32[8,128]{1,0:T(8,128)S(1)} %get-tuple-element.52), channel_id=1, source_target_pairs={{0,2},{1,3},{2,0},{3,1},{4,6},{5,7},{6,4},{7,5},{8,10},{9,11},{10,... | collective-permute-start | bytes 12296 | tf_op jit(solution)/shard_map/ppermute | solution.py:27
  24.6 4.5 %collective-permute-start.8 = (f32[8,128]{1,0:T(8,128)S(1)}, f32[8,128]{1,0:T(8,128)S(1)}, u32[]{:S(2)}, u32[]{:S(2)}) collective-permute-start(f32[8,128]{1,0:T(8,128)S(1)} %get-tuple-element.53), channel_id=1, source_target_pairs={{0,6},{1,7},{2,4},{3,5},{4,2},{5,3},{6,0},{7,1},{8,14},{9,15},{10,... | collective-permute-start | bytes 12296 | tf_op jit(solution)/shard_map/ppermute | solution.py:27
  26.0 3.6 %collective-permute-start.9 = (f32[8,128]{1,0:T(8,128)S(1)}, f32[8,128]{1,0:T(8,128)S(1)}, u32[]{:S(2)}, u32[]{:S(2)}) collective-permute-start(f32[8,128]{1,0:T(8,128)S(1)} %get-tuple-element.54), channel_id=1, source_target_pairs={{0,4},{1,5},{2,6},{3,7},{4,0},{5,1},{6,2},{7,3},{8,12},{9,13},{10,... | collective-permute-start | bytes 12296 | tf_op jit(solution)/shard_map/ppermute | solution.py:27

commit v6 on v5

--- a/solution.py
+++ b/solution.py
@@ -159,20 +159,19 @@
     )(*pieces)
 
 
-def pair_kernel(core, rows, chips, first_ref, last_ref, *refs):
+def pair_kernel(core, rows, chips, sources, first_ref, last_ref, *refs):
     chunks, before = refs[:chips], refs[chips : -chips - 2]
     outs, full, precond = refs[-chips - 2 : -2], refs[-2], refs[-1]
     me = lax.axis_index("seq")
     if core:
         first_ref = first_ref.at[1 - lax.rem(lax.axis_index("blk"), CORES)]
-    m = 0
+    whose = iter(sources)
     for pieces in (first_ref, last_ref):
         for first in range(0, pieces.shape[0], 5 * rows):
-            place = pl.ds(pl.multiple_of((me ^ m) * rows, rows), rows)
+            place = pl.ds(pl.multiple_of(next(whose)(me) * rows, rows), rows)
             for part in range(5):
                 start = first + part * rows
                 full[part, place, :] = pieces[start : start + rows, :]
-            m += 1
     basis_act, basis_grad = full[0], full[1]
     qrot_acts = jnp.dot(full[2], basis_act, preferred_element_type=jnp.float32).astype(jnp.bfloat16)
     qrot_grads = jnp.dot(full[3], basis_grad, preferred_element_type=jnp.float32).astype(jnp.bfloat16)
@@ -205,12 +204,12 @@
             outs[m + s][...] = part
 
 
-def pair_scores(core, first, last, chunks, before):
+def pair_scores(core, sources, first, last, chunks, before):
     chips, tokens = len(chunks), chunks[0].shape[1]
     rows = BLOCK // lax.axis_size("seq")
     operands = (first, last, *chunks, *before)
     return pl.pallas_call(
-        functools.partial(pair_kernel, core, rows, chips),
+        functools.partial(pair_kernel, core, rows, chips, sources),
         out_shape=(jax.ShapeDtypeStruct((QUERIES, tokens), jnp.float32),) * chips,
         in_specs=[VMEM] * len(operands),
         out_specs=(VMEM,) * chips,
@@ -253,9 +252,23 @@
         query_grads,
         eigenvalues,
     )
-    own = [packed]
-    for m in range(1, groups):
-        own.append(swap(own[m & (m - 1)], "seq", m & -m))
+    if groups == 4:
+        ahead_of = lax.ppermute(packed, "seq", [(0, 2), (2, 3), (3, 1), (1, 0)])
+        behind = lax.ppermute(packed, "seq", [(2, 0), (3, 2), (1, 3), (0, 1)])
+        me = lax.axis_index("seq")
+        relay = jnp.where((me == 1) | (me == 2), ahead_of, behind)
+        own = [packed, ahead_of, behind, swap(relay, "seq", 1)]
+        sources = [
+            lambda me: me,
+            lambda me: lax.rem(2 * me + 1, 5),
+            lambda me: lax.rem(3 * me + 2, 5),
+            lambda me: 3 - me,
+        ]
+    else:
+        own = [packed]
+        for m in range(1, groups):
+            own.append(swap(own[m & (m - 1)], "seq", m & -m))
+        sources = [lambda me, m=m: me ^ m for m in range(groups)]
     others = far[1:] + [0]
     chunks = dict(zip(far[:1], ahead)) | dict(
         zip(others, take_blocks(others, block_table.T, train_acts, train_grads))
@@ -268,8 +281,8 @@
     first, last, both, chunks = lax.optimization_barrier((first, own[-1], both, chunks))
     chunks = [chunks[0]] + [chunks[1 + far.index(m)] for m in range(1, chips)]
     there = swap(last, "blk", 1)
-    scores = pair_scores(0, first, last, chunks, ())
-    scores = pair_scores(1, both, there, chunks, (mask, *scores))
+    scores = pair_scores(0, sources, first, last, chunks, ())
+    scores = pair_scores(1, sources, both, there, chunks, (mask, *scores))
     total = scores[0]
     for m in [k ^ (k >> 1) for k in range(1, chips)]:
         total = total + swap(scores[m], "blk", CORES * m)

time: 30.5 us -> 30.5 us (level)
    ppermute x10 -> x8, starting transfers between devices: 13.2 us -> 8.91 us  [swap(): lax.ppermute(array, axis, [(i, i ^ bits) for i in range(lax.axis_size(axi...]
    ppermute x0 -> x2, starting transfers between devices: none -> 4.15 us  [the longest x1 3.08 us: on_device(): behind = lax.ppermute(packed, 'seq', [(2, 0), (3, 2), (1, 3), (0, 1)])]
    ppermute x0 -> x2, waiting for transfers between devices: none -> 2.1 us  [the longest x1 2.1 us: on_device(): ahead_of = lax.ppermute(packed, 'seq', [(0, 2), (2, 3), (3, 1), (1, 0)])]
    ppermute x10 -> x8, waiting for transfers between devices: 7.32 us -> 5.47 us  [swap(): lax.ppermute(array, axis, [(i, i ^ bits) for i in range(lax.axis_size(axi...]
  transfers between devices with their start and end apart: 10 -> 10, of which waited for: 8 -> 7; matrix products, arithmetic and copies ran while one was open for 0% -> 0% of each run, Pallas kernels for 11% -> 11%
where the time goes in v6:
time: 30.5 us; the launch traced here: 30.2 us
  starting transfers between devices  13.1 us (43%)
  waiting for transfers between devices  7.57 us (25%)
  Pallas kernels  6.41 us (21%)
  blocking collectives  2.51 us (8%)
  other arithmetic  0.62 us (2%)
    ppermute x8, starting transfers between devices, swap(): lax.ppermute(array, axis, [(i, i ^ bits) for i in range(lax.axis_size(axi...  8.91 us
    ppermute x8, waiting for transfers between devices, swap(): lax.ppermute(array, axis, [(i, i ^ bits) for i in range(lax.axis_size(axi...  5.47 us
    ppermute x1, starting transfers between devices, on_device(): behind = lax.ppermute(packed, 'seq', [(2, 0), (3, 2), (1, 3), (0, 1)])  3.08 us
    pallas_call x2, Pallas kernels, pair_scores(): pl.pallas_call(functools.partial(pair_kernel, core, rows, chips, sources)...  2.54 us
    all_gather x1, blocking collectives, on_device(): both = lax.all_gather(first, 'blk', axis=0, axis_index_groups=pairs)  2.51 us
    ppermute x1, waiting for transfers between devices, on_device(): ahead_of = lax.ppermute(packed, 'seq', [(0, 2), (2, 3), (3, 1), (1, 0)])  2.1 us
    pallas_call x1, Pallas kernels, take_blocks(): pl.pallas_call(functools.partial(blocks_kernel, distances), out_shape=(pl...  1.98 us
    pallas_call x1, Pallas kernels, pack(): pl.pallas_call(functools.partial(pack_kernel, distances), out_shape=(pack...  1.85 us
  transfers between devices with their start and end apart: 10, of which 7 were waited for; matrix products, arithmetic and copies ran while one was open for 0% of the time, Pallas kernels for 11%

profile of v6, /device:TPU:0, one launch (start us, length us, event | category | flops | bytes accessed | tf_op | source)
XLA Modules:
  0.0 30.2 jit_solution(10259582524028103585)
XLA Ops:
  0.0 1.9 %pack.1 = (bf16[320,256]{1,0:T(8,128)(2,1)S(1)}, f32[4,8,128]{2,1,0:T(8,128)S(1)}, bf16[2,128,512]{2,1,0:T(8,128)(2,1)S(1)}) custom-call(s32[2,8]{1,0:T(2,128)} %bitcast.3, s32[4]{0:T(128)} %lengths_ref.1, bf16[128,4096]{1,0:T(8,128)(2,1)} %acts_ref.3, bf16[128,14336]{1,0:T(8,128)(2,1)} %grads_ref.3, bf16[1,64,256]{2,1,0:T(8,128)(2,1)} %refs_0_.1, ...), custom_call_target="tpu_custom_call" | custom-call | bytes 2097152 | tf_op jit(solution)/shard_map/pack/pallas_call | solution.py:124
  1.9 3.1 %collective-permute-start.1 = (bf16[320,256]{1,0:T(8,128)(2,1)S(1)}, bf16[320,256]{1,0:T(8,128)(2,1)S(1)}, u32[]{:S(2)}, u32[]{:S(2)}) collective-permute-start(bf16[320,256]{1,0:T(8,128)(2,1)S(1)} %get-tuple-element.32.refs_0_), channel_id=1, source_target_pairs={{16,0},{24,16},{8,24},{0,8},{17,1},{25,17},{9,25},{1,9},{18,2},{26... | collective-permute-start | bytes 491528 | tf_op jit(solution)/shard_map/ppermute | solution.py:257
  4.9 1.1 %collective-permute-start = (bf16[320,256]{1,0:T(8,128)(2,1)S(1)}, bf16[320,256]{1,0:T(8,128)(2,1)S(1)}, u32[]{:S(2)}, u32[]{:S(2)}) collective-permute-start(bf16[320,256]{1,0:T(8,128)(2,1)S(1)} %get-tuple-element.32.refs_0_), channel_id=1, source_target_pairs={{0,16},{16,24},{24,8},{8,0},{1,17},{17,25},{25,9},{9,1},{2,18},{18... | collective-permute-start | bytes 491528 | tf_op jit(solution)/shard_map/ppermute | solution.py:256
  6.0 2.7 %collective-permute-start.2 = (bf16[2,128,512]{2,1,0:T(8,128)(2,1)S(1)}, bf16[2,128,512]{2,1,0:T(8,128)(2,1)S(1)}, u32[]{:S(2)}, u32[]{:S(2)}) collective-permute-start(bf16[2,128,512]{2,1,0:T(8,128)(2,1)S(1)} %get-tuple-element.31), channel_id=1, source_target_pairs={{0,6},{1,7},{2,4},{3,5},{4,2},{5,3},{6,0},{7,1},{8,14},{9,15},{10,... | collective-permute-start | bytes 786440 | tf_op jit(solution)/shard_map/ppermute | solution.py:27
  8.7 2.0 %take_blocks.1 = (bf16[2,128,512]{2,1,0:T(8,128)(2,1)S(1)}, bf16[2,128,512]{2,1,0:T(8,128)(2,1)S(1)}, bf16[2,128,512]{2,1,0:T(8,128)(2,1)S(1)}) custom-call(s32[2,8]{1,0:T(2,128)} %bitcast.4, bf16[128,4096]{1,0:T(8,128)(2,1)} %acts_ref.3, bf16[128,14336]{1,0:T(8,128)(2,1)} %grads_ref.3), custom_call_target="tpu_custom_call" | custom-call | tf_op jit(solution)/shard_map/take_blocks/pallas_call | solution.py:71
  10.7 0.6 %collective-permute-start.4 = (bf16[2,128,512]{2,1,0:T(8,128)(2,1)S(1)}, bf16[2,128,512]{2,1,0:T(8,128)(2,1)S(1)}, u32[]{:S(2)}, u32[]{:S(2)}) collective-permute-start(bf16[2,128,512]{2,1,0:T(8,128)(2,1)S(1)} %get-tuple-element.37), channel_id=1, source_target_pairs={{0,2},{1,3},{2,0},{3,1},{4,6},{5,7},{6,4},{7,5},{8,10},{9,11},{10,... | collective-permute-start | bytes 786440 | tf_op jit(solution)/shard_map/ppermute | solution.py:27
  11.3 0.2 collective-permute-start.5
  11.6 0.0 collective-permute-done.1.refs_2_
  11.6 2.1 %collective-permute-done.refs_1_ = bf16[320,256]{1,0:T(8,128)(2,1)S(1)} collective-permute-done((bf16[320,256]{1,0:T(8,128)(2,1)S(1)}, bf16[320,256]{1,0:T(8,128)(2,1)S(1)}, u32[]{:S(2)}, u32[]{:S(2)}) %collective-permute-start) | collective-permute-done | bytes 163872 | tf_op jit(solution)/shard_map/ppermute | solution.py:256
  13.7 1.8 %collective-permute-start.3 = (bf16[320,256]{1,0:T(8,128)(2,1)S(1)}, bf16[320,256]{1,0:T(8,128)(2,1)S(1)}, u32[]{:S(2)}, u32[]{:S(2)}) collective-permute-start(bf16[320,256]{1,0:T(8,128)(2,1)S(1)} %broadcast_select_fusion), channel_id=1, source_target_pairs={{0,8},{8,0},{16,24},{24,16},{1,9},{9,1},{17,25},{25,17},{2,10},{10... | collective-permute-start | bytes 491528 | tf_op jit(solution)/shard_map/ppermute | solution.py:27
  15.5 0.7 %collective-permute-done.2.refs_3_ = bf16[2,128,512]{2,1,0:T(8,128)(2,1)S(1)} collective-permute-done((bf16[2,128,512]{2,1,0:T(8,128)(2,1)S(1)}, bf16[2,128,512]{2,1,0:T(8,128)(2,1)S(1)}, u32[]{:S(2)}, u32[]{:S(2)}) %collective-permute-start.2) | collective-permute-done | bytes 262176 | tf_op jit(solution)/shard_map/ppermute | solution.py:27
  16.2 2.5 %all-gather = bf16[1920,256]{1,0:T(8,128)(2,1)S(1)} all-gather(bf16[960,256]{1,0:T(8,128)(2,1)S(1)} %join.1.first_ref), channel_id=2, replica_groups={{0,1},{2,3},{4,5},{6,7},{8,9},{10,11},{12,13},{14,15},{16,17},{18,19},{..., dimensions={0}, use_global_device_ids=true | all-gather | bytes 1474560 | tf_op jit(solution)/shard_map/all_gather | solution.py:280
  18.7 1.7 %collective-permute-done.4.refs_1_ = bf16[2,128,512]{2,1,0:T(8,128)(2,1)S(1)} collective-permute-done((bf16[2,128,512]{2,1,0:T(8,128)(2,1)S(1)}, bf16[2,128,512]{2,1,0:T(8,128)(2,1)S(1)}, u32[]{:S(2)}, u32[]{:S(2)}) %collective-permute-start.4) | collective-permute-done | bytes 262176 | tf_op jit(solution)/shard_map/ppermute | solution.py:27
  20.4 0.0 collective-permute-done.5.refs_2_
  20.4 0.0 collective-permute-done.3.last_ref
  20.4 0.0 collective-permute-start.6
  20.4 1.3 %pair_scores.2 = (f32[8,128]{1,0:T(8,128)S(1)}, f32[8,128]{1,0:T(8,128)S(1)}, f32[8,128]{1,0:T(8,128)S(1)}, f32[8,128]{1,0:T(8,128)S(1)}) custom-call(bf16[960,256]{1,0:T(8,128)(2,1)S(1)} %join.1.first_ref, bf16[320,256]{1,0:T(8,128)(2,1)S(1)} %collective-permute-done.3.last_ref, bf16[2,128,512]{2,1,0:T(8,128)(2,1)S(1)} %get-tuple-element.41.refs_0_, ...), custom_call_target="tpu_custom_call" | custom-call | flops 671088640 | bytes 1835008 | tf_op jit(solution)/shard_map/pair_scores/pallas_call | solution.py:211
  21.7 0.1 collective-permute-done.6.last_ref
  21.8 1.3 %pair_scores.3 = (f32[8,128]{1,0:T(8,128)S(1)}, f32[8,128]{1,0:T(8,128)S(1)}, f32[8,128]{1,0:T(8,128)S(1)}, f32[8,128]{1,0:T(8,128)S(1)}) custom-call(bf16[2,960,256]{2,1,0:T(8,128)(2,1)S(1)} %bitcast.2, bf16[320,256]{1,0:T(8,128)(2,1)S(1)} %collective-permute-done.6.last_ref, bf16[2,128,512]{2,1,0:T(8,128)(2,1)S(1)} %get-tuple-element.41.refs_0_, ...), custom_call_target="tpu_custom_call" | custom-call | flops 671088640 | bytes 1835008 | tf_op jit(solution)/shard_map/pair_scores/pallas_call | solution.py:211
  23.0 1.6 %collective-permute-start.7 = (f32[8,128]{1,0:T(8,128)S(1)}, f32[8,128]{1,0:T(8,128)S(1)}, u32[]{:S(2)}, u32[]{:S(2)}) collective-permute-start(f32[8,128]{1,0:T(8,128)S(1)} %get-tuple-element.52), channel_id=1, source_target_pairs={{0,2},{1,3},{2,0},{3,1},{4,6},{5,7},{6,4},{7,5},{8,10},{9,11},{10,... | collective-permute-start | bytes 12296 | tf_op jit(solution)/shard_map/ppermute | solution.py:27
  24.6 1.4 %collective-permute-start.8 = (f32[8,128]{1,0:T(8,128)S(1)}, f32[8,128]{1,0:T(8,128)S(1)}, u32[]{:S(2)}, u32[]{:S(2)}) collective-permute-start(f32[8,128]{1,0:T(8,128)S(1)} %get-tuple-element.53), channel_id=1, source_target_pairs={{0,6},{1,7},{2,4},{3,5},{4,2},{5,3},{6,0},{7,1},{8,14},{9,15},{10,... | collective-permute-start | bytes 12296 | tf_op jit(solution)/shard_map/ppermute | solution.py:27
  26.0 0.6 %collective-permute-start.9 = (f32[8,128]{1,0:T(8,128)S(1)}, f32[8,128]{1,0:T(8,128)S(1)}, u32[]{:S(2)}, u32[]{:S(2)}) collective-permute-start(f32[8,128]{1,0:T(8,128)S(1)} %get-tuple-element.54), channel_id=1, source_target_pairs={{0,4},{1,5},{2,6},{3,7},{4,0},{5,1},{6,2},{7,3},{8,12},{9,13},{10,... | collective-permute-start | bytes 12296 | tf_op jit(solution)/shard_map/ppermute | solution.py:27
  26.6 0.1 collective-permute-done.7
  26.7 2.4 %collective-permute-done.8 = f32[8,128]{1,0:T(8,128)S(1)} collective-permute-done((f32[8,128]{1,0:T(8,128)S(1)}, f32[8,128]{1,0:T(8,128)S(1)}, u32[]{:S(2)}, u32[]{:S(2)}) %collective-permute-start.8) | collective-permute-done | bytes 4128 | tf_op jit(solution)/shard_map/ppermute | solution.py:27
  29.1 0.5 %collective-permute-done.9 = f32[8,128]{1,0:T(8,128)S(1)} collective-permute-done((f32[8,128]{1,0:T(8,128)S(1)}, f32[8,128]{1,0:T(8,128)S(1)}, u32[]{:S(2)}, u32[]{:S(2)}) %collective-permute-start.9) | collective-permute-done | bytes 4128 | tf_op jit(solution)/shard_map/ppermute | solution.py:27
  29.6 0.6 %add_add_fusion = f32[8,128]{1,0:T(8,128)} fusion(f32[8,128]{1,0:T(8,128)S(1)} %collective-permute-done.9, f32[8,128]{1,0:T(8,128)S(1)} %collective-permute-done.8, f32[8,128]{1,0:T(8,128)S(1)} %get-tuple-element.51, f32[8,128]{1,0:T(8,128)S(1)} %collective-permute-done.7), kind=kLoop, calls=%fused_computation.1 | loop fusion | flops 3072 | bytes 20480 | tf_op jit(solution)/shard_map/add | solution.py:288
  (2 shorter events, 0.1 us)
Async XLA Ops:
  1.9 9.7 %collective-permute-start.1 = (bf16[320,256]{1,0:T(8,128)(2,1)S(1)}, bf16[320,256]{1,0:T(8,128)(2,1)S(1)}, u32[]{:S(2)}, u32[]{:S(2)}) collective-permute-start(bf16[320,256]{1,0:T(8,128)(2,1)S(1)} %get-tuple-element.32.refs_0_), channel_id=1, source_target_pairs={{16,0},{24,16},{8,24},{0,8},{17,1},{25,17},{9,25},{1,9},{18,2},{26... | collective-permute-start | bytes 491528 | tf_op jit(solution)/shard_map/ppermute | solution.py:257
  4.9 8.7 %collective-permute-start = (bf16[320,256]{1,0:T(8,128)(2,1)S(1)}, bf16[320,256]{1,0:T(8,128)(2,1)S(1)}, u32[]{:S(2)}, u32[]{:S(2)}) collective-permute-start(bf16[320,256]{1,0:T(8,128)(2,1)S(1)} %get-tuple-element.32.refs_0_), channel_id=1, source_target_pairs={{0,16},{16,24},{24,8},{8,0},{1,17},{17,25},{25,9},{9,1},{2,18},{18... | collective-permute-start | bytes 491528 | tf_op jit(solution)/shard_map/ppermute | solution.py:256
  6.0 10.1 %collective-permute-start.2 = (bf16[2,128,512]{2,1,0:T(8,128)(2,1)S(1)}, bf16[2,128,512]{2,1,0:T(8,128)(2,1)S(1)}, u32[]{:S(2)}, u32[]{:S(2)}) collective-permute-start(bf16[2,128,512]{2,1,0:T(8,128)(2,1)S(1)} %get-tuple-element.31), channel_id=1, source_target_pairs={{0,6},{1,7},{2,4},{3,5},{4,2},{5,3},{6,0},{7,1},{8,14},{9,15},{10,... | collective-permute-start | bytes 786440 | tf_op jit(solution)/shard_map/ppermute | solution.py:27
  10.7 9.6 %collective-permute-start.4 = (bf16[2,128,512]{2,1,0:T(8,128)(2,1)S(1)}, bf16[2,128,512]{2,1,0:T(8,128)(2,1)S(1)}, u32[]{:S(2)}, u32[]{:S(2)}) collective-permute-start(bf16[2,128,512]{2,1,0:T(8,128)(2,1)S(1)} %get-tuple-element.37), channel_id=1, source_target_pairs={{0,2},{1,3},{2,0},{3,1},{4,6},{5,7},{6,4},{7,5},{8,10},{9,11},{10,... | collective-permute-start | bytes 786440 | tf_op jit(solution)/shard_map/ppermute | solution.py:27
  11.3 9.0 %collective-permute-start.5 = (bf16[2,128,512]{2,1,0:T(8,128)(2,1)S(1)}, bf16[2,128,512]{2,1,0:T(8,128)(2,1)S(1)}, u32[]{:S(2)}, u32[]{:S(2)}) collective-permute-start(bf16[2,128,512]{2,1,0:T(8,128)(2,1)S(1)} %get-tuple-element.38), channel_id=1, source_target_pairs={{0,4},{1,5},{2,6},{3,7},{4,0},{5,1},{6,2},{7,3},{8,12},{9,13},{10,... | collective-permute-start | bytes 786440 | tf_op jit(solution)/shard_map/ppermute | solution.py:27
  13.7 6.7 %collective-permute-start.3 = (bf16[320,256]{1,0:T(8,128)(2,1)S(1)}, bf16[320,256]{1,0:T(8,128)(2,1)S(1)}, u32[]{:S(2)}, u32[]{:S(2)}) collective-permute-start(bf16[320,256]{1,0:T(8,128)(2,1)S(1)} %broadcast_select_fusion), channel_id=1, source_target_pairs={{0,8},{8,0},{16,24},{24,16},{1,9},{9,1},{17,25},{25,17},{2,10},{10... | collective-permute-start | bytes 491528 | tf_op jit(solution)/shard_map/ppermute | solution.py:27
  20.4 1.4 %collective-permute-start.6 = (bf16[320,256]{1,0:T(8,128)(2,1)S(1)}, bf16[320,256]{1,0:T(8,128)(2,1)S(1)}, u32[]{:S(2)}, u32[]{:S(2)}) collective-permute-start(bf16[320,256]{1,0:T(8,128)(2,1)S(1)} %collective-permute-done.3.last_ref), channel_id=1, source_target_pairs={{0,1},{1,0},{2,3},{3,2},{4,5},{5,4},{6,7},{7,6},{8,9},{9,8},{10,11... | collective-permute-start | bytes 491528 | tf_op jit(solution)/shard_map/ppermute | solution.py:27
  23.0 3.7 %collective-permute-start.7 = (f32[8,128]{1,0:T(8,128)S(1)}, f32[8,128]{1,0:T(8,128)S(1)}, u32[]{:S(2)}, u32[]{:S(2)}) collective-permute-start(f32[8,128]{1,0:T(8,128)S(1)} %get-tuple-element.52), channel_id=1, source_target_pairs={{0,2},{1,3},{2,0},{3,1},{4,6},{5,7},{6,4},{7,5},{8,10},{9,11},{10,... | collective-permute-start | bytes 12296 | tf_op jit(solution)/shard_map/ppermute | solution.py:27
  24.6 4.5 %collective-permute-start.8 = (f32[8,128]{1,0:T(8,128)S(1)}, f32[8,128]{1,0:T(8,128)S(1)}, u32[]{:S(2)}, u32[]{:S(2)}) collective-permute-start(f32[8,128]{1,0:T(8,128)S(1)} %get-tuple-element.53), channel_id=1, source_target_pairs={{0,6},{1,7},{2,4},{3,5},{4,2},{5,3},{6,0},{7,1},{8,14},{9,15},{10,... | collective-permute-start | bytes 12296 | tf_op jit(solution)/shard_map/ppermute | solution.py:27
  26.0 3.6 %collective-permute-start.9 = (f32[8,128]{1,0:T(8,128)S(1)}, f32[8,128]{1,0:T(8,128)S(1)}, u32[]{:S(2)}, u32[]{:S(2)}) collective-permute-start(f32[8,128]{1,0:T(8,128)S(1)} %get-tuple-element.54), channel_id=1, source_target_pairs={{0,4},{1,5},{2,6},{3,7},{4,0},{5,1},{6,2},{7,3},{8,12},{9,13},{10,... | collective-permute-start | bytes 12296 | tf_op jit(solution)/shard_map/ppermute | solution.py:27

commit v7 on v5

--- a/solution.py
+++ b/solution.py
@@ -56,55 +56,63 @@
     return copies
 
 
-def blocks_kernel(distances, table_ref, acts_ref, grads_ref, *refs):
-    chunks, (table, sem, table_sem) = refs[:-3], refs[-3:]
-    copy = pltpu.make_async_copy(table_ref, table, table_sem)
-    copy.start()
-    copy.wait()
-    for copy in copy_blocks(table, distances, acts_ref, grads_ref, chunks, sem):
+def blocks_kernel(distances, table_ref, lengths_ref, acts_ref, grads_ref, mask_ref, *refs):
+    chunks, (table, lengths, sem) = refs[:-3], refs[-3:]
+    count = 2 * CORES * len(distances)
+    scalars = [
+        pltpu.make_async_copy(table_ref, table, sem.at[count]),
+        pltpu.make_async_copy(lengths_ref, lengths, sem.at[count + 1]),
+    ]
+    for copy in scalars:
+        copy.start()
+    scalars[0].wait()
+    copies = copy_blocks(table, distances, acts_ref, grads_ref, chunks, sem)
+    scalars[1].wait()
+    me = lax.axis_index("blk")
+    group = lax.axis_index("seq") * lax.axis_size("blk")
+    chips, _, tokens = mask_ref.shape
+    for m in range(chips):
+        start = (group + (me ^ (CORES * m))) * tokens
+        mask_ref[m] = valid_mask(lengths, lengths_ref.shape[0], start, mask_ref.shape[1:])
+    for copy in copies:
         copy.wait()
 
 
-def take_blocks(distances, table, acts, grads):
-    tokens = acts.shape[0]
-    operands = [pltpu.with_memory_space_constraint(a, pltpu.HBM) for a in (table, acts, grads)]
+def take_blocks(distances, table, lengths, acts, grads):
+    tokens, chips = acts.shape[0], table.shape[1] // CORES
+    operands = [
+        pltpu.with_memory_space_constraint(a, pltpu.HBM) for a in (table, lengths, acts, grads)
+    ]
     return pl.pallas_call(
         functools.partial(blocks_kernel, distances),
-        out_shape=(pltpu.VMEM((CORES, tokens, 2 * BLOCK), jnp.bfloat16),) * len(distances),
-        in_specs=[HBM] * 3,
-        out_specs=(VMEM,) * len(distances),
+        out_shape=(pltpu.VMEM((chips, QUERIES, tokens), jnp.float32),)
+        + (pltpu.VMEM((CORES, tokens, 2 * BLOCK), jnp.bfloat16),) * len(distances),
+        in_specs=[HBM] * 4,
+        out_specs=(VMEM,) * (1 + len(distances)),
         scratch_shapes=[
             pltpu.SMEM(table.shape, jnp.int32),
-            pltpu.SemaphoreType.DMA((2 * CORES * len(distances),)),
-            pltpu.SemaphoreType.DMA,
+            pltpu.SMEM(lengths.shape, jnp.int32),
+            pltpu.SemaphoreType.DMA((2 * CORES * len(distances) + 2,)),
         ],
         compiler_params=pltpu.CompilerParams(vmem_limit_bytes=VMEM_BYTES),
         name="take_blocks",
     )(*operands)
 
 
-def pack_kernel(distances, table_ref, lengths_ref, acts_ref, grads_ref, *refs):
-    shards, packed_ref, mask_ref = refs[:5], refs[5], refs[6]
-    chunks, (raw_eigen, table, lengths, sem) = refs[7:-4], refs[-4:]
-    me = lax.axis_index("blk")
-    rows, tokens = raw_eigen.shape[0], acts_ref.shape[0]
-    scalars = [
-        pltpu.make_async_copy(table_ref, table, sem.at[0]),
-        pltpu.make_async_copy(lengths_ref, lengths, sem.at[1]),
-    ]
+def pack_kernel(distances, table_ref, acts_ref, grads_ref, *refs):
+    shards, packed_ref = refs[:5], refs[5]
+    chunks, (raw_eigen, table, sem) = refs[6:-3], refs[-3:]
+    rows = raw_eigen.shape[0]
+    fetch = pltpu.make_async_copy(table_ref, table, sem.at[0])
+    fetch.start()
     weights = []
     for part, shard in enumerate(shards):
         target = raw_eigen if part == 4 else packed_ref.at[pl.ds(part * rows, rows), :]
-        weights.append(pltpu.make_async_copy(shard.at[0], target, sem.at[2 + part]))
-    for copy in scalars + weights:
+        weights.append(pltpu.make_async_copy(shard.at[0], target, sem.at[1 + part]))
+    for copy in weights:
         copy.start()
-    scalars[0].wait()
-    copies = copy_blocks(table, distances, acts_ref, grads_ref, chunks, sem.at[pl.ds(7, 2 * CORES)])
-    scalars[1].wait()
-    group = lax.axis_index("seq") * lax.axis_size("blk")
-    for m in range(mask_ref.shape[0]):
-        start = (group + (me ^ (CORES * m))) * tokens
-        mask_ref[m] = valid_mask(lengths, lengths_ref.shape[0], start, mask_ref.shape[1:])
+    fetch.wait()
+    copies = copy_blocks(table, distances, acts_ref, grads_ref, chunks, sem.at[pl.ds(6, 2 * CORES)])
     for copy in weights:
         copy.wait()
     packed_ref[4 * rows :, :] = raw_eigen[...].astype(jnp.bfloat16)
@@ -112,30 +120,22 @@
         copy.wait()
 
 
-def pack(distances, table, lengths, acts, grads, *shards):
-    pairs, tokens, rows = table.shape[1], acts.shape[0], shards[0].shape[1]
-    chips = pairs // CORES
+def pack(distances, table, acts, grads, *shards):
+    tokens, rows = acts.shape[0], shards[0].shape[1]
     chunk = pltpu.VMEM((CORES, tokens, 2 * BLOCK), jnp.bfloat16)
     packed = pltpu.VMEM((5 * rows, BLOCK), jnp.bfloat16)
-    mask = pltpu.VMEM((chips, QUERIES, tokens), jnp.float32)
-    operands = [
-        pltpu.with_memory_space_constraint(a, pltpu.HBM) for a in (table, lengths, acts, grads, *shards)
-    ]
+    operands = [pltpu.with_memory_space_constraint(a, pltpu.HBM) for a in (table, acts, grads, *shards)]
     return pl.pallas_call(
         functools.partial(pack_kernel, distances),
-        out_shape=(packed, mask) + (chunk,) * len(distances),
+        out_shape=(packed,) + (chunk,) * len(distances),
         in_specs=[HBM] * len(operands),
-        out_specs=(VMEM,) * (2 + len(distances)),
+        out_specs=(VMEM,) * (1 + len(distances)),
         scratch_shapes=[
             pltpu.VMEM((rows, BLOCK), jnp.float32),
             pltpu.SMEM(table.shape, jnp.int32),
-            pltpu.SMEM(lengths.shape, jnp.int32),
-            pltpu.SemaphoreType.DMA((7 + 2 * pairs,)),
+            pltpu.SemaphoreType.DMA((6 + 2 * CORES * len(distances),)),
         ],
         compiler_params=pltpu.CompilerParams(vmem_limit_bytes=PACK_VMEM),
-        cost_estimate=pl.CostEstimate(
-            flops=0, bytes_accessed=pairs * tokens * BLOCK * 8, transcendentals=0
-        ),
         name="pack",
     )(*operands)
 
@@ -241,10 +241,9 @@
 ):
     groups, chips = lax.axis_size("seq"), lax.axis_size("blk") // CORES
     far = sorted(range(1, chips), key=lambda m: -m.bit_count())
-    packed, mask, *ahead = pack(
+    packed, *ahead = pack(
         far[:1],
         block_table.T,
-        seq_lengths,
         train_acts,
         train_grads,
         basis_acts,
@@ -255,11 +254,13 @@
     )
     own = [packed]
     for m in range(1, groups):
-        own.append(swap(own[m & (m - 1)], "seq", m & -m))
+        piece = own[m & (m - 1)]
+        if m & (m - 1):
+            piece = jnp.where(lax.axis_index("seq") >= 0, piece, packed)
+        own.append(swap(piece, "seq", m & -m))
     others = far[1:] + [0]
-    chunks = dict(zip(far[:1], ahead)) | dict(
-        zip(others, take_blocks(others, block_table.T, train_acts, train_grads))
-    )
+    mask, *later = take_blocks(others, block_table.T, seq_lengths, train_acts, train_grads)
+    chunks = dict(zip(far[:1] + others, ahead + later))
     chunks = [chunks[0]] + [swap(chunks[m], "blk", CORES * m) for m in far]
     early, chunks[1] = lax.optimization_barrier((own[:-1], chunks[1]))
     first = join(early)

time: 30.5 us -> 30.4 us (level)
  no operation moved by 1% of the time
where the time goes in v7:
time: 30.4 us; the launch traced here: 30.1 us
  starting transfers between devices  13.5 us (44%)
  waiting for transfers between devices  7.08 us (23%)
  Pallas kernels  6.3 us (21%)
  blocking collectives  2.51 us (8%)
  other arithmetic  0.62 us (2%)
    ppermute x10, starting transfers between devices, swap(): lax.ppermute(array, axis, [(i, i ^ bits) for i in range(lax.axis_size(axi...  13.5 us
    ppermute x10, waiting for transfers between devices, swap(): lax.ppermute(array, axis, [(i, i ^ bits) for i in range(lax.axis_size(axi...  7.08 us
    pallas_call x2, Pallas kernels, pair_scores(): pl.pallas_call(functools.partial(pair_kernel, core, rows, chips), out_sha...  2.53 us
    all_gather x1, blocking collectives, on_device(): both = lax.all_gather(first, 'blk', axis=0, axis_index_groups=pairs)  2.51 us
    pallas_call x1, Pallas kernels, take_blocks(): pl.pallas_call(functools.partial(blocks_kernel, distances), out_shape=(pl...  1.99 us
    pallas_call x1, Pallas kernels, pack(): pl.pallas_call(functools.partial(pack_kernel, distances), out_shape=(pack...  1.75 us
  transfers between devices with their start and end apart: 10, of which 8 were waited for; matrix products, arithmetic and copies ran while one was open for 0% of the time, Pallas kernels for 11%

profile of v7, /device:TPU:0, one launch (start us, length us, event | category | flops | bytes accessed | tf_op | source)
XLA Modules:
  0.0 30.1 jit_solution(9808417275401450570)
XLA Ops:
  0.0 1.7 %pack.1 = (bf16[320,256]{1,0:T(8,128)(2,1)S(1)}, bf16[2,128,512]{2,1,0:T(8,128)(2,1)S(1)}) custom-call(s32[2,8]{1,0:T(2,128)} %bitcast.3, bf16[128,4096]{1,0:T(8,128)(2,1)} %acts_ref.3, bf16[128,14336]{1,0:T(8,128)(2,1)} %grads_ref.3, bf16[1,64,256]{2,1,0:T(8,128)(2,1)} %refs_0_.1, bf16[1,64,256]{2,1,0:T(8,128)(2,1)} %refs_1_.1, ...), custom_call_target="tpu_custom_call" | custom-call | tf_op jit(solution)/shard_map/pack/pallas_call | solution.py:128
  1.8 4.1 %collective-permute-start.1 = (bf16[320,256]{1,0:T(8,128)(2,1)S(1)}, bf16[320,256]{1,0:T(8,128)(2,1)S(1)}, u32[]{:S(2)}, u32[]{:S(2)}) collective-permute-start(bf16[320,256]{1,0:T(8,128)(2,1)S(1)} %get-tuple-element.32.refs_0_), channel_id=1, source_target_pairs={{0,16},{8,24},{16,0},{24,8},{1,17},{9,25},{17,1},{25,9},{2,18},{10... | collective-permute-start | bytes 491528 | tf_op jit(solution)/shard_map/ppermute | solution.py:27
  5.9 2.4 %collective-permute-start.2 = (bf16[2,128,512]{2,1,0:T(8,128)(2,1)S(1)}, bf16[2,128,512]{2,1,0:T(8,128)(2,1)S(1)}, u32[]{:S(2)}, u32[]{:S(2)}) collective-permute-start(bf16[2,128,512]{2,1,0:T(8,128)(2,1)S(1)} %get-tuple-element.31), channel_id=1, source_target_pairs={{0,6},{1,7},{2,4},{3,5},{4,2},{5,3},{6,0},{7,1},{8,14},{9,15},{10,... | collective-permute-start | bytes 786440 | tf_op jit(solution)/shard_map/ppermute | solution.py:27
  8.3 1.6 %collective-permute-start = (bf16[320,256]{1,0:T(8,128)(2,1)S(1)}, bf16[320,256]{1,0:T(8,128)(2,1)S(1)}, u32[]{:S(2)}, u32[]{:S(2)}) collective-permute-start(bf16[320,256]{1,0:T(8,128)(2,1)S(1)} %get-tuple-element.32.refs_0_), channel_id=1, source_target_pairs={{0,8},{8,0},{16,24},{24,16},{1,9},{9,1},{17,25},{25,17},{2,10},{10... | collective-permute-start | bytes 491528 | tf_op jit(solution)/shard_map/ppermute | solution.py:27
  9.9 2.0 %take_blocks.1 = (f32[4,8,128]{2,1,0:T(8,128)S(1)}, bf16[2,128,512]{2,1,0:T(8,128)(2,1)S(1)}, bf16[2,128,512]{2,1,0:T(8,128)(2,1)S(1)}, bf16[2,128,512]{2,1,0:T(8,128)(2,1)S(1)}) custom-call(s32[2,8]{1,0:T(2,128)} %bitcast.4, s32[4]{0:T(128)} %lengths_ref.1, bf16[128,4096]{1,0:T(8,128)(2,1)} %acts_ref.3, bf16[128,14336]{1,0:T(8,128)(2,1)} %grads_ref.3), custom_call_target="tpu_custom_call" | custom-call | tf_op jit(solution)/shard_map/take_blocks/pallas_call | solution.py:86
  11.9 0.6 %collective-permute-start.4 = (bf16[2,128,512]{2,1,0:T(8,128)(2,1)S(1)}, bf16[2,128,512]{2,1,0:T(8,128)(2,1)S(1)}, u32[]{:S(2)}, u32[]{:S(2)}) collective-permute-start(bf16[2,128,512]{2,1,0:T(8,128)(2,1)S(1)} %get-tuple-element.37), channel_id=1, source_target_pairs={{0,2},{1,3},{2,0},{3,1},{4,6},{5,7},{6,4},{7,5},{8,10},{9,11},{10,... | collective-permute-start | bytes 786440 | tf_op jit(solution)/shard_map/ppermute | solution.py:27
  12.5 0.5 %collective-permute-start.5 = (bf16[2,128,512]{2,1,0:T(8,128)(2,1)S(1)}, bf16[2,128,512]{2,1,0:T(8,128)(2,1)S(1)}, u32[]{:S(2)}, u32[]{:S(2)}) collective-permute-start(bf16[2,128,512]{2,1,0:T(8,128)(2,1)S(1)} %get-tuple-element.38), channel_id=1, source_target_pairs={{0,4},{1,5},{2,6},{3,7},{4,0},{5,1},{6,2},{7,3},{8,12},{9,13},{10,... | collective-permute-start | bytes 786440 | tf_op jit(solution)/shard_map/ppermute | solution.py:27
  13.0 0.7 %collective-permute-done.1.refs_2_ = bf16[320,256]{1,0:T(8,128)(2,1)S(1)} collective-permute-done((bf16[320,256]{1,0:T(8,128)(2,1)S(1)}, bf16[320,256]{1,0:T(8,128)(2,1)S(1)}, u32[]{:S(2)}, u32[]{:S(2)}) %collective-permute-start.1) | collective-permute-done | bytes 163872 | tf_op jit(solution)/shard_map/ppermute | solution.py:27
  13.7 0.7 %collective-permute-start.3 = (bf16[320,256]{1,0:T(8,128)(2,1)S(1)}, bf16[320,256]{1,0:T(8,128)(2,1)S(1)}, u32[]{:S(2)}, u32[]{:S(2)}) collective-permute-start(bf16[320,256]{1,0:T(8,128)(2,1)S(1)} %broadcast_select_fusion), channel_id=1, source_target_pairs={{0,8},{8,0},{16,24},{24,16},{1,9},{9,1},{17,25},{25,17},{2,10},{10... | collective-permute-start | bytes 491528 | tf_op jit(solution)/shard_map/ppermute | solution.py:27
  14.4 2.0 %collective-permute-done.refs_1_ = bf16[320,256]{1,0:T(8,128)(2,1)S(1)} collective-permute-done((bf16[320,256]{1,0:T(8,128)(2,1)S(1)}, bf16[320,256]{1,0:T(8,128)(2,1)S(1)}, u32[]{:S(2)}, u32[]{:S(2)}) %collective-permute-start) | collective-permute-done | bytes 163872 | tf_op jit(solution)/shard_map/ppermute | solution.py:27
  16.5 0.0 collective-permute-done.2.refs_3_
  16.5 2.5 %all-gather = bf16[1920,256]{1,0:T(8,128)(2,1)S(1)} all-gather(bf16[960,256]{1,0:T(8,128)(2,1)S(1)} %join.1.first_ref), channel_id=2, replica_groups={{0,1},{2,3},{4,5},{6,7},{8,9},{10,11},{12,13},{14,15},{16,17},{18,19},{..., dimensions={0}, use_global_device_ids=true | all-gather | bytes 1474560 | tf_op jit(solution)/shard_map/all_gather | solution.py:268
  19.0 1.2 %collective-permute-done.4.refs_1_ = bf16[2,128,512]{2,1,0:T(8,128)(2,1)S(1)} collective-permute-done((bf16[2,128,512]{2,1,0:T(8,128)(2,1)S(1)}, bf16[2,128,512]{2,1,0:T(8,128)(2,1)S(1)}, u32[]{:S(2)}, u32[]{:S(2)}) %collective-permute-start.4) | collective-permute-done | bytes 262176 | tf_op jit(solution)/shard_map/ppermute | solution.py:27
  20.2 0.1 collective-permute-done.5.refs_2_
  20.3 0.0 collective-permute-done.3.last_ref
  20.3 0.0 collective-permute-start.6
  20.3 1.3 %pair_scores.2 = (f32[8,128]{1,0:T(8,128)S(1)}, f32[8,128]{1,0:T(8,128)S(1)}, f32[8,128]{1,0:T(8,128)S(1)}, f32[8,128]{1,0:T(8,128)S(1)}) custom-call(bf16[960,256]{1,0:T(8,128)(2,1)S(1)} %join.1.first_ref, bf16[320,256]{1,0:T(8,128)(2,1)S(1)} %collective-permute-done.3.last_ref, bf16[2,128,512]{2,1,0:T(8,128)(2,1)S(1)} %get-tuple-element.41.refs_0_, ...), custom_call_target="tpu_custom_call" | custom-call | flops 671088640 | bytes 1835008 | tf_op jit(solution)/shard_map/pair_scores/pallas_call | solution.py:212
  21.5 0.1 collective-permute-done.6.last_ref
  21.7 1.3 %pair_scores.3 = (f32[8,128]{1,0:T(8,128)S(1)}, f32[8,128]{1,0:T(8,128)S(1)}, f32[8,128]{1,0:T(8,128)S(1)}, f32[8,128]{1,0:T(8,128)S(1)}) custom-call(bf16[2,960,256]{2,1,0:T(8,128)(2,1)S(1)} %bitcast.2, bf16[320,256]{1,0:T(8,128)(2,1)S(1)} %collective-permute-done.6.last_ref, bf16[2,128,512]{2,1,0:T(8,128)(2,1)S(1)} %get-tuple-element.41.refs_0_, ...), custom_call_target="tpu_custom_call" | custom-call | flops 671088640 | bytes 1835008 | tf_op jit(solution)/shard_map/pair_scores/pallas_call | solution.py:212
  22.9 1.8 %collective-permute-start.7 = (f32[8,128]{1,0:T(8,128)S(1)}, f32[8,128]{1,0:T(8,128)S(1)}, u32[]{:S(2)}, u32[]{:S(2)}) collective-permute-start(f32[8,128]{1,0:T(8,128)S(1)} %get-tuple-element.52), channel_id=1, source_target_pairs={{0,2},{1,3},{2,0},{3,1},{4,6},{5,7},{6,4},{7,5},{8,10},{9,11},{10,... | collective-permute-start | bytes 12296 | tf_op jit(solution)/shard_map/ppermute | solution.py:27
  24.7 1.1 %collective-permute-start.8 = (f32[8,128]{1,0:T(8,128)S(1)}, f32[8,128]{1,0:T(8,128)S(1)}, u32[]{:S(2)}, u32[]{:S(2)}) collective-permute-start(f32[8,128]{1,0:T(8,128)S(1)} %get-tuple-element.53), channel_id=1, source_target_pairs={{0,6},{1,7},{2,4},{3,5},{4,2},{5,3},{6,0},{7,1},{8,14},{9,15},{10,... | collective-permute-start | bytes 12296 | tf_op jit(solution)/shard_map/ppermute | solution.py:27
  25.9 0.6 %collective-permute-start.9 = (f32[8,128]{1,0:T(8,128)S(1)}, f32[8,128]{1,0:T(8,128)S(1)}, u32[]{:S(2)}, u32[]{:S(2)}) collective-permute-start(f32[8,128]{1,0:T(8,128)S(1)} %get-tuple-element.54), channel_id=1, source_target_pairs={{0,4},{1,5},{2,6},{3,7},{4,0},{5,1},{6,2},{7,3},{8,12},{9,13},{10,... | collective-permute-start | bytes 12296 | tf_op jit(solution)/shard_map/ppermute | solution.py:27
  26.5 0.1 collective-permute-done.7
  26.6 2.6 %collective-permute-done.8 = f32[8,128]{1,0:T(8,128)S(1)} collective-permute-done((f32[8,128]{1,0:T(8,128)S(1)}, f32[8,128]{1,0:T(8,128)S(1)}, u32[]{:S(2)}, u32[]{:S(2)}) %collective-permute-start.8) | collective-permute-done | bytes 4128 | tf_op jit(solution)/shard_map/ppermute | solution.py:27
  29.2 0.2 collective-permute-done.9
  29.5 0.6 %add_add_fusion = f32[8,128]{1,0:T(8,128)} fusion(f32[8,128]{1,0:T(8,128)S(1)} %collective-permute-done.9, f32[8,128]{1,0:T(8,128)S(1)} %collective-permute-done.8, f32[8,128]{1,0:T(8,128)S(1)} %get-tuple-element.51, f32[8,128]{1,0:T(8,128)S(1)} %collective-permute-done.7), kind=kLoop, calls=%fused_computation.1 | loop fusion | flops 3072 | bytes 20480 | tf_op jit(solution)/shard_map/add | solution.py:276
  (2 shorter events, 0.1 us)
Async XLA Ops:
  1.8 11.9 %collective-permute-start.1 = (bf16[320,256]{1,0:T(8,128)(2,1)S(1)}, bf16[320,256]{1,0:T(8,128)(2,1)S(1)}, u32[]{:S(2)}, u32[]{:S(2)}) collective-permute-start(bf16[320,256]{1,0:T(8,128)(2,1)S(1)} %get-tuple-element.32.refs_0_), channel_id=1, source_target_pairs={{0,16},{8,24},{16,0},{24,8},{1,17},{9,25},{17,1},{25,9},{2,18},{10... | collective-permute-start | bytes 491528 | tf_op jit(solution)/shard_map/ppermute | solution.py:27
  5.9 10.6 %collective-permute-start.2 = (bf16[2,128,512]{2,1,0:T(8,128)(2,1)S(1)}, bf16[2,128,512]{2,1,0:T(8,128)(2,1)S(1)}, u32[]{:S(2)}, u32[]{:S(2)}) collective-permute-start(bf16[2,128,512]{2,1,0:T(8,128)(2,1)S(1)} %get-tuple-element.31), channel_id=1, source_target_pairs={{0,6},{1,7},{2,4},{3,5},{4,2},{5,3},{6,0},{7,1},{8,14},{9,15},{10,... | collective-permute-start | bytes 786440 | tf_op jit(solution)/shard_map/ppermute | solution.py:27
  8.3 8.2 %collective-permute-start = (bf16[320,256]{1,0:T(8,128)(2,1)S(1)}, bf16[320,256]{1,0:T(8,128)(2,1)S(1)}, u32[]{:S(2)}, u32[]{:S(2)}) collective-permute-start(bf16[320,256]{1,0:T(8,128)(2,1)S(1)} %get-tuple-element.32.refs_0_), channel_id=1, source_target_pairs={{0,8},{8,0},{16,24},{24,16},{1,9},{9,1},{17,25},{25,17},{2,10},{10... | collective-permute-start | bytes 491528 | tf_op jit(solution)/shard_map/ppermute | solution.py:27
  11.9 8.3 %collective-permute-start.4 = (bf16[2,128,512]{2,1,0:T(8,128)(2,1)S(1)}, bf16[2,128,512]{2,1,0:T(8,128)(2,1)S(1)}, u32[]{:S(2)}, u32[]{:S(2)}) collective-permute-start(bf16[2,128,512]{2,1,0:T(8,128)(2,1)S(1)} %get-tuple-element.37), channel_id=1, source_target_pairs={{0,2},{1,3},{2,0},{3,1},{4,6},{5,7},{6,4},{7,5},{8,10},{9,11},{10,... | collective-permute-start | bytes 786440 | tf_op jit(solution)/shard_map/ppermute | solution.py:27
  12.5 7.8 %collective-permute-start.5 = (bf16[2,128,512]{2,1,0:T(8,128)(2,1)S(1)}, bf16[2,128,512]{2,1,0:T(8,128)(2,1)S(1)}, u32[]{:S(2)}, u32[]{:S(2)}) collective-permute-start(bf16[2,128,512]{2,1,0:T(8,128)(2,1)S(1)} %get-tuple-element.38), channel_id=1, source_target_pairs={{0,4},{1,5},{2,6},{3,7},{4,0},{5,1},{6,2},{7,3},{8,12},{9,13},{10,... | collective-permute-start | bytes 786440 | tf_op jit(solution)/shard_map/ppermute | solution.py:27
  13.7 6.6 %collective-permute-start.3 = (bf16[320,256]{1,0:T(8,128)(2,1)S(1)}, bf16[320,256]{1,0:T(8,128)(2,1)S(1)}, u32[]{:S(2)}, u32[]{:S(2)}) collective-permute-start(bf16[320,256]{1,0:T(8,128)(2,1)S(1)} %broadcast_select_fusion), channel_id=1, source_target_pairs={{0,8},{8,0},{16,24},{24,16},{1,9},{9,1},{17,25},{25,17},{2,10},{10... | collective-permute-start | bytes 491528 | tf_op jit(solution)/shard_map/ppermute | solution.py:27
  20.3 1.4 %collective-permute-start.6 = (bf16[320,256]{1,0:T(8,128)(2,1)S(1)}, bf16[320,256]{1,0:T(8,128)(2,1)S(1)}, u32[]{:S(2)}, u32[]{:S(2)}) collective-permute-start(bf16[320,256]{1,0:T(8,128)(2,1)S(1)} %collective-permute-done.3.last_ref), channel_id=1, source_target_pairs={{0,1},{1,0},{2,3},{3,2},{4,5},{5,4},{6,7},{7,6},{8,9},{9,8},{10,11... | collective-permute-start | bytes 491528 | tf_op jit(solution)/shard_map/ppermute | solution.py:27
  22.9 3.7 %collective-permute-start.7 = (f32[8,128]{1,0:T(8,128)S(1)}, f32[8,128]{1,0:T(8,128)S(1)}, u32[]{:S(2)}, u32[]{:S(2)}) collective-permute-start(f32[8,128]{1,0:T(8,128)S(1)} %get-tuple-element.52), channel_id=1, source_target_pairs={{0,2},{1,3},{2,0},{3,1},{4,6},{5,7},{6,4},{7,5},{8,10},{9,11},{10,... | collective-permute-start | bytes 12296 | tf_op jit(solution)/shard_map/ppermute | solution.py:27
  24.7 4.5 %collective-permute-start.8 = (f32[8,128]{1,0:T(8,128)S(1)}, f32[8,128]{1,0:T(8,128)S(1)}, u32[]{:S(2)}, u32[]{:S(2)}) collective-permute-start(f32[8,128]{1,0:T(8,128)S(1)} %get-tuple-element.53), channel_id=1, source_target_pairs={{0,6},{1,7},{2,4},{3,5},{4,2},{5,3},{6,0},{7,1},{8,14},{9,15},{10,... | collective-permute-start | bytes 12296 | tf_op jit(solution)/shard_map/ppermute | solution.py:27
  25.9 3.6 %collective-permute-start.9 = (f32[8,128]{1,0:T(8,128)S(1)}, f32[8,128]{1,0:T(8,128)S(1)}, u32[]{:S(2)}, u32[]{:S(2)}) collective-permute-start(f32[8,128]{1,0:T(8,128)S(1)} %get-tuple-element.54), channel_id=1, source_target_pairs={{0,4},{1,5},{2,6},{3,7},{4,0},{5,1},{6,2},{7,3},{8,12},{9,13},{10,... | collective-permute-start | bytes 12296 | tf_op jit(solution)/shard_map/ppermute | solution.py:27

commit v8 on v7

--- a/solution.py
+++ b/solution.py
@@ -240,7 +240,7 @@
     eigenvalues,
 ):
     groups, chips = lax.axis_size("seq"), lax.axis_size("blk") // CORES
-    far = sorted(range(1, chips), key=lambda m: -m.bit_count())
+    far = sorted(range(1, chips), key=lambda m: (-m.bit_count(), -m))
     packed, *ahead = pack(
         far[:1],
         block_table.T,
@@ -254,10 +254,7 @@
     )
     own = [packed]
     for m in range(1, groups):
-        piece = own[m & (m - 1)]
-        if m & (m - 1):
-            piece = jnp.where(lax.axis_index("seq") >= 0, piece, packed)
-        own.append(swap(piece, "seq", m & -m))
+        own.append(swap(own[m & (m - 1)], "seq", m & -m))
     others = far[1:] + [0]
     mask, *later = take_blocks(others, block_table.T, seq_lengths, train_acts, train_grads)
     chunks = dict(zip(far[:1] + others, ahead + later))

time: 30.4 us -> 30.4 us (level)
  no operation moved by 1% of the time
where the time goes in v8:
time: 30.4 us; the launch traced here: 30.1 us
  starting transfers between devices  13.4 us (44%)
  waiting for transfers between devices  7.31 us (24%)
  Pallas kernels  6.3 us (21%)
  blocking collectives  2.51 us (8%)
  other arithmetic  0.6 us (2%)
    ppermute x10, starting transfers between devices, swap(): lax.ppermute(array, axis, [(i, i ^ bits) for i in range(lax.axis_size(axi...  13.4 us
    ppermute x10, waiting for transfers between devices, swap(): lax.ppermute(array, axis, [(i, i ^ bits) for i in range(lax.axis_size(axi...  7.31 us
    pallas_call x2, Pallas kernels, pair_scores(): pl.pallas_call(functools.partial(pair_kernel, core, rows, chips), out_sha...  2.53 us
    all_gather x1, blocking collectives, on_device(): both = lax.all_gather(first, 'blk', axis=0, axis_index_groups=pairs)  2.51 us
    pallas_call x1, Pallas kernels, take_blocks(): pl.pallas_call(functools.partial(blocks_kernel, distances), out_shape=(pl...  1.99 us
    pallas_call x1, Pallas kernels, pack(): pl.pallas_call(functools.partial(pack_kernel, distances), out_shape=(pack...  1.75 us
  transfers between devices with their start and end apart: 10, of which 8 were waited for; matrix products, arithmetic and copies ran while one was open for 0% of the time, Pallas kernels for 11%

profile of v8, /device:TPU:0, one launch (start us, length us, event | category | flops | bytes accessed | tf_op | source)
XLA Modules:
  0.0 30.1 jit_solution(5455120052666711986)
XLA Ops:
  0.0 1.7 %pack.1 = (bf16[320,256]{1,0:T(8,128)(2,1)S(1)}, bf16[2,128,512]{2,1,0:T(8,128)(2,1)S(1)}) custom-call(s32[2,8]{1,0:T(2,128)} %bitcast.3, bf16[128,4096]{1,0:T(8,128)(2,1)} %acts_ref.3, bf16[128,14336]{1,0:T(8,128)(2,1)} %grads_ref.3, bf16[1,64,256]{2,1,0:T(8,128)(2,1)} %refs_0_.1, bf16[1,64,256]{2,1,0:T(8,128)(2,1)} %refs_1_.1, ...), custom_call_target="tpu_custom_call" | custom-call | tf_op jit(solution)/shard_map/pack/pallas_call | solution.py:128
  1.8 4.0 %collective-permute-start.2 = (bf16[2,128,512]{2,1,0:T(8,128)(2,1)S(1)}, bf16[2,128,512]{2,1,0:T(8,128)(2,1)S(1)}, u32[]{:S(2)}, u32[]{:S(2)}) collective-permute-start(bf16[2,128,512]{2,1,0:T(8,128)(2,1)S(1)} %get-tuple-element.31), channel_id=1, source_target_pairs={{0,6},{1,7},{2,4},{3,5},{4,2},{5,3},{6,0},{7,1},{8,14},{9,15},{10,... | collective-permute-start | bytes 786440 | tf_op jit(solution)/shard_map/ppermute | solution.py:27
  5.7 2.6 %collective-permute-start.1 = (bf16[320,256]{1,0:T(8,128)(2,1)S(1)}, bf16[320,256]{1,0:T(8,128)(2,1)S(1)}, u32[]{:S(2)}, u32[]{:S(2)}) collective-permute-start(bf16[320,256]{1,0:T(8,128)(2,1)S(1)} %get-tuple-element.32.refs_0_), channel_id=1, source_target_pairs={{0,16},{8,24},{16,0},{24,8},{1,17},{9,25},{17,1},{25,9},{2,18},{10... | collective-permute-start | bytes 491528 | tf_op jit(solution)/shard_map/ppermute | solution.py:27
  8.3 1.6 %collective-permute-start = (bf16[320,256]{1,0:T(8,128)(2,1)S(1)}, bf16[320,256]{1,0:T(8,128)(2,1)S(1)}, u32[]{:S(2)}, u32[]{:S(2)}) collective-permute-start(bf16[320,256]{1,0:T(8,128)(2,1)S(1)} %get-tuple-element.32.refs_0_), channel_id=1, source_target_pairs={{0,8},{8,0},{16,24},{24,16},{1,9},{9,1},{17,25},{25,17},{2,10},{10... | collective-permute-start | bytes 491528 | tf_op jit(solution)/shard_map/ppermute | solution.py:27
  9.9 2.0 %take_blocks.1 = (f32[4,8,128]{2,1,0:T(8,128)S(1)}, bf16[2,128,512]{2,1,0:T(8,128)(2,1)S(1)}, bf16[2,128,512]{2,1,0:T(8,128)(2,1)S(1)}, bf16[2,128,512]{2,1,0:T(8,128)(2,1)S(1)}) custom-call(s32[2,8]{1,0:T(2,128)} %bitcast.4, s32[4]{0:T(128)} %lengths_ref.1, bf16[128,4096]{1,0:T(8,128)(2,1)} %acts_ref.3, bf16[128,14336]{1,0:T(8,128)(2,1)} %grads_ref.3), custom_call_target="tpu_custom_call" | custom-call | tf_op jit(solution)/shard_map/take_blocks/pallas_call | solution.py:86
  11.9 0.6 %collective-permute-start.4 = (bf16[2,128,512]{2,1,0:T(8,128)(2,1)S(1)}, bf16[2,128,512]{2,1,0:T(8,128)(2,1)S(1)}, u32[]{:S(2)}, u32[]{:S(2)}) collective-permute-start(bf16[2,128,512]{2,1,0:T(8,128)(2,1)S(1)} %get-tuple-element.37), channel_id=1, source_target_pairs={{0,4},{1,5},{2,6},{3,7},{4,0},{5,1},{6,2},{7,3},{8,12},{9,13},{10,... | collective-permute-start | bytes 786440 | tf_op jit(solution)/shard_map/ppermute | solution.py:27
  12.5 0.5 %collective-permute-start.5 = (bf16[2,128,512]{2,1,0:T(8,128)(2,1)S(1)}, bf16[2,128,512]{2,1,0:T(8,128)(2,1)S(1)}, u32[]{:S(2)}, u32[]{:S(2)}) collective-permute-start(bf16[2,128,512]{2,1,0:T(8,128)(2,1)S(1)} %get-tuple-element.38), channel_id=1, source_target_pairs={{0,2},{1,3},{2,0},{3,1},{4,6},{5,7},{6,4},{7,5},{8,10},{9,11},{10,... | collective-permute-start | bytes 786440 | tf_op jit(solution)/shard_map/ppermute | solution.py:27
  13.0 2.9 %collective-permute-done.1.refs_2_ = bf16[320,256]{1,0:T(8,128)(2,1)S(1)} collective-permute-done((bf16[320,256]{1,0:T(8,128)(2,1)S(1)}, bf16[320,256]{1,0:T(8,128)(2,1)S(1)}, u32[]{:S(2)}, u32[]{:S(2)}) %collective-permute-start.1) | collective-permute-done | bytes 163872 | tf_op jit(solution)/shard_map/ppermute | solution.py:27
  15.9 0.6 %collective-permute-start.3 = (bf16[320,256]{1,0:T(8,128)(2,1)S(1)}, bf16[320,256]{1,0:T(8,128)(2,1)S(1)}, u32[]{:S(2)}, u32[]{:S(2)}) collective-permute-start(bf16[320,256]{1,0:T(8,128)(2,1)S(1)} %collective-permute-done.1.refs_2_), channel_id=1, source_target_pairs={{0,8},{8,0},{16,24},{24,16},{1,9},{9,1},{17,25},{25,17},{2,10},{10... | collective-permute-start | bytes 491528 | tf_op jit(solution)/shard_map/ppermute | solution.py:27
  16.5 0.0 collective-permute-done.refs_1_
  16.5 0.0 collective-permute-done.2.refs_3_
  16.5 2.5 %all-gather = bf16[1920,256]{1,0:T(8,128)(2,1)S(1)} all-gather(bf16[960,256]{1,0:T(8,128)(2,1)S(1)} %join.1.first_ref), channel_id=2, replica_groups={{0,1},{2,3},{4,5},{6,7},{8,9},{10,11},{12,13},{14,15},{16,17},{18,19},{..., dimensions={0}, use_global_device_ids=true | all-gather | bytes 1474560 | tf_op jit(solution)/shard_map/all_gather | solution.py:265
  19.0 0.1 collective-permute-done.4.refs_2_
  19.2 0.2 collective-permute-done.5.refs_1_
  19.4 1.8 %collective-permute-done.3.last_ref = bf16[320,256]{1,0:T(8,128)(2,1)S(1)} collective-permute-done((bf16[320,256]{1,0:T(8,128)(2,1)S(1)}, bf16[320,256]{1,0:T(8,128)(2,1)S(1)}, u32[]{:S(2)}, u32[]{:S(2)}) %collective-permute-start.3) | collective-permute-done | bytes 163872 | tf_op jit(solution)/shard_map/ppermute | solution.py:27
  21.2 0.0 collective-permute-start.6
  21.2 1.3 %pair_scores.2 = (f32[8,128]{1,0:T(8,128)S(1)}, f32[8,128]{1,0:T(8,128)S(1)}, f32[8,128]{1,0:T(8,128)S(1)}, f32[8,128]{1,0:T(8,128)S(1)}) custom-call(bf16[960,256]{1,0:T(8,128)(2,1)S(1)} %join.1.first_ref, bf16[320,256]{1,0:T(8,128)(2,1)S(1)} %collective-permute-done.3.last_ref, bf16[2,128,512]{2,1,0:T(8,128)(2,1)S(1)} %get-tuple-element.41.refs_0_, ...), custom_call_target="tpu_custom_call" | custom-call | flops 671088640 | bytes 1835008 | tf_op jit(solution)/shard_map/pair_scores/pallas_call | solution.py:212
  22.5 0.1 collective-permute-done.6.last_ref
  22.6 1.3 %pair_scores.3 = (f32[8,128]{1,0:T(8,128)S(1)}, f32[8,128]{1,0:T(8,128)S(1)}, f32[8,128]{1,0:T(8,128)S(1)}, f32[8,128]{1,0:T(8,128)S(1)}) custom-call(bf16[2,960,256]{2,1,0:T(8,128)(2,1)S(1)} %bitcast.2, bf16[320,256]{1,0:T(8,128)(2,1)S(1)} %collective-permute-done.6.last_ref, bf16[2,128,512]{2,1,0:T(8,128)(2,1)S(1)} %get-tuple-element.41.refs_0_, ...), custom_call_target="tpu_custom_call" | custom-call | flops 671088640 | bytes 1835008 | tf_op jit(solution)/shard_map/pair_scores/pallas_call | solution.py:212
  23.9 0.6 %collective-permute-start.7 = (f32[8,128]{1,0:T(8,128)S(1)}, f32[8,128]{1,0:T(8,128)S(1)}, u32[]{:S(2)}, u32[]{:S(2)}) collective-permute-start(f32[8,128]{1,0:T(8,128)S(1)} %get-tuple-element.52), channel_id=1, source_target_pairs={{0,2},{1,3},{2,0},{3,1},{4,6},{5,7},{6,4},{7,5},{8,10},{9,11},{10,... | collective-permute-start | bytes 12296 | tf_op jit(solution)/shard_map/ppermute | solution.py:27
  24.5 1.4 %collective-permute-start.8 = (f32[8,128]{1,0:T(8,128)S(1)}, f32[8,128]{1,0:T(8,128)S(1)}, u32[]{:S(2)}, u32[]{:S(2)}) collective-permute-start(f32[8,128]{1,0:T(8,128)S(1)} %get-tuple-element.53), channel_id=1, source_target_pairs={{0,6},{1,7},{2,4},{3,5},{4,2},{5,3},{6,0},{7,1},{8,14},{9,15},{10,... | collective-permute-start | bytes 12296 | tf_op jit(solution)/shard_map/ppermute | solution.py:27
  25.9 1.5 %collective-permute-start.9 = (f32[8,128]{1,0:T(8,128)S(1)}, f32[8,128]{1,0:T(8,128)S(1)}, u32[]{:S(2)}, u32[]{:S(2)}) collective-permute-start(f32[8,128]{1,0:T(8,128)S(1)} %get-tuple-element.54), channel_id=1, source_target_pairs={{0,4},{1,5},{2,6},{3,7},{4,0},{5,1},{6,2},{7,3},{8,12},{9,13},{10,... | collective-permute-start | bytes 12296 | tf_op jit(solution)/shard_map/ppermute | solution.py:27
  27.4 0.1 collective-permute-done.7
  27.6 1.4 %collective-permute-done.8 = f32[8,128]{1,0:T(8,128)S(1)} collective-permute-done((f32[8,128]{1,0:T(8,128)S(1)}, f32[8,128]{1,0:T(8,128)S(1)}, u32[]{:S(2)}, u32[]{:S(2)}) %collective-permute-start.8) | collective-permute-done | bytes 4128 | tf_op jit(solution)/shard_map/ppermute | solution.py:27
  29.0 0.5 %collective-permute-done.9 = f32[8,128]{1,0:T(8,128)S(1)} collective-permute-done((f32[8,128]{1,0:T(8,128)S(1)}, f32[8,128]{1,0:T(8,128)S(1)}, u32[]{:S(2)}, u32[]{:S(2)}) %collective-permute-start.9) | collective-permute-done | bytes 4128 | tf_op jit(solution)/shard_map/ppermute | solution.py:27
  29.5 0.6 %add_add_fusion = f32[8,128]{1,0:T(8,128)} fusion(f32[8,128]{1,0:T(8,128)S(1)} %collective-permute-done.9, f32[8,128]{1,0:T(8,128)S(1)} %collective-permute-done.8, f32[8,128]{1,0:T(8,128)S(1)} %get-tuple-element.51, f32[8,128]{1,0:T(8,128)S(1)} %collective-permute-done.7), kind=kLoop, calls=%fused_computation | loop fusion | flops 3072 | bytes 20480 | tf_op jit(solution)/shard_map/add | solution.py:273
  (1 shorter events, 0.0 us)
Async XLA Ops:
  1.8 14.7 %collective-permute-start.2 = (bf16[2,128,512]{2,1,0:T(8,128)(2,1)S(1)}, bf16[2,128,512]{2,1,0:T(8,128)(2,1)S(1)}, u32[]{:S(2)}, u32[]{:S(2)}) collective-permute-start(bf16[2,128,512]{2,1,0:T(8,128)(2,1)S(1)} %get-tuple-element.31), channel_id=1, source_target_pairs={{0,6},{1,7},{2,4},{3,5},{4,2},{5,3},{6,0},{7,1},{8,14},{9,15},{10,... | collective-permute-start | bytes 786440 | tf_op jit(solution)/shard_map/ppermute | solution.py:27
  5.7 10.2 %collective-permute-start.1 = (bf16[320,256]{1,0:T(8,128)(2,1)S(1)}, bf16[320,256]{1,0:T(8,128)(2,1)S(1)}, u32[]{:S(2)}, u32[]{:S(2)}) collective-permute-start(bf16[320,256]{1,0:T(8,128)(2,1)S(1)} %get-tuple-element.32.refs_0_), channel_id=1, source_target_pairs={{0,16},{8,24},{16,0},{24,8},{1,17},{9,25},{17,1},{25,9},{2,18},{10... | collective-permute-start | bytes 491528 | tf_op jit(solution)/shard_map/ppermute | solution.py:27
  8.3 8.2 %collective-permute-start = (bf16[320,256]{1,0:T(8,128)(2,1)S(1)}, bf16[320,256]{1,0:T(8,128)(2,1)S(1)}, u32[]{:S(2)}, u32[]{:S(2)}) collective-permute-start(bf16[320,256]{1,0:T(8,128)(2,1)S(1)} %get-tuple-element.32.refs_0_), channel_id=1, source_target_pairs={{0,8},{8,0},{16,24},{24,16},{1,9},{9,1},{17,25},{25,17},{2,10},{10... | collective-permute-start | bytes 491528 | tf_op jit(solution)/shard_map/ppermute | solution.py:27
  11.9 7.3 %collective-permute-start.4 = (bf16[2,128,512]{2,1,0:T(8,128)(2,1)S(1)}, bf16[2,128,512]{2,1,0:T(8,128)(2,1)S(1)}, u32[]{:S(2)}, u32[]{:S(2)}) collective-permute-start(bf16[2,128,512]{2,1,0:T(8,128)(2,1)S(1)} %get-tuple-element.37), channel_id=1, source_target_pairs={{0,4},{1,5},{2,6},{3,7},{4,0},{5,1},{6,2},{7,3},{8,12},{9,13},{10,... | collective-permute-start | bytes 786440 | tf_op jit(solution)/shard_map/ppermute | solution.py:27
  12.5 6.9 %collective-permute-start.5 = (bf16[2,128,512]{2,1,0:T(8,128)(2,1)S(1)}, bf16[2,128,512]{2,1,0:T(8,128)(2,1)S(1)}, u32[]{:S(2)}, u32[]{:S(2)}) collective-permute-start(bf16[2,128,512]{2,1,0:T(8,128)(2,1)S(1)} %get-tuple-element.38), channel_id=1, source_target_pairs={{0,2},{1,3},{2,0},{3,1},{4,6},{5,7},{6,4},{7,5},{8,10},{9,11},{10,... | collective-permute-start | bytes 786440 | tf_op jit(solution)/shard_map/ppermute | solution.py:27
  15.9 5.3 %collective-permute-start.3 = (bf16[320,256]{1,0:T(8,128)(2,1)S(1)}, bf16[320,256]{1,0:T(8,128)(2,1)S(1)}, u32[]{:S(2)}, u32[]{:S(2)}) collective-permute-start(bf16[320,256]{1,0:T(8,128)(2,1)S(1)} %collective-permute-done.1.refs_2_), channel_id=1, source_target_pairs={{0,8},{8,0},{16,24},{24,16},{1,9},{9,1},{17,25},{25,17},{2,10},{10... | collective-permute-start | bytes 491528 | tf_op jit(solution)/shard_map/ppermute | solution.py:27
  21.2 1.4 %collective-permute-start.6 = (bf16[320,256]{1,0:T(8,128)(2,1)S(1)}, bf16[320,256]{1,0:T(8,128)(2,1)S(1)}, u32[]{:S(2)}, u32[]{:S(2)}) collective-permute-start(bf16[320,256]{1,0:T(8,128)(2,1)S(1)} %collective-permute-done.3.last_ref), channel_id=1, source_target_pairs={{0,1},{1,0},{2,3},{3,2},{4,5},{5,4},{6,7},{7,6},{8,9},{9,8},{10,11... | collective-permute-start | bytes 491528 | tf_op jit(solution)/shard_map/ppermute | solution.py:27
  23.9 3.7 %collective-permute-start.7 = (f32[8,128]{1,0:T(8,128)S(1)}, f32[8,128]{1,0:T(8,128)S(1)}, u32[]{:S(2)}, u32[]{:S(2)}) collective-permute-start(f32[8,128]{1,0:T(8,128)S(1)} %get-tuple-element.52), channel_id=1, source_target_pairs={{0,2},{1,3},{2,0},{3,1},{4,6},{5,7},{6,4},{7,5},{8,10},{9,11},{10,... | collective-permute-start | bytes 12296 | tf_op jit(solution)/shard_map/ppermute | solution.py:27
  24.5 4.5 %collective-permute-start.8 = (f32[8,128]{1,0:T(8,128)S(1)}, f32[8,128]{1,0:T(8,128)S(1)}, u32[]{:S(2)}, u32[]{:S(2)}) collective-permute-start(f32[8,128]{1,0:T(8,128)S(1)} %get-tuple-element.53), channel_id=1, source_target_pairs={{0,6},{1,7},{2,4},{3,5},{4,2},{5,3},{6,0},{7,1},{8,14},{9,15},{10,... | collective-permute-start | bytes 12296 | tf_op jit(solution)/shard_map/ppermute | solution.py:27
  25.9 3.6 %collective-permute-start.9 = (f32[8,128]{1,0:T(8,128)S(1)}, f32[8,128]{1,0:T(8,128)S(1)}, u32[]{:S(2)}, u32[]{:S(2)}) collective-permute-start(f32[8,128]{1,0:T(8,128)S(1)} %get-tuple-element.54), channel_id=1, source_target_pairs={{0,4},{1,5},{2,6},{3,7},{4,0},{5,1},{6,2},{7,3},{8,12},{9,13},{10,... | collective-permute-start | bytes 12296 | tf_op jit(solution)/shard_map/ppermute | solution.py:27

commit v9 on v8

--- a/solution.py
+++ b/solution.py
@@ -138,25 +138,6 @@
         compiler_params=pltpu.CompilerParams(vmem_limit_bytes=PACK_VMEM),
         name="pack",
     )(*operands)
-
-
-def join_kernel(*refs):
-    pieces, out = refs[:-1], refs[-1]
-    rows = pieces[0].shape[0]
-    for m, piece in enumerate(pieces):
-        out[m * rows : (m + 1) * rows, :] = piece[...]
-
-
-def join(pieces):
-    rows = pieces[0].shape[0]
-    return pl.pallas_call(
-        join_kernel,
-        out_shape=jax.ShapeDtypeStruct((len(pieces) * rows, BLOCK), jnp.bfloat16),
-        in_specs=[VMEM] * len(pieces),
-        out_specs=VMEM,
-        compiler_params=pltpu.CompilerParams(vmem_limit_bytes=VMEM_BYTES),
-        name="join",
-    )(*pieces)
 
 
 def pair_kernel(core, rows, chips, first_ref, last_ref, *refs):
@@ -260,7 +241,7 @@
     chunks = dict(zip(far[:1] + others, ahead + later))
     chunks = [chunks[0]] + [swap(chunks[m], "blk", CORES * m) for m in far]
     early, chunks[1] = lax.optimization_barrier((own[:-1], chunks[1]))
-    first = join(early)
+    first = jnp.concatenate(early, axis=0)
     pairs = [list(range(c, c + CORES)) for c in range(0, chips * CORES, CORES)]
     both = lax.all_gather(first, "blk", axis=0, axis_index_groups=pairs)
     first, last, both, chunks = lax.optimization_barrier((first, own[-1], both, chunks))

time: 30.4 us -> 30.4 us (level)
  no operation moved by 1% of the time
where the time goes in v9:
time: 30.4 us; the launch traced here: 30.1 us
  starting transfers between devices  13.4 us (44%)
  waiting for transfers between devices  7.29 us (24%)
  Pallas kernels  6.27 us (21%)
  blocking collectives  2.51 us (8%)
  other arithmetic  0.6 us (2%)
    ppermute x10, starting transfers between devices, swap(): lax.ppermute(array, axis, [(i, i ^ bits) for i in range(lax.axis_size(axi...  13.4 us
    ppermute x10, waiting for transfers between devices, swap(): lax.ppermute(array, axis, [(i, i ^ bits) for i in range(lax.axis_size(axi...  7.29 us
    pallas_call x2, Pallas kernels, pair_scores(): pl.pallas_call(functools.partial(pair_kernel, core, rows, chips), out_sha...  2.53 us
    all_gather x1, blocking collectives, on_device(): both = lax.all_gather(first, 'blk', axis=0, axis_index_groups=pairs)  2.51 us
    pallas_call x1, Pallas kernels, take_blocks(): pl.pallas_call(functools.partial(blocks_kernel, distances), out_shape=(pl...  1.99 us
    pallas_call x1, Pallas kernels, pack(): pl.pallas_call(functools.partial(pack_kernel, distances), out_shape=(pack...  1.75 us
  transfers between devices with their start and end apart: 10, of which 8 were waited for; matrix products, arithmetic and copies ran while one was open for 0% of the time, Pallas kernels for 11%

profile of v9, /device:TPU:0, one launch (start us, length us, event | category | flops | bytes accessed | tf_op | source)
XLA Modules:
  0.0 30.1 jit_solution(9911787023118268333)
XLA Ops:
  0.0 1.7 %pack.1 = (bf16[320,256]{1,0:T(8,128)(2,1)S(1)}, bf16[2,128,512]{2,1,0:T(8,128)(2,1)S(1)}) custom-call(s32[2,8]{1,0:T(2,128)} %bitcast.3, bf16[128,4096]{1,0:T(8,128)(2,1)} %acts_ref.3, bf16[128,14336]{1,0:T(8,128)(2,1)} %grads_ref.3, bf16[1,64,256]{2,1,0:T(8,128)(2,1)} %refs_0_.1, bf16[1,64,256]{2,1,0:T(8,128)(2,1)} %refs_1_.1, ...), custom_call_target="tpu_custom_call" | custom-call | tf_op jit(solution)/shard_map/pack/pallas_call | solution.py:128
  1.8 4.0 %collective-permute-start.2 = (bf16[2,128,512]{2,1,0:T(8,128)(2,1)S(1)}, bf16[2,128,512]{2,1,0:T(8,128)(2,1)S(1)}, u32[]{:S(2)}, u32[]{:S(2)}) collective-permute-start(bf16[2,128,512]{2,1,0:T(8,128)(2,1)S(1)} %get-tuple-element.31), channel_id=1, source_target_pairs={{0,6},{1,7},{2,4},{3,5},{4,2},{5,3},{6,0},{7,1},{8,14},{9,15},{10,... | collective-permute-start | bytes 786440 | tf_op jit(solution)/shard_map/ppermute | solution.py:27
  5.7 2.6 %collective-permute-start.1 = (bf16[320,256]{1,0:T(8,128)(2,1)S(1)}, bf16[320,256]{1,0:T(8,128)(2,1)S(1)}, u32[]{:S(2)}, u32[]{:S(2)}) collective-permute-start(bf16[320,256]{1,0:T(8,128)(2,1)S(1)} %get-tuple-element.32), channel_id=1, source_target_pairs={{0,16},{8,24},{16,0},{24,8},{1,17},{9,25},{17,1},{25,9},{2,18},{10... | collective-permute-start | bytes 491528 | tf_op jit(solution)/shard_map/ppermute | solution.py:27
  8.3 1.6 %collective-permute-start = (bf16[320,256]{1,0:T(8,128)(2,1)S(1)}, bf16[320,256]{1,0:T(8,128)(2,1)S(1)}, u32[]{:S(2)}, u32[]{:S(2)}) collective-permute-start(bf16[320,256]{1,0:T(8,128)(2,1)S(1)} %get-tuple-element.32), channel_id=1, source_target_pairs={{0,8},{8,0},{16,24},{24,16},{1,9},{9,1},{17,25},{25,17},{2,10},{10... | collective-permute-start | bytes 491528 | tf_op jit(solution)/shard_map/ppermute | solution.py:27
  9.9 2.0 %take_blocks.1 = (f32[4,8,128]{2,1,0:T(8,128)S(1)}, bf16[2,128,512]{2,1,0:T(8,128)(2,1)S(1)}, bf16[2,128,512]{2,1,0:T(8,128)(2,1)S(1)}, bf16[2,128,512]{2,1,0:T(8,128)(2,1)S(1)}) custom-call(s32[2,8]{1,0:T(2,128)} %bitcast.4, s32[4]{0:T(128)} %lengths_ref.1, bf16[128,4096]{1,0:T(8,128)(2,1)} %acts_ref.3, bf16[128,14336]{1,0:T(8,128)(2,1)} %grads_ref.3), custom_call_target="tpu_custom_call" | custom-call | tf_op jit(solution)/shard_map/take_blocks/pallas_call | solution.py:86
  11.9 0.6 %collective-permute-start.4 = (bf16[2,128,512]{2,1,0:T(8,128)(2,1)S(1)}, bf16[2,128,512]{2,1,0:T(8,128)(2,1)S(1)}, u32[]{:S(2)}, u32[]{:S(2)}) collective-permute-start(bf16[2,128,512]{2,1,0:T(8,128)(2,1)S(1)} %get-tuple-element.37), channel_id=1, source_target_pairs={{0,4},{1,5},{2,6},{3,7},{4,0},{5,1},{6,2},{7,3},{8,12},{9,13},{10,... | collective-permute-start | bytes 786440 | tf_op jit(solution)/shard_map/ppermute | solution.py:27
  12.5 0.5 %collective-permute-start.5 = (bf16[2,128,512]{2,1,0:T(8,128)(2,1)S(1)}, bf16[2,128,512]{2,1,0:T(8,128)(2,1)S(1)}, u32[]{:S(2)}, u32[]{:S(2)}) collective-permute-start(bf16[2,128,512]{2,1,0:T(8,128)(2,1)S(1)} %get-tuple-element.38), channel_id=1, source_target_pairs={{0,2},{1,3},{2,0},{3,1},{4,6},{5,7},{6,4},{7,5},{8,10},{9,11},{10,... | collective-permute-start | bytes 786440 | tf_op jit(solution)/shard_map/ppermute | solution.py:27
  13.0 2.9 %collective-permute-done.1 = bf16[320,256]{1,0:T(8,128)(2,1)S(1)} collective-permute-done((bf16[320,256]{1,0:T(8,128)(2,1)S(1)}, bf16[320,256]{1,0:T(8,128)(2,1)S(1)}, u32[]{:S(2)}, u32[]{:S(2)}) %collective-permute-start.1) | collective-permute-done | bytes 163872 | tf_op jit(solution)/shard_map/ppermute | solution.py:27
  15.9 0.6 %collective-permute-start.3 = (bf16[320,256]{1,0:T(8,128)(2,1)S(1)}, bf16[320,256]{1,0:T(8,128)(2,1)S(1)}, u32[]{:S(2)}, u32[]{:S(2)}) collective-permute-start(bf16[320,256]{1,0:T(8,128)(2,1)S(1)} %collective-permute-done.1), channel_id=1, source_target_pairs={{0,8},{8,0},{16,24},{24,16},{1,9},{9,1},{17,25},{25,17},{2,10},{10... | collective-permute-start | bytes 491528 | tf_op jit(solution)/shard_map/ppermute | solution.py:27
  16.5 0.0 collective-permute-done
  16.5 0.0 collective-permute-done.2.refs_3_
  16.5 2.5 %all-gather = bf16[1920,256]{1,0:T(8,128)(2,1)S(1)} all-gather(bf16[960,256]{1,0:T(8,128)(2,1)S(1)} %constant_dynamic-update-slice_fusion.first_ref), channel_id=2, replica_groups={{0,1},{2,3},{4,5},{6,7},{8,9},{10,11},{12,13},{14,15},{16,17},{18,19},{..., dimensions={0}, use_global_device_ids=true | all-gather | bytes 1474560 | tf_op jit(solution)/shard_map/all_gather | solution.py:246
  19.0 0.1 collective-permute-done.4.refs_2_
  19.2 0.2 collective-permute-done.5.refs_1_
  19.4 1.8 %collective-permute-done.3.last_ref = bf16[320,256]{1,0:T(8,128)(2,1)S(1)} collective-permute-done((bf16[320,256]{1,0:T(8,128)(2,1)S(1)}, bf16[320,256]{1,0:T(8,128)(2,1)S(1)}, u32[]{:S(2)}, u32[]{:S(2)}) %collective-permute-start.3) | collective-permute-done | bytes 163872 | tf_op jit(solution)/shard_map/ppermute | solution.py:27
  21.2 0.0 collective-permute-start.6
  21.2 1.3 %pair_scores.2 = (f32[8,128]{1,0:T(8,128)S(1)}, f32[8,128]{1,0:T(8,128)S(1)}, f32[8,128]{1,0:T(8,128)S(1)}, f32[8,128]{1,0:T(8,128)S(1)}) custom-call(bf16[960,256]{1,0:T(8,128)(2,1)S(1)} %constant_dynamic-update-slice_fusion.first_ref, bf16[320,256]{1,0:T(8,128)(2,1)S(1)} %collective-permute-done.3.last_ref, ...), custom_call_target="tpu_custom_call" | custom-call | flops 671088640 | bytes 1835008 | tf_op jit(solution)/shard_map/pair_scores/pallas_call | solution.py:193
  22.5 0.1 collective-permute-done.6.last_ref
  22.6 1.3 %pair_scores.3 = (f32[8,128]{1,0:T(8,128)S(1)}, f32[8,128]{1,0:T(8,128)S(1)}, f32[8,128]{1,0:T(8,128)S(1)}, f32[8,128]{1,0:T(8,128)S(1)}) custom-call(bf16[2,960,256]{2,1,0:T(8,128)(2,1)S(1)} %bitcast.2, bf16[320,256]{1,0:T(8,128)(2,1)S(1)} %collective-permute-done.6.last_ref, bf16[2,128,512]{2,1,0:T(8,128)(2,1)S(1)} %get-tuple-element.41.refs_0_, ...), custom_call_target="tpu_custom_call" | custom-call | flops 671088640 | bytes 1835008 | tf_op jit(solution)/shard_map/pair_scores/pallas_call | solution.py:193
  23.9 0.6 %collective-permute-start.7 = (f32[8,128]{1,0:T(8,128)S(1)}, f32[8,128]{1,0:T(8,128)S(1)}, u32[]{:S(2)}, u32[]{:S(2)}) collective-permute-start(f32[8,128]{1,0:T(8,128)S(1)} %get-tuple-element.52), channel_id=1, source_target_pairs={{0,2},{1,3},{2,0},{3,1},{4,6},{5,7},{6,4},{7,5},{8,10},{9,11},{10,... | collective-permute-start | bytes 12296 | tf_op jit(solution)/shard_map/ppermute | solution.py:27
  24.5 1.4 %collective-permute-start.8 = (f32[8,128]{1,0:T(8,128)S(1)}, f32[8,128]{1,0:T(8,128)S(1)}, u32[]{:S(2)}, u32[]{:S(2)}) collective-permute-start(f32[8,128]{1,0:T(8,128)S(1)} %get-tuple-element.53), channel_id=1, source_target_pairs={{0,6},{1,7},{2,4},{3,5},{4,2},{5,3},{6,0},{7,1},{8,14},{9,15},{10,... | collective-permute-start | bytes 12296 | tf_op jit(solution)/shard_map/ppermute | solution.py:27
  25.9 1.5 %collective-permute-start.9 = (f32[8,128]{1,0:T(8,128)S(1)}, f32[8,128]{1,0:T(8,128)S(1)}, u32[]{:S(2)}, u32[]{:S(2)}) collective-permute-start(f32[8,128]{1,0:T(8,128)S(1)} %get-tuple-element.54), channel_id=1, source_target_pairs={{0,4},{1,5},{2,6},{3,7},{4,0},{5,1},{6,2},{7,3},{8,12},{9,13},{10,... | collective-permute-start | bytes 12296 | tf_op jit(solution)/shard_map/ppermute | solution.py:27
  27.4 0.1 collective-permute-done.7
  27.6 1.4 %collective-permute-done.8 = f32[8,128]{1,0:T(8,128)S(1)} collective-permute-done((f32[8,128]{1,0:T(8,128)S(1)}, f32[8,128]{1,0:T(8,128)S(1)}, u32[]{:S(2)}, u32[]{:S(2)}) %collective-permute-start.8) | collective-permute-done | bytes 4128 | tf_op jit(solution)/shard_map/ppermute | solution.py:27
  29.0 0.5 %collective-permute-done.9 = f32[8,128]{1,0:T(8,128)S(1)} collective-permute-done((f32[8,128]{1,0:T(8,128)S(1)}, f32[8,128]{1,0:T(8,128)S(1)}, u32[]{:S(2)}, u32[]{:S(2)}) %collective-permute-start.9) | collective-permute-done | bytes 4128 | tf_op jit(solution)/shard_map/ppermute | solution.py:27
  29.5 0.6 %add_add_fusion = f32[8,128]{1,0:T(8,128)} fusion(f32[8,128]{1,0:T(8,128)S(1)} %collective-permute-done.9, f32[8,128]{1,0:T(8,128)S(1)} %collective-permute-done.8, f32[8,128]{1,0:T(8,128)S(1)} %get-tuple-element.51, f32[8,128]{1,0:T(8,128)S(1)} %collective-permute-done.7), kind=kLoop, calls=%fused_computation.3 | loop fusion | flops 3072 | bytes 20480 | tf_op jit(solution)/shard_map/add | solution.py:254
  (3 shorter events, 0.0 us)
Async XLA Ops:
  1.8 14.7 %collective-permute-start.2 = (bf16[2,128,512]{2,1,0:T(8,128)(2,1)S(1)}, bf16[2,128,512]{2,1,0:T(8,128)(2,1)S(1)}, u32[]{:S(2)}, u32[]{:S(2)}) collective-permute-start(bf16[2,128,512]{2,1,0:T(8,128)(2,1)S(1)} %get-tuple-element.31), channel_id=1, source_target_pairs={{0,6},{1,7},{2,4},{3,5},{4,2},{5,3},{6,0},{7,1},{8,14},{9,15},{10,... | collective-permute-start | bytes 786440 | tf_op jit(solution)/shard_map/ppermute | solution.py:27
  5.7 10.2 %collective-permute-start.1 = (bf16[320,256]{1,0:T(8,128)(2,1)S(1)}, bf16[320,256]{1,0:T(8,128)(2,1)S(1)}, u32[]{:S(2)}, u32[]{:S(2)}) collective-permute-start(bf16[320,256]{1,0:T(8,128)(2,1)S(1)} %get-tuple-element.32), channel_id=1, source_target_pairs={{0,16},{8,24},{16,0},{24,8},{1,17},{9,25},{17,1},{25,9},{2,18},{10... | collective-permute-start | bytes 491528 | tf_op jit(solution)/shard_map/ppermute | solution.py:27
  8.3 8.2 %collective-permute-start = (bf16[320,256]{1,0:T(8,128)(2,1)S(1)}, bf16[320,256]{1,0:T(8,128)(2,1)S(1)}, u32[]{:S(2)}, u32[]{:S(2)}) collective-permute-start(bf16[320,256]{1,0:T(8,128)(2,1)S(1)} %get-tuple-element.32), channel_id=1, source_target_pairs={{0,8},{8,0},{16,24},{24,16},{1,9},{9,1},{17,25},{25,17},{2,10},{10... | collective-permute-start | bytes 491528 | tf_op jit(solution)/shard_map/ppermute | solution.py:27
  11.9 7.3 %collective-permute-start.4 = (bf16[2,128,512]{2,1,0:T(8,128)(2,1)S(1)}, bf16[2,128,512]{2,1,0:T(8,128)(2,1)S(1)}, u32[]{:S(2)}, u32[]{:S(2)}) collective-permute-start(bf16[2,128,512]{2,1,0:T(8,128)(2,1)S(1)} %get-tuple-element.37), channel_id=1, source_target_pairs={{0,4},{1,5},{2,6},{3,7},{4,0},{5,1},{6,2},{7,3},{8,12},{9,13},{10,... | collective-permute-start | bytes 786440 | tf_op jit(solution)/shard_map/ppermute | solution.py:27
  12.5 6.9 %collective-permute-start.5 = (bf16[2,128,512]{2,1,0:T(8,128)(2,1)S(1)}, bf16[2,128,512]{2,1,0:T(8,128)(2,1)S(1)}, u32[]{:S(2)}, u32[]{:S(2)}) collective-permute-start(bf16[2,128,512]{2,1,0:T(8,128)(2,1)S(1)} %get-tuple-element.38), channel_id=1, source_target_pairs={{0,2},{1,3},{2,0},{3,1},{4,6},{5,7},{6,4},{7,5},{8,10},{9,11},{10,... | collective-permute-start | bytes 786440 | tf_op jit(solution)/shard_map/ppermute | solution.py:27
  15.9 5.3 %collective-permute-start.3 = (bf16[320,256]{1,0:T(8,128)(2,1)S(1)}, bf16[320,256]{1,0:T(8,128)(2,1)S(1)}, u32[]{:S(2)}, u32[]{:S(2)}) collective-permute-start(bf16[320,256]{1,0:T(8,128)(2,1)S(1)} %collective-permute-done.1), channel_id=1, source_target_pairs={{0,8},{8,0},{16,24},{24,16},{1,9},{9,1},{17,25},{25,17},{2,10},{10... | collective-permute-start | bytes 491528 | tf_op jit(solution)/shard_map/ppermute | solution.py:27
  21.2 1.4 %collective-permute-start.6 = (bf16[320,256]{1,0:T(8,128)(2,1)S(1)}, bf16[320,256]{1,0:T(8,128)(2,1)S(1)}, u32[]{:S(2)}, u32[]{:S(2)}) collective-permute-start(bf16[320,256]{1,0:T(8,128)(2,1)S(1)} %collective-permute-done.3.last_ref), channel_id=1, source_target_pairs={{0,1},{1,0},{2,3},{3,2},{4,5},{5,4},{6,7},{7,6},{8,9},{9,8},{10,11... | collective-permute-start | bytes 491528 | tf_op jit(solution)/shard_map/ppermute | solution.py:27
  23.9 3.7 %collective-permute-start.7 = (f32[8,128]{1,0:T(8,128)S(1)}, f32[8,128]{1,0:T(8,128)S(1)}, u32[]{:S(2)}, u32[]{:S(2)}) collective-permute-start(f32[8,128]{1,0:T(8,128)S(1)} %get-tuple-element.52), channel_id=1, source_target_pairs={{0,2},{1,3},{2,0},{3,1},{4,6},{5,7},{6,4},{7,5},{8,10},{9,11},{10,... | collective-permute-start | bytes 12296 | tf_op jit(solution)/shard_map/ppermute | solution.py:27
  24.5 4.5 %collective-permute-start.8 = (f32[8,128]{1,0:T(8,128)S(1)}, f32[8,128]{1,0:T(8,128)S(1)}, u32[]{:S(2)}, u32[]{:S(2)}) collective-permute-start(f32[8,128]{1,0:T(8,128)S(1)} %get-tuple-element.53), channel_id=1, source_target_pairs={{0,6},{1,7},{2,4},{3,5},{4,2},{5,3},{6,0},{7,1},{8,14},{9,15},{10,... | collective-permute-start | bytes 12296 | tf_op jit(solution)/shard_map/ppermute | solution.py:27
  25.9 3.6 %collective-permute-start.9 = (f32[8,128]{1,0:T(8,128)S(1)}, f32[8,128]{1,0:T(8,128)S(1)}, u32[]{:S(2)}, u32[]{:S(2)}) collective-permute-start(f32[8,128]{1,0:T(8,128)S(1)} %get-tuple-element.54), channel_id=1, source_target_pairs={{0,4},{1,5},{2,6},{3,7},{4,0},{5,1},{6,2},{7,3},{8,12},{9,13},{10,... | collective-permute-start | bytes 12296 | tf_op jit(solution)/shard_map/ppermute | solution.py:27

commit v10 on v8

--- a/solution.py
+++ b/solution.py
@@ -269,7 +269,7 @@
     scores = pair_scores(0, first, last, chunks, ())
     scores = pair_scores(1, both, there, chunks, (mask, *scores))
     total = scores[0]
-    for m in [k ^ (k >> 1) for k in range(1, chips)]:
+    for m in sorted(range(1, chips), key=lambda m: (-m.bit_count(), m)):
         total = total + swap(scores[m], "blk", CORES * m)
     return total
 

time: 30.4 us -> 30.4 us (level)
  transfers between devices with their start and end apart: 10 -> 10, of which waited for: 8 -> 7; matrix products, arithmetic and copies ran while one was open for 0% -> 0% of each run, Pallas kernels for 11% -> 11%
where the time goes in v10:
time: 30.4 us; the launch traced here: 30.1 us
  starting transfers between devices  13.4 us (44%)
  waiting for transfers between devices  7.31 us (24%)
  Pallas kernels  6.3 us (21%)
  blocking collectives  2.51 us (8%)
  other arithmetic  0.6 us (2%)
    ppermute x10, starting transfers between devices, swap(): lax.ppermute(array, axis, [(i, i ^ bits) for i in range(lax.axis_size(axi...  13.4 us
    ppermute x10, waiting for transfers between devices, swap(): lax.ppermute(array, axis, [(i, i ^ bits) for i in range(lax.axis_size(axi...  7.31 us
    pallas_call x2, Pallas kernels, pair_scores(): pl.pallas_call(functools.partial(pair_kernel, core, rows, chips), out_sha...  2.53 us
    all_gather x1, blocking collectives, on_device(): both = lax.all_gather(first, 'blk', axis=0, axis_index_groups=pairs)  2.51 us
    pallas_call x1, Pallas kernels, take_blocks(): pl.pallas_call(functools.partial(blocks_kernel, distances), out_shape=(pl...  1.99 us
    pallas_call x1, Pallas kernels, pack(): pl.pallas_call(functools.partial(pack_kernel, distances), out_shape=(pack...  1.75 us
  transfers between devices with their start and end apart: 10, of which 7 were waited for; matrix products, arithmetic and copies ran while one was open for 0% of the time, Pallas kernels for 11%

profile of v10, /device:TPU:0, one launch (start us, length us, event | category | flops | bytes accessed | tf_op | source)
XLA Modules:
  0.0 30.1 jit_solution(14324783422132000219)
XLA Ops:
  0.0 1.7 %pack.1 = (bf16[320,256]{1,0:T(8,128)(2,1)S(1)}, bf16[2,128,512]{2,1,0:T(8,128)(2,1)S(1)}) custom-call(s32[2,8]{1,0:T(2,128)} %bitcast.3, bf16[128,4096]{1,0:T(8,128)(2,1)} %acts_ref.3, bf16[128,14336]{1,0:T(8,128)(2,1)} %grads_ref.3, bf16[1,64,256]{2,1,0:T(8,128)(2,1)} %refs_0_.1, bf16[1,64,256]{2,1,0:T(8,128)(2,1)} %refs_1_.1, ...), custom_call_target="tpu_custom_call" | custom-call | tf_op jit(solution)/shard_map/pack/pallas_call | solution.py:128
  1.8 4.0 %collective-permute-start.2 = (bf16[2,128,512]{2,1,0:T(8,128)(2,1)S(1)}, bf16[2,128,512]{2,1,0:T(8,128)(2,1)S(1)}, u32[]{:S(2)}, u32[]{:S(2)}) collective-permute-start(bf16[2,128,512]{2,1,0:T(8,128)(2,1)S(1)} %get-tuple-element.31), channel_id=1, source_target_pairs={{0,6},{1,7},{2,4},{3,5},{4,2},{5,3},{6,0},{7,1},{8,14},{9,15},{10,... | collective-permute-start | bytes 786440 | tf_op jit(solution)/shard_map/ppermute | solution.py:27
  5.7 2.6 %collective-permute-start.1 = (bf16[320,256]{1,0:T(8,128)(2,1)S(1)}, bf16[320,256]{1,0:T(8,128)(2,1)S(1)}, u32[]{:S(2)}, u32[]{:S(2)}) collective-permute-start(bf16[320,256]{1,0:T(8,128)(2,1)S(1)} %get-tuple-element.32.refs_0_), channel_id=1, source_target_pairs={{0,16},{8,24},{16,0},{24,8},{1,17},{9,25},{17,1},{25,9},{2,18},{10... | collective-permute-start | bytes 491528 | tf_op jit(solution)/shard_map/ppermute | solution.py:27
  8.3 1.6 %collective-permute-start = (bf16[320,256]{1,0:T(8,128)(2,1)S(1)}, bf16[320,256]{1,0:T(8,128)(2,1)S(1)}, u32[]{:S(2)}, u32[]{:S(2)}) collective-permute-start(bf16[320,256]{1,0:T(8,128)(2,1)S(1)} %get-tuple-element.32.refs_0_), channel_id=1, source_target_pairs={{0,8},{8,0},{16,24},{24,16},{1,9},{9,1},{17,25},{25,17},{2,10},{10... | collective-permute-start | bytes 491528 | tf_op jit(solution)/shard_map/ppermute | solution.py:27
  9.9 2.0 %take_blocks.1 = (f32[4,8,128]{2,1,0:T(8,128)S(1)}, bf16[2,128,512]{2,1,0:T(8,128)(2,1)S(1)}, bf16[2,128,512]{2,1,0:T(8,128)(2,1)S(1)}, bf16[2,128,512]{2,1,0:T(8,128)(2,1)S(1)}) custom-call(s32[2,8]{1,0:T(2,128)} %bitcast.4, s32[4]{0:T(128)} %lengths_ref.1, bf16[128,4096]{1,0:T(8,128)(2,1)} %acts_ref.3, bf16[128,14336]{1,0:T(8,128)(2,1)} %grads_ref.3), custom_call_target="tpu_custom_call" | custom-call | tf_op jit(solution)/shard_map/take_blocks/pallas_call | solution.py:86
  11.9 0.6 %collective-permute-start.4 = (bf16[2,128,512]{2,1,0:T(8,128)(2,1)S(1)}, bf16[2,128,512]{2,1,0:T(8,128)(2,1)S(1)}, u32[]{:S(2)}, u32[]{:S(2)}) collective-permute-start(bf16[2,128,512]{2,1,0:T(8,128)(2,1)S(1)} %get-tuple-element.37), channel_id=1, source_target_pairs={{0,4},{1,5},{2,6},{3,7},{4,0},{5,1},{6,2},{7,3},{8,12},{9,13},{10,... | collective-permute-start | bytes 786440 | tf_op jit(solution)/shard_map/ppermute | solution.py:27
  12.5 0.5 %collective-permute-start.5 = (bf16[2,128,512]{2,1,0:T(8,128)(2,1)S(1)}, bf16[2,128,512]{2,1,0:T(8,128)(2,1)S(1)}, u32[]{:S(2)}, u32[]{:S(2)}) collective-permute-start(bf16[2,128,512]{2,1,0:T(8,128)(2,1)S(1)} %get-tuple-element.38), channel_id=1, source_target_pairs={{0,2},{1,3},{2,0},{3,1},{4,6},{5,7},{6,4},{7,5},{8,10},{9,11},{10,... | collective-permute-start | bytes 786440 | tf_op jit(solution)/shard_map/ppermute | solution.py:27
  13.0 2.9 %collective-permute-done.1.refs_2_ = bf16[320,256]{1,0:T(8,128)(2,1)S(1)} collective-permute-done((bf16[320,256]{1,0:T(8,128)(2,1)S(1)}, bf16[320,256]{1,0:T(8,128)(2,1)S(1)}, u32[]{:S(2)}, u32[]{:S(2)}) %collective-permute-start.1) | collective-permute-done | bytes 163872 | tf_op jit(solution)/shard_map/ppermute | solution.py:27
  15.9 0.6 %collective-permute-start.3 = (bf16[320,256]{1,0:T(8,128)(2,1)S(1)}, bf16[320,256]{1,0:T(8,128)(2,1)S(1)}, u32[]{:S(2)}, u32[]{:S(2)}) collective-permute-start(bf16[320,256]{1,0:T(8,128)(2,1)S(1)} %collective-permute-done.1.refs_2_), channel_id=1, source_target_pairs={{0,8},{8,0},{16,24},{24,16},{1,9},{9,1},{17,25},{25,17},{2,10},{10... | collective-permute-start | bytes 491528 | tf_op jit(solution)/shard_map/ppermute | solution.py:27
  16.5 0.0 collective-permute-done.refs_1_
  16.5 0.0 collective-permute-done.2.refs_3_
  16.5 2.5 %all-gather = bf16[1920,256]{1,0:T(8,128)(2,1)S(1)} all-gather(bf16[960,256]{1,0:T(8,128)(2,1)S(1)} %join.1.first_ref), channel_id=2, replica_groups={{0,1},{2,3},{4,5},{6,7},{8,9},{10,11},{12,13},{14,15},{16,17},{18,19},{..., dimensions={0}, use_global_device_ids=true | all-gather | bytes 1474560 | tf_op jit(solution)/shard_map/all_gather | solution.py:265
  19.0 0.1 collective-permute-done.4.refs_2_
  19.2 0.2 collective-permute-done.5.refs_1_
  19.4 1.8 %collective-permute-done.3.last_ref = bf16[320,256]{1,0:T(8,128)(2,1)S(1)} collective-permute-done((bf16[320,256]{1,0:T(8,128)(2,1)S(1)}, bf16[320,256]{1,0:T(8,128)(2,1)S(1)}, u32[]{:S(2)}, u32[]{:S(2)}) %collective-permute-start.3) | collective-permute-done | bytes 163872 | tf_op jit(solution)/shard_map/ppermute | solution.py:27
  21.2 0.0 collective-permute-start.6
  21.2 1.3 %pair_scores.2 = (f32[8,128]{1,0:T(8,128)S(1)}, f32[8,128]{1,0:T(8,128)S(1)}, f32[8,128]{1,0:T(8,128)S(1)}, f32[8,128]{1,0:T(8,128)S(1)}) custom-call(bf16[960,256]{1,0:T(8,128)(2,1)S(1)} %join.1.first_ref, bf16[320,256]{1,0:T(8,128)(2,1)S(1)} %collective-permute-done.3.last_ref, bf16[2,128,512]{2,1,0:T(8,128)(2,1)S(1)} %get-tuple-element.41.refs_0_, ...), custom_call_target="tpu_custom_call" | custom-call | flops 671088640 | bytes 1835008 | tf_op jit(solution)/shard_map/pair_scores/pallas_call | solution.py:212
  22.5 0.1 collective-permute-done.6.last_ref
  22.6 1.3 %pair_scores.3 = (f32[8,128]{1,0:T(8,128)S(1)}, f32[8,128]{1,0:T(8,128)S(1)}, f32[8,128]{1,0:T(8,128)S(1)}, f32[8,128]{1,0:T(8,128)S(1)}) custom-call(bf16[2,960,256]{2,1,0:T(8,128)(2,1)S(1)} %bitcast.2, bf16[320,256]{1,0:T(8,128)(2,1)S(1)} %collective-permute-done.6.last_ref, bf16[2,128,512]{2,1,0:T(8,128)(2,1)S(1)} %get-tuple-element.41.refs_0_, ...), custom_call_target="tpu_custom_call" | custom-call | flops 671088640 | bytes 1835008 | tf_op jit(solution)/shard_map/pair_scores/pallas_call | solution.py:212
  23.9 0.5 %collective-permute-start.7 = (f32[8,128]{1,0:T(8,128)S(1)}, f32[8,128]{1,0:T(8,128)S(1)}, u32[]{:S(2)}, u32[]{:S(2)}) collective-permute-start(f32[8,128]{1,0:T(8,128)S(1)} %get-tuple-element.52), channel_id=1, source_target_pairs={{0,6},{1,7},{2,4},{3,5},{4,2},{5,3},{6,0},{7,1},{8,14},{9,15},{10,... | collective-permute-start | bytes 12296 | tf_op jit(solution)/shard_map/ppermute | solution.py:27
  24.4 1.5 %collective-permute-start.8 = (f32[8,128]{1,0:T(8,128)S(1)}, f32[8,128]{1,0:T(8,128)S(1)}, u32[]{:S(2)}, u32[]{:S(2)}) collective-permute-start(f32[8,128]{1,0:T(8,128)S(1)} %get-tuple-element.53), channel_id=1, source_target_pairs={{0,2},{1,3},{2,0},{3,1},{4,6},{5,7},{6,4},{7,5},{8,10},{9,11},{10,... | collective-permute-start | bytes 12296 | tf_op jit(solution)/shard_map/ppermute | solution.py:27
  25.9 1.5 %collective-permute-start.9 = (f32[8,128]{1,0:T(8,128)S(1)}, f32[8,128]{1,0:T(8,128)S(1)}, u32[]{:S(2)}, u32[]{:S(2)}) collective-permute-start(f32[8,128]{1,0:T(8,128)S(1)} %get-tuple-element.54), channel_id=1, source_target_pairs={{0,4},{1,5},{2,6},{3,7},{4,0},{5,1},{6,2},{7,3},{8,12},{9,13},{10,... | collective-permute-start | bytes 12296 | tf_op jit(solution)/shard_map/ppermute | solution.py:27
  27.4 1.0 %collective-permute-done.7 = f32[8,128]{1,0:T(8,128)S(1)} collective-permute-done((f32[8,128]{1,0:T(8,128)S(1)}, f32[8,128]{1,0:T(8,128)S(1)}, u32[]{:S(2)}, u32[]{:S(2)}) %collective-permute-start.7) | collective-permute-done | bytes 4128 | tf_op jit(solution)/shard_map/ppermute | solution.py:27
  28.5 0.0 collective-permute-done.8
  28.5 1.1 %collective-permute-done.9 = f32[8,128]{1,0:T(8,128)S(1)} collective-permute-done((f32[8,128]{1,0:T(8,128)S(1)}, f32[8,128]{1,0:T(8,128)S(1)}, u32[]{:S(2)}, u32[]{:S(2)}) %collective-permute-start.9) | collective-permute-done | bytes 4128 | tf_op jit(solution)/shard_map/ppermute | solution.py:27
  29.5 0.6 %add_add_fusion = f32[8,128]{1,0:T(8,128)} fusion(f32[8,128]{1,0:T(8,128)S(1)} %collective-permute-done.9, f32[8,128]{1,0:T(8,128)S(1)} %collective-permute-done.8, f32[8,128]{1,0:T(8,128)S(1)} %get-tuple-element.51, f32[8,128]{1,0:T(8,128)S(1)} %collective-permute-done.7), kind=kLoop, calls=%fused_computation | loop fusion | flops 3072 | bytes 20480 | tf_op jit(solution)/shard_map/add | solution.py:273
  (1 shorter events, 0.0 us)
Async XLA Ops:
  1.8 14.7 %collective-permute-start.2 = (bf16[2,128,512]{2,1,0:T(8,128)(2,1)S(1)}, bf16[2,128,512]{2,1,0:T(8,128)(2,1)S(1)}, u32[]{:S(2)}, u32[]{:S(2)}) collective-permute-start(bf16[2,128,512]{2,1,0:T(8,128)(2,1)S(1)} %get-tuple-element.31), channel_id=1, source_target_pairs={{0,6},{1,7},{2,4},{3,5},{4,2},{5,3},{6,0},{7,1},{8,14},{9,15},{10,... | collective-permute-start | bytes 786440 | tf_op jit(solution)/shard_map/ppermute | solution.py:27
  5.7 10.2 %collective-permute-start.1 = (bf16[320,256]{1,0:T(8,128)(2,1)S(1)}, bf16[320,256]{1,0:T(8,128)(2,1)S(1)}, u32[]{:S(2)}, u32[]{:S(2)}) collective-permute-start(bf16[320,256]{1,0:T(8,128)(2,1)S(1)} %get-tuple-element.32.refs_0_), channel_id=1, source_target_pairs={{0,16},{8,24},{16,0},{24,8},{1,17},{9,25},{17,1},{25,9},{2,18},{10... | collective-permute-start | bytes 491528 | tf_op jit(solution)/shard_map/ppermute | solution.py:27
  8.3 8.2 %collective-permute-start = (bf16[320,256]{1,0:T(8,128)(2,1)S(1)}, bf16[320,256]{1,0:T(8,128)(2,1)S(1)}, u32[]{:S(2)}, u32[]{:S(2)}) collective-permute-start(bf16[320,256]{1,0:T(8,128)(2,1)S(1)} %get-tuple-element.32.refs_0_), channel_id=1, source_target_pairs={{0,8},{8,0},{16,24},{24,16},{1,9},{9,1},{17,25},{25,17},{2,10},{10... | collective-permute-start | bytes 491528 | tf_op jit(solution)/shard_map/ppermute | solution.py:27
  11.9 7.3 %collective-permute-start.4 = (bf16[2,128,512]{2,1,0:T(8,128)(2,1)S(1)}, bf16[2,128,512]{2,1,0:T(8,128)(2,1)S(1)}, u32[]{:S(2)}, u32[]{:S(2)}) collective-permute-start(bf16[2,128,512]{2,1,0:T(8,128)(2,1)S(1)} %get-tuple-element.37), channel_id=1, source_target_pairs={{0,4},{1,5},{2,6},{3,7},{4,0},{5,1},{6,2},{7,3},{8,12},{9,13},{10,... | collective-permute-start | bytes 786440 | tf_op jit(solution)/shard_map/ppermute | solution.py:27
  12.5 6.9 %collective-permute-start.5 = (bf16[2,128,512]{2,1,0:T(8,128)(2,1)S(1)}, bf16[2,128,512]{2,1,0:T(8,128)(2,1)S(1)}, u32[]{:S(2)}, u32[]{:S(2)}) collective-permute-start(bf16[2,128,512]{2,1,0:T(8,128)(2,1)S(1)} %get-tuple-element.38), channel_id=1, source_target_pairs={{0,2},{1,3},{2,0},{3,1},{4,6},{5,7},{6,4},{7,5},{8,10},{9,11},{10,... | collective-permute-start | bytes 786440 | tf_op jit(solution)/shard_map/ppermute | solution.py:27
  15.9 5.3 %collective-permute-start.3 = (bf16[320,256]{1,0:T(8,128)(2,1)S(1)}, bf16[320,256]{1,0:T(8,128)(2,1)S(1)}, u32[]{:S(2)}, u32[]{:S(2)}) collective-permute-start(bf16[320,256]{1,0:T(8,128)(2,1)S(1)} %collective-permute-done.1.refs_2_), channel_id=1, source_target_pairs={{0,8},{8,0},{16,24},{24,16},{1,9},{9,1},{17,25},{25,17},{2,10},{10... | collective-permute-start | bytes 491528 | tf_op jit(solution)/shard_map/ppermute | solution.py:27
  21.2 1.4 %collective-permute-start.6 = (bf16[320,256]{1,0:T(8,128)(2,1)S(1)}, bf16[320,256]{1,0:T(8,128)(2,1)S(1)}, u32[]{:S(2)}, u32[]{:S(2)}) collective-permute-start(bf16[320,256]{1,0:T(8,128)(2,1)S(1)} %collective-permute-done.3.last_ref), channel_id=1, source_target_pairs={{0,1},{1,0},{2,3},{3,2},{4,5},{5,4},{6,7},{7,6},{8,9},{9,8},{10,11... | collective-permute-start | bytes 491528 | tf_op jit(solution)/shard_map/ppermute | solution.py:27
  23.9 4.6 %collective-permute-start.7 = (f32[8,128]{1,0:T(8,128)S(1)}, f32[8,128]{1,0:T(8,128)S(1)}, u32[]{:S(2)}, u32[]{:S(2)}) collective-permute-start(f32[8,128]{1,0:T(8,128)S(1)} %get-tuple-element.52), channel_id=1, source_target_pairs={{0,6},{1,7},{2,4},{3,5},{4,2},{5,3},{6,0},{7,1},{8,14},{9,15},{10,... | collective-permute-start | bytes 12296 | tf_op jit(solution)/shard_map/ppermute | solution.py:27
  24.4 4.1 %collective-permute-start.8 = (f32[8,128]{1,0:T(8,128)S(1)}, f32[8,128]{1,0:T(8,128)S(1)}, u32[]{:S(2)}, u32[]{:S(2)}) collective-permute-start(f32[8,128]{1,0:T(8,128)S(1)} %get-tuple-element.53), channel_id=1, source_target_pairs={{0,2},{1,3},{2,0},{3,1},{4,6},{5,7},{6,4},{7,5},{8,10},{9,11},{10,... | collective-permute-start | bytes 12296 | tf_op jit(solution)/shard_map/ppermute | solution.py:27
  25.9 3.6 %collective-permute-start.9 = (f32[8,128]{1,0:T(8,128)S(1)}, f32[8,128]{1,0:T(8,128)S(1)}, u32[]{:S(2)}, u32[]{:S(2)}) collective-permute-start(f32[8,128]{1,0:T(8,128)S(1)} %get-tuple-element.54), channel_id=1, source_target_pairs={{0,4},{1,5},{2,6},{3,7},{4,0},{5,1},{6,2},{7,3},{8,12},{9,13},{10,... | collective-permute-start | bytes 12296 | tf_op jit(solution)/shard_map/ppermute | solution.py:27
